TPU v7x, 32 devices: a whole 2x2x4 slice. The times are simulated.
32 devices in a mesh: dp: 4 (over y, x), fsdp: 8 (over z, core).
Axes of the slice: x: 2, y: 2, z: 4, core: 2. Of those that a mesh axis runs over, the one named last changes fastest.
Arguments:
- tokens: bfloat16 [64, 128, 768], P(('dp', 'fsdp')), may hold values from -6 to 6
- lengths: int32 [64], P(('dp', 'fsdp')), may hold values from 1 to 128, as said below
- timesteps: int32 [64], P(('dp', 'fsdp')), may hold values from 0 to 1999
- cotangent: bfloat16 [64, 128, 768], P(('dp', 'fsdp')), may hold values from -6 to 6
- params: float32 [7547136], P('fsdp')
- moment_one: float32 [7547136], P('fsdp')
- moment_two: float32 [7547136], P('fsdp')
Outputs:
- output: bfloat16 [64, 128, 768], P(('dp', 'fsdp'))
- token_grad: float32 [64, 128, 768], P(('dp', 'fsdp'))
- new_params: float32 [7547136], P('fsdp')
- new_moment_one: float32 [7547136], P('fsdp')
- new_moment_two: float32 [7547136], P('fsdp')
Inputs may be any that keep to these rules, and one draw needn't show every extreme that they name: `lengths`: padding follows each sequence's length; some sequence has length 128 in every draw.
All inputs are finite; a program needn't handle non-finite values.
Results may differ from a plain program's by a relative error of at most 0.013.
The roundings to bfloat16 on the way count: a program that leaves them out, or rounds other values in their place, can miss the bound.
Values may be sent and summed in bfloat16 or wider, within the bound.
No kernel may reach another device: no remote copies, remote signals or barrier semaphores. Data moves between devices by JAX's collectives and lax.ppermute only.
A program may use at most 192 MiB of HBM per device.

v0:
```python
from functools import partial
import math

import jax
import jax.numpy as jnp
from jax import lax
from jax.sharding import PartitionSpec as P

D = 768
HEADS = 12
HEAD_DIM = 64
FF = 3072
TFREQ = 128
THID = 512
STEP = 10
MATS = 7536640


NORM_EPS = 1e-05
ADAM_EPS = 1e-08
BETA_ONE = 0.5
BETA_TWO = 0.5
RATE_MATRIX = 0.02
RATE_SMALL = 0.2
WEIGHT_DECAY = 0.01


def segment_shapes():
    return [
        (TFREQ, THID),
        (THID, D),
        (D, 3 * D),
        (D, D),
        (D, FF),
        (FF, D),
        (THID,),
        (D,),
        (D,),
        (D,),
        (D,),
        (D,),
        (D,),
        (FF,),
        (D,),
        (D,),
        (D,),
    ]


def split_flat(flat_vec):
    pieces = []
    offset = 0
    for seg_shape in segment_shapes():
        extent = math.prod(seg_shape)
        pieces.append(flat_vec[offset : offset + extent].reshape(seg_shape))
        offset += extent
    return pieces


def layer_norm(values, gain_vec, shift_vec):
    center = values - jnp.mean(values, axis=-1, keepdims=True)
    variance = jnp.mean(center * center, axis=-1, keepdims=True)
    return center * lax.rsqrt(variance + NORM_EPS) * gain_vec + shift_vec


def attention_scores(q_heads, k_heads, key_valid):
    raw_scores = jnp.einsum("bqhd,bkhd->bhqk", q_heads, k_heads, preferred_element_type=jnp.float32)
    return jnp.where(key_valid, raw_scores * HEAD_DIM ** (-0.5), -1e30)


def run_forward(weights, tokens, timesteps, lengths):
    (
        time_in,
        time_out,
        qkv_weight,
        out_weight,
        up_weight,
        down_weight,
        time_in_bias,
        time_out_bias,
        q_bias,
        v_bias,
        out_bias,
        gain_one,
        shift_one,
        up_bias,
        down_bias,
        gain_two,
        shift_two,
    ) = weights
    seq_count, length, model_width = tokens.shape
    half_freq = TFREQ // 2
    frequencies = jnp.exp(-math.log(10000.0) * jnp.arange(half_freq, dtype=jnp.float32) / half_freq)
    angles = timesteps.astype(jnp.float32)[:, None] * frequencies[None, :]
    sinusoid = jnp.concatenate([jnp.cos(angles), jnp.sin(angles)], axis=1).astype(jnp.bfloat16)
    time_pre = jnp.dot(sinusoid, time_in, preferred_element_type=jnp.float32) + time_in_bias.astype(
        jnp.float32
    )
    time_act = jax.nn.silu(time_pre).astype(jnp.bfloat16)
    time_emb = jnp.dot(
        time_act, time_out, preferred_element_type=jnp.float32
    ) + time_out_bias.astype(jnp.float32)
    rows_zero = (tokens.astype(jnp.float32) + time_emb[:, None, :]).reshape(
        seq_count * length, model_width
    )
    rows_low = rows_zero.astype(jnp.bfloat16)
    qkv_rows = jnp.dot(rows_low, qkv_weight, preferred_element_type=jnp.float32)
    quad = (seq_count, length, HEADS, HEAD_DIM)
    q_heads = (
        (qkv_rows[:, :model_width] + q_bias.astype(jnp.float32)).astype(jnp.bfloat16).reshape(quad)
    )
    k_heads = qkv_rows[:, model_width : 2 * model_width].astype(jnp.bfloat16).reshape(quad)
    v_heads = (
        (qkv_rows[:, 2 * model_width :] + v_bias.astype(jnp.float32))
        .astype(jnp.bfloat16)
        .reshape(quad)
    )
    key_valid = (jnp.arange(length, dtype=jnp.int32)[None, :] < lengths[:, None])[:, None, None, :]
    masked = attention_scores(q_heads, k_heads, key_valid)
    row_top = jnp.max(masked, axis=-1, keepdims=True)
    log_total = row_top + jnp.log(jnp.sum(jnp.exp(masked - row_top), axis=-1, keepdims=True))
    attn_probs = jnp.exp(masked - log_total).astype(jnp.bfloat16)
    context = jnp.einsum("bhqk,bkhd->bqhd", attn_probs, v_heads, preferred_element_type=jnp.float32)
    context = context.reshape(seq_count * length, model_width).astype(jnp.bfloat16)
    attn_out = jnp.dot(context, out_weight, preferred_element_type=jnp.float32) + out_bias.astype(
        jnp.float32
    )
    sum_one = rows_zero + attn_out
    hidden_one = layer_norm(sum_one, gain_one.astype(jnp.float32), shift_one.astype(jnp.float32))
    hidden_low = hidden_one.astype(jnp.bfloat16)
    up_pre = jnp.dot(hidden_low, up_weight, preferred_element_type=jnp.float32) + up_bias.astype(
        jnp.float32
    )
    act_low = jax.nn.gelu(up_pre, approximate=False).astype(jnp.bfloat16)
    down_out = jnp.dot(act_low, down_weight, preferred_element_type=jnp.float32) + down_bias.astype(
        jnp.float32
    )
    sum_two = hidden_one + down_out
    result = layer_norm(sum_two, gain_two.astype(jnp.float32), shift_two.astype(jnp.float32))
    return (
        sinusoid,
        time_pre,
        time_act,
        rows_low,
        q_heads,
        k_heads,
        v_heads,
        key_valid,
        log_total,
        context,
        sum_one,
        hidden_low,
        up_pre,
        act_low,
        sum_two,
        result,
    )


def column_sums(values):
    return jnp.sum(values.astype(jnp.float32), axis=0)


def run_backward(weights, saved, cotangent):
    (
        time_in,
        time_out,
        qkv_weight,
        out_weight,
        up_weight,
        down_weight,
        time_in_bias,
        time_out_bias,
        q_bias,
        v_bias,
        out_bias,
        gain_one,
        shift_one,
        up_bias,
        down_bias,
        gain_two,
        shift_two,
    ) = weights
    (
        sinusoid,
        time_pre,
        time_act,
        rows_low,
        q_heads,
        k_heads,
        v_heads,
        key_valid,
        log_total,
        context,
        sum_one,
        hidden_low,
        up_pre,
        act_low,
        sum_two,
        result,
    ) = saved
    seq_count, length, model_width = cotangent.shape
    rows_total = seq_count * length
    d_result = cotangent.astype(jnp.float32).reshape(rows_total, model_width)
    ignored, pull_two = jax.vjp(
        layer_norm, sum_two, gain_two.astype(jnp.float32), shift_two.astype(jnp.float32)
    )
    d_sum_two, g_gain_two, g_shift_two = pull_two(d_result)
    d_down = d_sum_two.astype(jnp.bfloat16)
    g_down_bias = column_sums(d_down)
    g_down = jnp.einsum("rf,rd->fd", act_low, d_down, preferred_element_type=jnp.float32)
    d_act = jnp.dot(d_down, down_weight.T, preferred_element_type=jnp.float32)
    ignored, pull_gelu = jax.vjp(partial(jax.nn.gelu, approximate=False), up_pre)
    d_up = pull_gelu(d_act)[0].astype(jnp.bfloat16)
    g_up_bias = column_sums(d_up)
    g_up = jnp.einsum("rd,rf->df", hidden_low, d_up, preferred_element_type=jnp.float32)
    d_hidden_one = d_sum_two + jnp.dot(d_up, up_weight.T, preferred_element_type=jnp.float32)
    ignored, pull_one = jax.vjp(
        layer_norm, sum_one, gain_one.astype(jnp.float32), shift_one.astype(jnp.float32)
    )
    d_sum_one, g_gain_one, g_shift_one = pull_one(d_hidden_one)
    d_attn = d_sum_one.astype(jnp.bfloat16)
    g_out_bias = column_sums(d_attn)
    g_out = jnp.einsum("rd,re->de", context, d_attn, preferred_element_type=jnp.float32)
    d_context = jnp.dot(d_attn, out_weight.T, preferred_element_type=jnp.float32).astype(
        jnp.bfloat16
    )
    d_context = d_context.reshape(seq_count, length, HEADS, HEAD_DIM)
    masked = attention_scores(q_heads, k_heads, key_valid)
    attn_exact = jnp.exp(masked - log_total)
    probs_low = attn_exact.astype(jnp.bfloat16)
    d_v = jnp.einsum("bhqk,bqhd->bkhd", probs_low, d_context, preferred_element_type=jnp.float32)
    d_probs = jnp.einsum("bqhd,bkhd->bhqk", d_context, v_heads, preferred_element_type=jnp.float32)
    row_delta = jnp.sum(attn_exact * d_probs, axis=-1, keepdims=True)
    d_scores = (attn_exact * (d_probs - row_delta)).astype(jnp.bfloat16)
    d_q = jnp.einsum(
        "bhqk,bkhd->bqhd", d_scores, k_heads, preferred_element_type=jnp.float32
    ) * HEAD_DIM ** (-0.5)
    d_k = jnp.einsum(
        "bhqk,bqhd->bkhd", d_scores, q_heads, preferred_element_type=jnp.float32
    ) * HEAD_DIM ** (-0.5)
    d_qkv = jnp.concatenate(
        [
            d_q.reshape(rows_total, model_width),
            d_k.reshape(rows_total, model_width),
            d_v.reshape(rows_total, model_width),
        ],
        axis=1,
    ).astype(jnp.bfloat16)
    g_q_bias = column_sums(d_qkv[:, :model_width])
    g_v_bias = column_sums(d_qkv[:, 2 * model_width :])
    g_qkv = jnp.einsum("rd,re->de", rows_low, d_qkv, preferred_element_type=jnp.float32)
    d_rows = d_sum_one + jnp.dot(d_qkv, qkv_weight.T, preferred_element_type=jnp.float32)
    d_time = jnp.sum(d_rows.reshape(seq_count, length, model_width), axis=1).astype(jnp.bfloat16)
    g_time_out_bias = column_sums(d_time)
    g_time_out = jnp.einsum("nt,nd->td", time_act, d_time, preferred_element_type=jnp.float32)
    d_time_act = jnp.dot(d_time, time_out.T, preferred_element_type=jnp.float32)
    ignored, pull_silu = jax.vjp(jax.nn.silu, time_pre)
    d_time_pre = pull_silu(d_time_act)[0].astype(jnp.bfloat16)
    g_time_in_bias = column_sums(d_time_pre)
    g_time_in = jnp.einsum("nf,nt->ft", sinusoid, d_time_pre, preferred_element_type=jnp.float32)
    gradients = [
        g_time_in,
        g_time_out,
        g_qkv,
        g_out,
        g_up,
        g_down,
        g_time_in_bias,
        g_time_out_bias,
        g_q_bias,
        g_v_bias,
        g_out_bias,
        g_gain_one,
        g_shift_one,
        g_up_bias,
        g_down_bias,
        g_gain_two,
        g_shift_two,
    ]
    flat_grad = jnp.concatenate([item.reshape(-1) for item in gradients])
    return (flat_grad, d_rows.reshape(seq_count, length, model_width))


def local(tokens, lengths, timesteps, cotangent, params, moment_one, moment_two):
    shard_len = params.shape[0]
    low_shard = params.astype(jnp.bfloat16)
    gathered = lax.all_gather(low_shard, "fsdp", axis=0, tiled=True)
    weights = split_flat(gathered)
    saved = run_forward(weights, tokens, timesteps, lengths)
    output = saved[-1].reshape(tokens.shape).astype(jnp.bfloat16)
    regathered = lax.all_gather(low_shard, "fsdp", axis=0, tiled=True)
    back_weights = split_flat(regathered)
    back_saved = run_forward(back_weights, tokens, timesteps, lengths)
    flat_grad, token_grad = run_backward(back_weights, back_saved, cotangent)
    shard_sum = lax.psum_scatter(flat_grad, "fsdp", scatter_dimension=0, tiled=True)
    quarter_sum = lax.psum_scatter(
        shard_sum.astype(jnp.bfloat16), "dp", scatter_dimension=0, tiled=True
    ).astype(jnp.float32)
    grad_shard = lax.all_gather(quarter_sum.astype(jnp.bfloat16), "dp", axis=0, tiled=True).astype(
        quarter_sum.dtype
    )
    moment_new = BETA_ONE * moment_one + (1.0 - BETA_ONE) * grad_shard
    second_new = BETA_TWO * moment_two + (1.0 - BETA_TWO) * grad_shard * grad_shard
    corr_one = 1.0 - BETA_ONE**STEP
    corr_two = 1.0 - BETA_TWO**STEP
    shard_start = lax.axis_index("fsdp") * shard_len
    index_local = shard_start + jnp.arange(shard_len, dtype=jnp.int32)
    is_matrix = index_local < MATS
    rates = jnp.where(is_matrix, RATE_MATRIX, RATE_SMALL)
    decays = jnp.where(is_matrix, WEIGHT_DECAY, 0.0)
    update = moment_new / corr_one / (jnp.sqrt(second_new / corr_two) + ADAM_EPS)
    new_params = params - rates * (update + decays * params)
    return (output, token_grad, new_params, moment_new, second_new)


def solution(mesh):
    return jax.shard_map(
        local,
        mesh=mesh,
        in_specs=(
            P(("dp", "fsdp"), None, None),
            P(("dp", "fsdp")),
            P(("dp", "fsdp")),
            P(("dp", "fsdp"), None, None),
            P("fsdp"),
            P("fsdp"),
            P("fsdp"),
        ),
        out_specs=(
            P(("dp", "fsdp"), None, None),
            P(("dp", "fsdp"), None, None),
            P("fsdp"),
            P("fsdp"),
            P("fsdp"),
        ),
        check_vma=False,
    )
```

profile of v0, /device:TPU:0, one launch (start us, length us, event | category | flops | bytes accessed | tf_op | source)
XLA Modules:
  0.0 1278.1 jit_solution(11006683398150457714)
XLA Ops:
  7.3 2.3 convert_element_type.167
  10.8 5.5 broadcast.255
  16.3 29.2 %dynamic-update-slice = bf16[7547136]{0:T(1024)(128)(2,1)} dynamic-update-slice(bf16[7547136]{0:T(1024)(128)(2,1)} %broadcast.255, bf16[943392]{0:T(1024)(128)(2,1)S(1)} %convert_element_type.167, u32[]{:T(128)} %bitcast) | dynamic-update-slice | bytes 3773572
  47.7 303.0 %all-reduce.9.cloned.1.call-done = bf16[7547136]{0:T(1024)(128)(2,1)} async-done(((bf16[7547136]{0:T(1024)(128)(2,1)}), bf16[7547136]{0:T(1024)(128)(2,1)}) %all-reduce.9.cloned.1.call-update) | async-done | bytes 15094288
  350.7 8.3 fusion.59
  359.1 8.3 reshape.210
  367.3 1.6 reshape.203
  369.7 1.9 reshape.209
  371.6 2.0 slice-done.9
  373.6 5.1 reshape.205
  380.4 1.4 slice_convert_fusion.3
  381.8 1.3 convolution_add_fusion.5
  383.2 2.0 fusion.39
  385.1 3.1 fusion.65
  390.0 1.7 fusion.62
  395.6 9.3 reshape.211
  405.6 10.2 multiply_convert_fusion
  415.8 1.5 fusion.64
  420.5 2.7 convert_reduce_fusion
  423.3 2.3 multiply_reduce_fusion.1
  430.8 1.6 multiply_reduce_fusion
  439.1 11.9 fusion.23
  451.0 5.2 convolution_bitcast_fusion
  456.2 5.0 fusion.67
  464.0 5.3 fusion.66
  469.3 8.1 reshape.220
  477.4 1.6 reshape.221
  478.9 9.4 copy.93
  488.4 10.8 reshape.223
  500.5 6.8 constant_dynamic-update-slice_fusion.15
  507.3 1.5 constant_dynamic-update-slice_fusion.14
  509.8 4.9 constant_dynamic-update-slice_fusion.13
  515.9 3.9 constant_dynamic-update-slice_fusion.12
  519.8 1.3 constant_dynamic-update-slice_fusion.11
  521.1 1.3 constant_dynamic-update-slice_fusion.10
  523.7 1.3 constant_dynamic-update-slice_fusion.8
  525.0 1.3 constant_dynamic-update-slice_fusion.7
  526.3 1.3 constant_dynamic-update-slice_fusion.6
  529.4 1.3 constant_dynamic-update-slice_fusion.3
  530.7 1.3 constant_dynamic-update-slice_fusion.2
  532.0 1.3 constant_dynamic-update-slice_fusion.1
  533.3 586.2 %all-reduce.14 = bf16[7547136]{0:T(1024)(128)(2,1)} all-reduce(f32[7547136]{0:T(1024)} %constant_dynamic-update-slice_fusion.1), channel_id=2, replica_groups=mesh['dp'=4,'fsdp'=8] {'fsdp'}, use_global_device_ids=true, to_apply=%region_23.24.clone | all-reduce | flops 7547136 | bytes 45282816
  1119.5 3.8 dynamic-slice.7
  1124.6 64.1 %all-reduce.13.cloned.1.call-done = bf16[943392]{0:T(1024)(128)(2,1)} async-done(((bf16[943392]{0:T(1024)(128)(2,1)}), bf16[943392]{0:T(1024)(128)(2,1)}) %all-reduce.13.cloned.1.call-update) | async-done | bytes 1886800
  1188.6 1.3 dynamic-slice.5
  1190.1 4.4 dynamic-update-slice.1
  1195.8 66.4 %all-reduce.11.cloned.1.call-done = bf16[943392]{0:T(1024)(128)(2,1)} async-done(((bf16[943392]{0:T(1024)(128)(2,1)}), bf16[943392]{0:T(1024)(128)(2,1)}) %all-reduce.11.cloned.1.call-update) | async-done | bytes 1886800
  1262.2 9.1 multiply_subtract_fusion
  (228 shorter events, 36.5 us)
Async XLA Ops:
  7.2 343.5 %all-reduce.9.cloned.1.call-start = ((), (), s32[]{:S(2)}) async-start(), calls=%async_computation | async-start | bytes 30191616
  45.6 1143.1 %all-reduce.13.cloned.1.call-start = ((), (), s32[]{:S(2)}) async-start(), calls=%async_computation.2 | async-start | bytes 3776512
  47.7 331.6 %copy-start.51 = (bf16[2,64]{1,0:T(2,128)(2,1)}, bf16[2,64]{1,0:T(2,128)(2,1)S(1)}, u32[]{:S(2)}) copy-start(bf16[2,64]{1,0:T(2,128)(2,1)S(1)} %get-tuple-element.41) | copy-start | bytes 772
  47.7 331.6 %copy-start.53 = (bf16[2,64]{1,0:T(2,128)(2,1)}, bf16[2,64]{1,0:T(2,128)(2,1)S(1)}, u32[]{:S(2)}) copy-start(bf16[2,64]{1,0:T(2,128)(2,1)S(1)} %get-tuple-element.42) | copy-start | bytes 772
  359.1 8.3 slice-start.6
  367.3 2.4 slice-start.8
  388.7 3.3 copy-start.16
  389.0 3.0 copy-start.24
  390.0 2.8 copy-start.1
  390.0 2.8 copy-start.6
  390.0 2.8 copy-start.41
  405.5 10.2 copy-start.9
  405.5 10.2 copy-start.30
  405.5 10.2 copy-start.32
  405.5 10.2 copy-start.38
  405.5 10.2 copy-start.46
  405.6 10.2 copy-start.55
  415.8 2.8 copy-start.40
  418.6 4.6 slice-start.10
  420.5 2.8 copy-start.22
  420.5 2.8 slice-start.11
  437.4 13.6 %copy-start.29 = (f32[256,768]{1,0:T(8,128)}, f32[256,768]{1,0:T(8,128)S(1)}, u32[]{:S(2)}) copy-start(f32[256,768]{1,0:T(8,128)S(1)} %convolution_add_fusion.2) | copy-start | bytes 2359300
  438.1 12.9 %copy-start.28 = (bf16[256,3072]{1,0:T(8,128)(2,1)S(1)}, bf16[256,3072]{1,0:T(8,128)(2,1)}, u32[]{:S(2)}) copy-start(bf16[256,3072]{1,0:T(8,128)(2,1)} %copy-done.27) | copy-start | bytes 4718596
  438.1 12.9 %copy-start.31 = (f32[768]{0:T(1024)S(1)}, f32[768]{0:T(1024)}, u32[]{:S(2)}) copy-start(f32[768]{0:T(1024)} %get-tuple-element.28) | copy-start | bytes 9220
  438.1 12.8 %copy-start.33 = (f32[768]{0:T(1024)S(1)}, f32[768]{0:T(1024)}, u32[]{:S(2)}) copy-start(f32[768]{0:T(1024)} %get-tuple-element.27) | copy-start | bytes 9220
  438.1 12.8 %copy-start.39 = (f32[256]{0:T(256)S(1)}, f32[256]{0:T(256)}, u32[]{:S(2)}) copy-start(f32[256]{0:T(256)} %copy-done.37) | copy-start | bytes 3076
  438.1 12.8 %copy-start.47 = (f32[256]{0:T(256)S(1)}, f32[256]{0:T(256)}, u32[]{:S(2)}) copy-start(f32[256]{0:T(256)} %fusion.45) | copy-start | bytes 3076
  451.0 5.2 copy-start.20
  451.0 5.2 copy-start.23
  456.2 5.4 copy-start.52
  456.2 5.4 copy-start.54
  469.3 8.1 copy-start.2
  488.4 10.8 copy-start.8
  499.2 9.6 slice-start.3
  500.5 6.8 copy-start.3
  500.5 8.6 slice-start.4
  500.5 9.3 slice-start.5
  507.2 7.5 slice-start
  509.8 5.1 slice-start.1
  509.8 6.0 slice-start.2
  515.8 9.1 copy-start.45
  515.9 10.4 copy-start.57
  515.9 11.7 copy-start.56
  515.9 13.0 %copy-start.48 = (f32[3072]{0:T(1024)S(1)}, f32[3072]{0:T(1024)}, u32[]{:S(2)}) copy-start(f32[3072]{0:T(1024)} %get-tuple-element.15) | copy-start | bytes 36868
  515.9 13.6 %copy-start.44 = (f32[768]{0:T(1024)S(1)}, f32[768]{0:T(1024)}, u32[]{:S(2)}) copy-start(f32[768]{0:T(1024)} %get-tuple-element.13) | copy-start | bytes 9220
  515.9 14.9 %copy-start.43 = (f32[768]{0:T(1024)S(1)}, f32[768]{0:T(1024)}, u32[]{:S(2)}) copy-start(f32[768]{0:T(1024)} %get-tuple-element.7) | copy-start | bytes 9220
  515.9 16.2 %copy-start.42 = (f32[768]{0:T(1024)S(1)}, f32[768]{0:T(1024)}, u32[]{:S(2)}) copy-start(f32[768]{0:T(1024)} %convert_reduce_fusion.1) | copy-start | bytes 9220
  1123.3 138.9 %all-reduce.11.cloned.1.call-start = ((), (), s32[]{:S(2)}) async-start(), calls=%async_computation.1 | async-start | bytes 3776512
  (31 other events, 48.4 us)
Sparse Core Ops, SparseCore 0:
  45.7 305.0 all-reduce.8
  1123.4 65.1 all-reduce.12
  1195.9 66.2 all-reduce.10
where the time goes:
time: 1290 us; the launch traced here: 1280 us
  blocking collectives  586 us (45%)
  waiting for transfers between devices  434 us (34%)
  local copies, waits for them, and re-layouts  159 us (12%)
  matrix products  58.8 us (5%)
  other arithmetic  23.2 us (2%)
  between operations  17.3 us (1%)
    unnamed x1, blocking collectives  586 us
    unnamed x6, waiting for transfers between devices  434 us
    unnamed x171, local copies, waits for them, and re-layouts  94.1 us
    reshape x6, local copies, waits for them, and re-layouts, split_flat(): pieces.append(flat_vec[offset:offset + extent].reshape(seg_shape))  26.9 us
  transfers between devices with their start and end apart: 3, of which 3 were waited for; matrix products, arithmetic and copies ran while one was open for 0% of the time, Pallas kernels for 0%

commit v1 on v0

v1 whole, which is shorter than its diff:
```python
import math

import jax
import jax.numpy as jnp
from jax import lax
from jax.experimental import pallas as pl
from jax.experimental.pallas import tpu as pltpu
from jax.sharding import PartitionSpec as P

D = 768
HEADS = 12
HEAD_DIM = 64
FF = 3072
TFREQ = 128
THID = 512
STEP = 10
MATS = 7536640
L = 128

NORM_EPS = 1e-05
ADAM_EPS = 1e-08
BETA_ONE = 0.5
BETA_TWO = 0.5
RATE_MATRIX = 0.02
RATE_SMALL = 0.2
WEIGHT_DECAY = 0.01

LANES = 128
ROUND = 16

TIME_IN, TIME_OUT, QKV, OUT, UP, DOWN, VEC = range(7)
MATRICES = [(TFREQ, THID), (THID, D), (D, 3 * D), (D, D), (D, FF), (FF, D), (82, LANES)]
VEC_ROWS = 96
V_TIME_IN, V_TIME_OUT, V_Q, V_V, V_OUT, V_GAIN1, V_SHIFT1, V_UP, V_DOWN, V_GAIN2, V_SHIFT2 = (
    0, 4, 10, 16, 22, 28, 34, 40, 64, 70, 76,
)

F32 = jnp.float32
BF16 = jnp.bfloat16


def up_to(value, step):
    return -(-value // step) * step


class Geometry:
    def __init__(self, total, shards):
        self.shards = shards
        self.length = total // shards
        self.offsets = []
        offset = 0
        for rows, cols in MATRICES:
            self.offsets.append(offset)
            offset += rows * cols
        assert offset == total and total % shards == 0
        self.regions = []
        for index in range(shards):
            low, high = index * self.length, (index + 1) * self.length
            base, found = 0, []
            for matrix, (rows, cols) in enumerate(MATRICES):
                start, stop = max(low, self.offsets[matrix]), min(high, self.offsets[matrix] + rows * cols)
                if start >= stop:
                    continue
                first = (start - self.offsets[matrix]) // cols // ROUND * ROUND
                last = up_to(up_to(stop - self.offsets[matrix], cols) // cols, ROUND)
                found.append((matrix, first, last, base))
                base += (last - first) * (cols // LANES)
            self.regions.append(found)
        used = [
            sum((last - first) * (MATRICES[matrix][1] // LANES) for matrix, first, last, _ in found)
            for found in self.regions
        ]
        self.rows = up_to(max(used), 8 * ROUND)
        self.quarter = self.rows // 4
        self.runs = []
        for matrix, (rows, cols) in enumerate(MATRICES):
            groups = []
            for group in range(up_to(rows, ROUND) // ROUND):
                row = group * ROUND
                places = []
                for index, found in enumerate(self.regions):
                    for which, first, last, base in found:
                        if which == matrix and first <= row < last:
                            places.append((index, first, last, base))
                assert places
                groups.append((row, places))
            runs = []
            for row, places in groups:
                if runs and runs[-1][2] == places:
                    runs[-1][1] = row + ROUND
                else:
                    runs.append([row, row + ROUND, places])
            self.runs.append([tuple(run) for run in runs])
        self.margin = ROUND * (FF // LANES)
        self.flat_rows = up_to(up_to(self.length, LANES) // LANES + 1, 8)
        self.buffer_rows = self.margin + self.flat_rows + self.margin + 8

    def table(self):
        out = []
        for index, found in enumerate(self.regions):
            line = [[0, 0, 0] for _ in MATRICES]
            first_row = index * self.length // LANES
            for matrix, first, last, base in found:
                width = MATRICES[matrix][1] // LANES
                start = self.offsets[matrix] // LANES + first * width - first_row + self.margin
                line[matrix] = [start, (last - first) // ROUND, base]
            out.extend(value for item in line for value in item)
        return jnp.array(out, jnp.int32)


def aligned(value, step=ROUND):
    return value if isinstance(value, int) else pl.multiple_of(value, step)


def spread_steps(length):
    steps = 4
    return steps, up_to(-(-length // steps), 8 * 1024)


def region_loop(table, index, body):
    for matrix, (_, cols) in enumerate(MATRICES):
        width = cols // LANES
        at = (index * len(MATRICES) + matrix) * 3
        start, groups, base = table[at], table[at + 1], table[at + 2]

        def group_step(group, carry, width=width, start=start, groups=groups, base=base):
            for column in range(width):
                flat = start + group * (ROUND * width) + column
                place = pl.multiple_of(base + (column * groups + group) * ROUND, ROUND)
                body(flat, width, place)
            return carry

        lax.fori_loop(0, groups, group_step, 0)


def pack_block(geo, params, where):
    steps, chunk = spread_steps(geo.length)
    rows = chunk // LANES

    def kernel(where_ref, table_ref, params_ref, block_ref, quarter_ref, buffer):
        step = pl.program_id(0)
        index = where_ref[0]
        shift = (index * geo.length) % LANES

        @pl.when(step == 0)
        def _():
            buffer[pl.ds(0, geo.margin), :] = jnp.zeros((geo.margin, LANES), F32)
            tail = geo.margin + geo.flat_rows - 8
            rest = buffer.shape[0] - tail
            buffer[pl.ds(tail, rest), :] = jnp.zeros((rest, LANES), F32)

        place = lax.broadcasted_iota(jnp.int32, (64, LANES), 0) * LANES + lax.broadcasted_iota(
            jnp.int32, (64, LANES), 1
        )

        def roll_in(part, carry):
            value = params_ref[pl.ds(pl.multiple_of(part * 8192, 8192), 8192)].reshape(64, LANES)
            before = step * chunk + part * 8192
            value = jnp.where(place + before < geo.length, value, 0.0)
            at = pl.multiple_of(geo.margin + step * rows + part * 64, 8)
            buffer[pl.ds(at, 64), :] = pltpu.roll(value, shift, 1)
            return carry

        lax.fori_loop(0, chunk // 8192, roll_in, 0)

        @pl.when(step == steps - 1)
        def _():
            late = lax.broadcasted_iota(jnp.int32, (ROUND, LANES), 1) >= shift

            def move(flat, width, place):
                here = buffer[pl.ds(flat, ROUND, stride=width), :]
                above = buffer[pl.ds(flat - 1, ROUND, stride=width), :]
                block_ref[pl.ds(place, ROUND), :] = jnp.where(late, here, above).astype(BF16)

            region_loop(table_ref, index, move)
            mine = pl.multiple_of(where_ref[1] * geo.quarter, ROUND)
            quarter_ref[...] = block_ref[pl.ds(mine, geo.quarter), :]

    buffer_rows = geo.margin + max(steps * rows, geo.flat_rows) + geo.margin + 8
    return pl.pallas_call(
        kernel,
        grid=(steps,),
        in_specs=[
            pl.BlockSpec(memory_space=pltpu.SMEM),
            pl.BlockSpec(memory_space=pltpu.SMEM),
            pl.BlockSpec((chunk,), lambda i: (i,)),
        ],
        out_specs=[
            pl.BlockSpec((geo.rows, LANES), lambda i: (0, 0)),
            pl.BlockSpec((geo.quarter, LANES), lambda i: (0, 0)),
        ],
        out_shape=[
            jax.ShapeDtypeStruct((geo.rows, LANES), BF16),
            jax.ShapeDtypeStruct((geo.quarter, LANES), BF16),
        ],
        scratch_shapes=[pltpu.VMEM((buffer_rows, LANES), F32)],
        compiler_params=pltpu.CompilerParams(vmem_limit_bytes=32 * 2**20),
        name="pack_block",
    )(where, geo.table(), params)


def optimizer_step(geo, params, moment_one, moment_two, where, pieces, piece_places):
    steps, chunk = spread_steps(geo.length)
    rows = chunk // LANES
    count = len(pieces)
    corr_one = 1.0 - BETA_ONE**STEP
    corr_two = 1.0 - BETA_TWO**STEP

    def kernel(where_ref, table_ref, *refs):
        piece_refs = refs[:count]
        params_ref, one_ref, two_ref, new_params_ref, new_one_ref, new_two_ref, block, buffer, sems = refs[count:]
        step = pl.program_id(0)
        index = where_ref[0]
        shift = (index * geo.length) % LANES

        @pl.when(step == 0)
        def _():
            places = piece_places(index, where_ref[1])
            copies = [
                pltpu.make_async_copy(ref, block.at[pl.ds(aligned(at), ref.shape[0]), :], sems.at[i])
                for i, (ref, at) in enumerate(zip(piece_refs, places))
            ]
            for copy in copies:
                copy.start()
            for copy in copies:
                copy.wait()

            def move(flat, width, place):
                buffer[pl.ds(flat, ROUND, stride=width), :] = block[pl.ds(place, ROUND), :].astype(F32)

            region_loop(table_ref, index, move)

        late = lax.broadcasted_iota(jnp.int32, (64, LANES), 1) >= shift
        place = lax.broadcasted_iota(jnp.int32, (64, LANES), 0) * LANES + lax.broadcasted_iota(
            jnp.int32, (64, LANES), 1
        )

        def update(part, carry):
            at = geo.margin + step * rows + part * 64
            here = buffer[pl.ds(pl.multiple_of(at, 8), 64), :]
            below = buffer[pl.ds(at + 1, 64), :]
            grad = pltpu.roll(jnp.where(late, here, below), LANES - shift, 1)
            span = pl.ds(pl.multiple_of(part * 8192, 8192), 8192)
            old = params_ref[span].reshape(64, LANES)
            new_one = BETA_ONE * one_ref[span].reshape(64, LANES) + (1.0 - BETA_ONE) * grad
            new_two = BETA_TWO * two_ref[span].reshape(64, LANES) + (1.0 - BETA_TWO) * grad * grad
            is_matrix = place + (index * geo.length + step * chunk + part * 8192) < MATS
            rates = jnp.where(is_matrix, RATE_MATRIX, RATE_SMALL)
            decays = jnp.where(is_matrix, WEIGHT_DECAY, 0.0)
            change = new_one / corr_one / (jnp.sqrt(new_two / corr_two) + ADAM_EPS)
            new_params_ref[span] = (old - rates * (change + decays * old)).reshape(8192)
            new_one_ref[span] = new_one.reshape(8192)
            new_two_ref[span] = new_two.reshape(8192)
            return carry

        lax.fori_loop(0, chunk // 8192, update, 0)

    buffer_rows = geo.margin + max(steps * rows, geo.flat_rows) + geo.margin + 8
    flat_spec = pl.BlockSpec((chunk,), lambda i: (i,))
    flat_shape = jax.ShapeDtypeStruct((geo.length,), F32)
    return pl.pallas_call(
        kernel,
        grid=(steps,),
        in_specs=[pl.BlockSpec(memory_space=pltpu.SMEM)] * 2
        + [pl.BlockSpec(memory_space=pl.ANY)] * count
        + [flat_spec] * 3,
        out_specs=[flat_spec] * 3,
        out_shape=[flat_shape] * 3,
        scratch_shapes=[
            pltpu.VMEM((geo.rows, LANES), BF16),
            pltpu.VMEM((buffer_rows, LANES), F32),
            pltpu.SemaphoreType.DMA((count,)),
        ],
        compiler_params=pltpu.CompilerParams(vmem_limit_bytes=48 * 2**20),
        name="optimizer_step",
    )(where, geo.table(), *pieces, params, moment_one, moment_two)


def nn(left, right):
    return lax.dot_general(left, right, (((1,), (0,)), ((), ())), preferred_element_type=F32)


def nt(left, right):
    return lax.dot_general(left, right, (((1,), (1,)), ((), ())), preferred_element_type=F32)


def norm_parts(values):
    center = values - jnp.mean(values, axis=-1, keepdims=True)
    inverse = lax.rsqrt(jnp.mean(center * center, axis=-1, keepdims=True) + NORM_EPS)
    return center * inverse, inverse


def norm_back(scaled, hat, inverse):
    return inverse * (
        scaled
        - jnp.mean(scaled, axis=-1, keepdims=True)
        - hat * jnp.mean(scaled * hat, axis=-1, keepdims=True)
    )


def model_step(geo, tokens, cotangent, lengths, sinusoid, where, weights, weight_places, outs_of):
    seqs = tokens.shape[0] // L
    rows = tokens.shape[0]
    count = len(weights)
    pairs = HEADS // 2
    grads = geo.shards
    scale = HEAD_DIM ** (-0.5)

    def kernel(where_ref, lengths_ref, tokens_ref, cotangent_ref, sinusoid_ref, *refs):
        weight_refs = refs[:count]
        refs = refs[count:]
        output_ref, token_grad_ref = refs[:2]
        grad_refs = refs[2 : 2 + grads] if outs_of else refs[2:3]
        (
            store, vecs, vec_grads, rows_zero, rows_low, qkv, probs, context, hat_one, hidden, hidden_low, hidden_t,
            act, slope, total, d_hidden, d_qkv, in_sems, out_sems,
        ) = refs[2 + len(grad_refs) :]

        index, replica = where_ref[0], where_ref[1]
        copies = []
        for i, (ref, (block, at)) in enumerate(zip(weight_refs, weight_places(index, replica))):
            target = store if block is None else store.at[block, pl.ds(aligned(at), ref.shape[0]), :]
            copies.append(pltpu.make_async_copy(ref, target, in_sems.at[i]))
        for copy in copies:
            copy.start()
        for copy in copies:
            copy.wait()

        def spans(matrix, low, high):
            for first, last, places in geo.runs[matrix]:
                start, stop = max(first, low), min(last, high)
                if start < stop:
                    yield start, stop, places

        def ref_rows(place, column, start, stop):
            block, first, last, base = place
            at = base + column * (last - first) + start - first
            return store.at[block, pl.ds(aligned(at), stop - start), :]

        def load(matrix, column, low=0, high=None):
            parts = []
            for start, stop, places in spans(matrix, low, high or up_to(MATRICES[matrix][0], ROUND)):
                value = ref_rows(places[0], column, start, stop)[...]
                for place in places[1:]:
                    value = value + ref_rows(place, column, start, stop)[...]
                parts.append(value)
            return parts[0] if len(parts) == 1 else jnp.concatenate(parts, axis=0)

        def load_wide(matrix, column, wide, low=0, high=None):
            return jnp.concatenate([load(matrix, column + i, low, high) for i in range(wide)], axis=1)

        def save(matrix, column, value, low=0):
            for start, stop, places in spans(matrix, low, low + value.shape[0]):
                for place in places:
                    ref_rows(place, column, start, stop)[...] = value[start - low : stop - low, :]

        def save_wide(matrix, column, value, low=0):
            value = value.astype(BF16)
            for i in range(value.shape[1] // LANES):
                save(matrix, column + i, value[:, i * LANES : (i + 1) * LANES], low)

        def vec(row, wide):
            return jnp.concatenate([vecs[pl.ds(row + i, 1), :] for i in range(wide)], axis=1)

        def vec_grad(row, value):
            sums = jnp.sum(value, axis=0, keepdims=True)
            for i in range(sums.shape[1] // LANES):
                vec_grads[pl.ds(row + i, 1), :] = sums[:, i * LANES : (i + 1) * LANES]

        vecs[...] = load(VEC, 0).astype(F32)
        vec_grads[...] = jnp.zeros((VEC_ROWS, LANES), F32)

        sines = sinusoid_ref[...]
        time_pre = nn(sines, load_wide(TIME_IN, 0, 4)) + vec(V_TIME_IN, 4)
        time_gate = 1.0 / (1.0 + jnp.exp(-time_pre))
        time_act = (time_pre * time_gate).astype(BF16)
        time_emb = nn(time_act, load_wide(TIME_OUT, 0, 6)) + vec(V_TIME_OUT, 6)
        for seq in range(seqs):
            span = pl.ds(seq * L, L)
            value = tokens_ref[span, :].astype(F32) + time_emb[seq : seq + 1, :]
            rows_zero[span, :] = value
            rows_low[span, :] = value.astype(BF16)

        for tile in range(9):
            value = nn(rows_low[...], load_wide(QKV, 2 * tile, 2))
            if tile < 3:
                value = value + vec(V_Q + 2 * tile, 2)
            if tile >= 6:
                value = value + vec(V_V + 2 * (tile - 6), 2)
            qkv[:, tile * 256 : (tile + 1) * 256] = value.astype(BF16)

        first_head = lax.broadcasted_iota(jnp.int32, (L, LANES), 1) < HEAD_DIM

        def split_heads(value):
            zero = jnp.zeros_like(value)
            return jnp.concatenate([jnp.where(first_head, value, zero), jnp.where(first_head, zero, value)], axis=0)

        def both(value):
            return jnp.concatenate([jnp.broadcast_to(item, (L, L)) for item in value], axis=1)

        def pair_at(seq, pair, part):
            return qkv[pl.ds(seq * L, L), pl.ds(part * D + pair * LANES, LANES)]

        key = lax.broadcasted_iota(jnp.int32, (L, 2 * L), 1) % L
        for seq in range(seqs):
            valid = key < lengths_ref[seq]
            for pair in range(pairs):
                scores = nt(pair_at(seq, pair, 0), split_heads(pair_at(seq, pair, 1))) * scale
                scores = jnp.where(valid, scores, -1e30)
                top = both([jnp.max(scores[:, i * L : (i + 1) * L], axis=1, keepdims=True) for i in range(2)])
                power = jnp.exp(scores - top)
                sums = [jnp.sum(power[:, i * L : (i + 1) * L], axis=1, keepdims=True) for i in range(2)]
                weight = power * both([1.0 / item for item in sums])
                probs[seq * pairs + pair] = weight
                value = nn(weight.astype(BF16), split_heads(pair_at(seq, pair, 2)))
                context[pl.ds(seq * L, L), pl.ds(pair * LANES, LANES)] = value.astype(BF16)

        for tile in range(3):
            cols = pl.ds(tile * 256, 256)
            value = nn(context[...], load_wide(OUT, 2 * tile, 2)) + vec(V_OUT + 2 * tile, 2)
            total[:, cols] = rows_zero[:, cols] + value
        hat, inverse_one = norm_parts(total[...])
        hat_one[...] = hat
        gain_one = vec(V_GAIN1, 6)
        value = hat * gain_one + vec(V_SHIFT1, 6)
        hidden[...] = value
        hidden_low[...] = value.astype(BF16)
        hidden_t[...] = value.astype(BF16).T

        def up_step(tile, carry):
            pre = nn(hidden_low[...], load_wide(UP, 2 * tile, 2)) + vec(V_UP + 2 * tile, 2)
            below = 0.5 * (1.0 + lax.erf(pre * (0.5**0.5)))
            cols = pl.ds(aligned(tile * 256, 256), 256)
            act[:, cols] = (pre * below).astype(BF16)
            slope[:, cols] = below + pre * (jnp.exp(-0.5 * pre * pre) * (1.0 / math.sqrt(2.0 * math.pi)))
            return carry

        lax.fori_loop(0, 12, up_step, 0)
        for tile in range(3):
            cols = pl.ds(tile * 256, 256)
            value = nn(act[...], load_wide(DOWN, 2 * tile, 2)) + vec(V_DOWN + 2 * tile, 2)
            total[:, cols] = hidden[:, cols] + value

        hat, inverse = norm_parts(total[...])
        gain_two = vec(V_GAIN2, 6)
        output_ref[...] = (hat * gain_two + vec(V_SHIFT2, 6)).astype(BF16)
        d_result = cotangent_ref[...].astype(F32)
        vec_grad(V_GAIN2, d_result * hat)
        vec_grad(V_SHIFT2, d_result)
        value = norm_back(d_result * gain_two, hat, inverse)
        d_hidden[...] = value
        d_down = value.astype(BF16)
        vec_grad(V_DOWN, d_down.astype(F32))

        for tile in range(12):
            low, high = tile * 256, (tile + 1) * 256
            cols = pl.ds(low, 256)
            d_act = nt(d_down, load_wide(DOWN, 0, 6, low, high))
            save_wide(DOWN, 0, nn(act[:, cols].T, d_down), low)
            d_up = (d_act * slope[:, cols]).astype(BF16)
            vec_grad(V_UP + 2 * tile, d_up.astype(F32))
            d_hidden[...] += nt(d_up, load_wide(UP, 2 * tile, 2))
            save_wide(UP, 2 * tile, nn(hidden_t[...], d_up))

        d_out = d_hidden[...]
        hat = hat_one[...]
        vec_grad(V_GAIN1, d_out * hat)
        vec_grad(V_SHIFT1, d_out)
        value = norm_back(d_out * gain_one, hat, inverse_one)
        total[...] = value
        d_attn = value.astype(BF16)
        vec_grad(V_OUT, d_attn.astype(F32))
        d_context = nt(d_attn, load_wide(OUT, 0, 6)).astype(BF16)
        context_t = context[...].T
        for tile in range(3):
            save_wide(OUT, 2 * tile, nn(context_t, d_attn[:, tile * 256 : (tile + 1) * 256]))
        context[...] = d_context

        for seq in range(seqs):
            span = pl.ds(seq * L, L)
            for pair in range(pairs):
                weight = probs[seq * pairs + pair]
                d_pair = context[span, pl.ds(pair * LANES, LANES)]
                query, keys = pair_at(seq, pair, 0), pair_at(seq, pair, 1)
                d_weight = nt(d_pair, split_heads(pair_at(seq, pair, 2)))
                mixed = weight * d_weight
                delta = both([jnp.sum(mixed[:, i * L : (i + 1) * L], axis=1, keepdims=True) for i in range(2)])
                d_scores = (weight * (d_weight - delta)).astype(BF16)
                d_query = nn(d_scores, split_heads(keys)) * scale
                stacked = nn(d_scores.T, query)
                d_key = jnp.where(first_head, stacked[:L], stacked[L:]) * scale
                stacked = nn(weight.astype(BF16).T, d_pair)
                d_value = jnp.where(first_head, stacked[:L], stacked[L:])
                for part, item in enumerate((d_query, d_key, d_value)):
                    d_qkv[span, pl.ds(part * D + pair * LANES, LANES)] = item.astype(BF16)

        rows_t = rows_low[...].T
        for tile in range(9):
            value = d_qkv[:, tile * 256 : (tile + 1) * 256]
            if tile < 3:
                vec_grad(V_Q + 2 * tile, value.astype(F32))
            if tile >= 6:
                vec_grad(V_V + 2 * (tile - 6), value.astype(F32))
            total[...] += nt(value, load_wide(QKV, 2 * tile, 2))
            save_wide(QKV, 2 * tile, nn(rows_t, value))
        d_rows = total[...]
        token_grad_ref[...] = d_rows

        d_time = [jnp.sum(d_rows[seq * L : (seq + 1) * L], axis=0, keepdims=True) for seq in range(seqs)]
        d_time = jnp.concatenate(d_time + [jnp.zeros((sines.shape[0] - seqs, D), F32)], axis=0).astype(BF16)
        vec_grad(V_TIME_OUT, d_time.astype(F32))
        d_time_act = nt(d_time, load_wide(TIME_OUT, 0, 6))
        save_wide(TIME_OUT, 0, nn(time_act.T, d_time))
        d_time_pre = (d_time_act * (time_gate * (1.0 + time_pre * (1.0 - time_gate)))).astype(BF16)
        vec_grad(V_TIME_IN, d_time_pre.astype(F32))
        save_wide(TIME_IN, 0, nn(sines.T, d_time_pre))
        save(VEC, 0, vec_grads[...].astype(BF16))

        if outs_of:
            copies = [
                pltpu.make_async_copy(store.at[block], ref, out_sems.at[i])
                for i, (ref, block) in enumerate(zip(grad_refs, outs_of(index)))
            ]
        else:
            copies = [pltpu.make_async_copy(store, grad_refs[0], out_sems.at[0])]
        for copy in copies:
            copy.start()
        for copy in copies:
            copy.wait()

    if outs_of:
        grad_shapes = [jax.ShapeDtypeStruct((geo.rows, LANES), BF16)] * grads
    else:
        grad_shapes = [jax.ShapeDtypeStruct((geo.shards, geo.rows, LANES), BF16)]
    whole = pl.BlockSpec(memory_space=pltpu.VMEM)
    return pl.pallas_call(
        kernel,
        in_specs=[pl.BlockSpec(memory_space=pltpu.SMEM)] * 2
        + [whole] * 3
        + [pl.BlockSpec(memory_space=pl.ANY)] * count,
        out_specs=[whole] * 2 + [pl.BlockSpec(memory_space=pl.ANY)] * len(grad_shapes),
        out_shape=[jax.ShapeDtypeStruct((rows, D), BF16), jax.ShapeDtypeStruct((rows, D), F32)] + grad_shapes,
        scratch_shapes=[
            pltpu.VMEM((geo.shards, geo.rows, LANES), BF16),
            pltpu.VMEM((VEC_ROWS, LANES), F32),
            pltpu.VMEM((VEC_ROWS, LANES), F32),
            pltpu.VMEM((rows, D), F32),
            pltpu.VMEM((rows, D), BF16),
            pltpu.VMEM((rows, 3 * D), BF16),
            pltpu.VMEM((seqs * pairs, L, 2 * L), F32),
            pltpu.VMEM((rows, D), BF16),
            pltpu.VMEM((rows, D), F32),
            pltpu.VMEM((rows, D), F32),
            pltpu.VMEM((rows, D), BF16),
            pltpu.VMEM((D, rows), BF16),
            pltpu.VMEM((rows, FF), BF16),
            pltpu.VMEM((rows, FF), F32),
            pltpu.VMEM((rows, D), F32),
            pltpu.VMEM((rows, D), F32),
            pltpu.VMEM((rows, 3 * D), BF16),
            pltpu.SemaphoreType.DMA((count,)),
            pltpu.SemaphoreType.DMA((len(grad_shapes),)),
        ],
        compiler_params=pltpu.CompilerParams(vmem_limit_bytes=60 * 2**20),
        name="model_step",
    )(where, lengths, tokens, cotangent, sinusoid, *weights)


def neighbor_quarters(index, replica):
    core = index % 2
    return replica, replica ^ (1 + core), replica ^ (2 - core), replica ^ 3


def add_cores(geo, keep, got, where):
    size = geo.quarter

    def kernel(where_ref, keep_ref, got_ref, near_ref, far_ref):
        order = neighbor_quarters(where_ref[0], where_ref[1])
        for i, quarter in enumerate(order):
            span = pl.ds(pl.multiple_of(quarter * size, ROUND), size)
            value = (keep_ref[span, :].astype(F32) + got_ref[span, :].astype(F32)).astype(BF16)
            (near_ref if i < 2 else far_ref)[i % 2] = value

    whole = pl.BlockSpec(memory_space=pltpu.VMEM)
    return pl.pallas_call(
        kernel,
        in_specs=[pl.BlockSpec(memory_space=pltpu.SMEM), whole, whole],
        out_specs=[whole, whole],
        out_shape=[jax.ShapeDtypeStruct((2, size, LANES), BF16)] * 2,
        compiler_params=pltpu.CompilerParams(vmem_limit_bytes=32 * 2**20),
        name="add_cores",
    )(where, keep, got)


def add_pair(near, got):
    size = near.shape[1]

    def kernel(near_ref, got_ref, own_ref, next_ref):
        for i, ref in enumerate((own_ref, next_ref)):
            ref[...] = (near_ref[i].astype(F32) + got_ref[i].astype(F32)).astype(BF16)

    whole = pl.BlockSpec(memory_space=pltpu.VMEM)
    return pl.pallas_call(
        kernel,
        in_specs=[whole, whole],
        out_specs=[whole, whole],
        out_shape=[jax.ShapeDtypeStruct((size, LANES), BF16)] * 2,
        compiler_params=pltpu.CompilerParams(vmem_limit_bytes=32 * 2**20),
        name="add_pair",
    )(near, got)


def add_all(*items):
    def kernel(*refs):
        value = refs[0][...].astype(F32)
        for ref in refs[1:-1]:
            value = value + ref[...].astype(F32)
        refs[-1][...] = value.astype(BF16)

    whole = pl.BlockSpec(memory_space=pltpu.VMEM)
    return pl.pallas_call(
        kernel,
        in_specs=[whole] * len(items),
        out_specs=whole,
        out_shape=jax.ShapeDtypeStruct(items[0].shape, BF16),
        compiler_params=pltpu.CompilerParams(vmem_limit_bytes=32 * 2**20),
        name="add_all",
    )(*items)


def ring_order(size):
    return list(range(0, size, 2))[:1] + list(range(1, size, 2)) + list(range(size - 2, 0, -2))


def select(value, choices):
    out = jnp.int32(choices[0])
    for i, choice in enumerate(choices[1:], 1):
        out = jnp.where(value == i, choice, out)
    return out


def make_local(dp, fsdp):
    direct = dp == 4 and fsdp == 8
    chips = fsdp // 2
    order = ring_order(chips)
    before = [order[order.index(chip) - 1] for chip in range(chips)]

    def chip_before(chip, hops):
        table = list(range(chips))
        for _ in range(hops):
            table = [before[item] for item in table]
        return select(chip, table)

    def permute(value, axes, target):
        pairs = []
        for replica in range(dp):
            for index in range(fsdp):
                pairs.append((replica * fsdp + index, target(replica, index)))
        return lax.ppermute(value, axes, pairs)

    def core_swap(value):
        return lax.ppermute(value, "fsdp", [(index, index ^ 1) for index in range(fsdp)])

    def ring_hop(value):
        return lax.ppermute(
            value, "fsdp", [(before[chip] * 2 + core, chip * 2 + core) for chip in range(chips) for core in range(2)]
        )

    def first_way(value):
        return permute(value, ("dp", "fsdp"), lambda r, i: (r ^ (1 + i % 2)) * fsdp + i)

    def second_way(value):
        return permute(value, ("dp", "fsdp"), lambda r, i: (r ^ (2 - i % 2)) * fsdp + i)

    def local(tokens, lengths, timesteps, cotangent, params, moment_one, moment_two):
        geo = Geometry(params.shape[0] * fsdp, fsdp)
        where = jnp.stack([lax.axis_index("fsdp"), lax.axis_index("dp")]).astype(jnp.int32)
        seqs = tokens.shape[0]

        half_freq = TFREQ // 2
        frequencies = jnp.exp(-math.log(10000.0) * jnp.arange(half_freq, dtype=F32) / half_freq)
        angles = timesteps.astype(F32)[:, None] * frequencies[None, :]
        sinusoid = jnp.concatenate([jnp.cos(angles), jnp.sin(angles)], axis=1).astype(BF16)
        sinusoid = jnp.pad(sinusoid, ((0, up_to(seqs, ROUND) - seqs), (0, 0)))

        block, quarter = pack_block(geo, params, where)

        if direct:
            weights = [block, core_swap(block)]
            for _ in range(1, chips):
                quarter = ring_hop(quarter)
                one = first_way(quarter)
                two = second_way(quarter)
                three = second_way(one)
                four = [quarter, one, two, three]
                weights += four + [core_swap(item) for item in four]

            def weight_places(index, replica):
                chip, core = index // 2, index % 2
                places = [(index, 0), (index ^ 1, 0)]
                for hops in range(1, chips):
                    for whose in (index, index ^ 1):
                        source = chip_before(chip, hops) * 2 + whose % 2
                        places += [(source, item * geo.quarter) for item in neighbor_quarters(whose, replica)]
                return places

            def outs_of(index):
                chip, core = index // 2, index % 2
                out = []
                for hops in range(1, chips + 1):
                    other = chip_before(chip, hops)
                    out += [other * 2 + core, other * 2 + 1 - core]
                return out

        else:
            weights = [lax.all_gather(block, "fsdp", axis=0)]

            def weight_places(index, replica):
                return [(None, 0)]

            outs_of = None

        output, token_grad, *grads = model_step(
            geo,
            tokens.reshape(seqs * L, D),
            cotangent.reshape(seqs * L, D),
            lengths,
            sinusoid,
            where,
            weights,
            weight_places,
            outs_of,
        )

        if direct:
            passed = []
            for hops in range(chips):
                keep, send = grads[2 * hops], grads[2 * hops + 1]
                near, far = add_cores(geo, keep, core_swap(send), where)
                own, other = add_pair(near, second_way(far))
                quarter = add_all(own, first_way(other), *passed)
                if hops < chips - 1:
                    passed = [ring_hop(quarter)]
            one = first_way(quarter)
            pieces = [quarter, one, second_way(quarter), second_way(one)]

            def piece_places(index, replica):
                return [item * geo.quarter for item in neighbor_quarters(index, replica)]

        else:
            mine = lax.psum_scatter(grads[0], "fsdp", scatter_dimension=0)
            pieces = [lax.psum(mine, "dp")]

            def piece_places(index, replica):
                return [0]

        new_params, new_one, new_two = optimizer_step(
            geo, params, moment_one, moment_two, where, pieces, piece_places
        )
        return (
            output.reshape(tokens.shape),
            token_grad.reshape(tokens.shape),
            new_params,
            new_one,
            new_two,
        )

    return local


def solution(mesh):
    batch = P(("dp", "fsdp"))
    rows = P(("dp", "fsdp"), None, None)
    flat = P("fsdp")
    return jax.shard_map(
        make_local(mesh.shape["dp"], mesh.shape["fsdp"]),
        mesh=mesh,
        in_specs=(rows, batch, batch, rows, flat, flat, flat),
        out_specs=(rows, rows, flat, flat, flat),
        check_vma=False,
    )
```

time: 1290 us -> 261 us (0.20)
  blocking collectives: 586 us -> 0 us
  waiting for transfers between devices: 434 us -> 133 us
  local copies, waits for them, and re-layouts: 159 us -> 5.83 us
  Pallas kernels: 0 us -> 71.6 us
  matrix products: 58.8 us -> 0 us
  starting transfers between devices: 0.12 us -> 47.9 us
  other arithmetic: 23.2 us -> 0.87 us
  between operations: 17.3 us -> 1.28 us
    unnamed x1 -> x0, blocking collectives: 586 us -> none
    unnamed x6 -> x0, waiting for transfers between devices: 434 us -> none
    ppermute x0 -> x43, waiting for transfers between devices: none -> 133 us  [the longest x20 90.1 us: permute(): return lax.ppermute(value, axes, pairs)]
    unnamed x171 -> x76, local copies, waits for them, and re-layouts: 94.1 us -> 5.83 us
    pallas_call x0 -> x15, Pallas kernels: none -> 71.6 us  [the longest x1 37 us: model_step(): pl.pallas_call(kernel, in_specs=[pl.BlockSpec(memory_space=pltpu.SMEM)] *...]
    dot_general x23 -> x0, matrix products: 58.8 us -> none  [the longest x1 11.9 us: run_backward(): jnp.einsum('rd,re->de', context, d_attn, preferred_element_type=jnp.float32)]
    reshape x14 -> x0, local copies, waits for them, and re-layouts: 49.8 us -> none  [the longest x6 26.9 us: split_flat(): pieces.append(flat_vec[offset:offset + extent].reshape(seg_shape))]
    ppermute x0 -> x43, starting transfers between devices: none -> 47.9 us  [the longest x20 28.4 us: permute(): return lax.ppermute(value, axes, pairs)]
  transfers between devices with their start and end apart: 3 -> 43, of which waited for: 3 -> 18; matrix products, arithmetic and copies ran while one was open for 0% -> 0% of each run, Pallas kernels for 0% -> 2%
where the time goes in v1:
time: 261 us; the launch traced here: 260 us
  waiting for transfers between devices  133 us (51%)
  Pallas kernels  71.6 us (27%)
  starting transfers between devices  47.9 us (18%)
  local copies, waits for them, and re-layouts  5.83 us (2%)
    ppermute x20, waiting for transfers between devices, permute(): return lax.ppermute(value, axes, pairs)  90.1 us
    ppermute x6, waiting for transfers between devices, ring_hop(): lax.ppermute(value, 'fsdp', [(before[chip] * 2 + core, chip * 2 + core) f...  38.5 us
    pallas_call x1, Pallas kernels, model_step(): pl.pallas_call(kernel, in_specs=[pl.BlockSpec(memory_space=pltpu.SMEM)] *...  37 us
    ppermute x20, starting transfers between devices, permute(): return lax.ppermute(value, axes, pairs)  28.4 us
    pallas_call x1, Pallas kernels, optimizer_step(): pl.pallas_call(kernel, grid=(steps,), in_specs=[pl.BlockSpec(memory_space...  18.2 us
    ppermute x6, starting transfers between devices, ring_hop(): lax.ppermute(value, 'fsdp', [(before[chip] * 2 + core, chip * 2 + core) f...  14.9 us
    pallas_call x1, Pallas kernels, pack_block(): pl.pallas_call(kernel, grid=(steps,), in_specs=[pl.BlockSpec(memory_space...  10.8 us
    unnamed x76, local copies, waits for them, and re-layouts  5.83 us
  transfers between devices with their start and end apart: 43, of which 18 were waited for; matrix products, arithmetic and copies ran while one was open for 0% of the time, Pallas kernels for 2%

profile of v1, /device:TPU:0, one launch (start us, length us, event | category | flops | bytes accessed | tf_op | source)
XLA Modules:
  0.0 260.4 jit_solution(6176292113047397261)
XLA Ops:
  0.7 2.1 copy-done
  3.5 10.8 %pack_block.1 = (bf16[7936,128]{1,0:T(8,128)(2,1)S(1)}, bf16[1984,128]{1,0:T(8,128)(2,1)S(1)}) custom-call(s32[2]{0:T(128)S(1)} %pad_add_fusion.where_ref, s32[168]{0:T(256)S(1)} %copy-done.10, f32[943392]{0:T(1024)S(1)} %copy-done), custom_call_target="tpu_custom_call" | custom-call | tf_op jit(solution)/shard_map/pack_block/pallas_call | solution.py:180
  14.3 3.1 %collective-permute-start.1 = (bf16[1984,128]{1,0:T(8,128)(2,1)S(1)}, bf16[1984,128]{1,0:T(8,128)(2,1)S(1)}, u32[]{:S(2)}, u32[]{:S(2)}) collective-permute-start(bf16[1984,128]{1,0:T(8,128)(2,1)S(1)} %get-tuple-element.37), channel_id=1, source_target_pairs={{4,0},{5,1},{0,2},{1,3},{6,4},{7,5},{2,6},{3,7},{12,8},{13,9},{8,1... | collective-permute-start | bytes 1523720 | tf_op jit(solution)/shard_map/ppermute | solution.py:665
  17.4 12.5 %collective-permute-done.1.refs_2_ = bf16[1984,128]{1,0:T(8,128)(2,1)S(1)} collective-permute-done((bf16[1984,128]{1,0:T(8,128)(2,1)S(1)}, bf16[1984,128]{1,0:T(8,128)(2,1)S(1)}, u32[]{:S(2)}, u32[]{:S(2)}) %collective-permute-start.1) | collective-permute-done | bytes 507936 | tf_op jit(solution)/shard_map/ppermute | solution.py:665
  29.9 0.9 collective-permute-start.9
  30.8 1.5 collective-permute-start.3
  32.3 1.5 collective-permute-start.2
  33.8 9.9 %collective-permute-done.9.refs_10_ = bf16[1984,128]{1,0:T(8,128)(2,1)S(1)} collective-permute-done((bf16[1984,128]{1,0:T(8,128)(2,1)S(1)}, bf16[1984,128]{1,0:T(8,128)(2,1)S(1)}, u32[]{:S(2)}, u32[]{:S(2)}) %collective-permute-start.9) | collective-permute-done | bytes 507936 | tf_op jit(solution)/shard_map/ppermute | solution.py:665
  44.2 1.6 collective-permute-start.11
  45.9 1.4 collective-permute-start.10
  47.3 9.2 %collective-permute-done.17.refs_18_ = bf16[1984,128]{1,0:T(8,128)(2,1)S(1)} collective-permute-done((bf16[1984,128]{1,0:T(8,128)(2,1)S(1)}, bf16[1984,128]{1,0:T(8,128)(2,1)S(1)}, u32[]{:S(2)}, u32[]{:S(2)}) %collective-permute-start.17) | collective-permute-done | bytes 507936 | tf_op jit(solution)/shard_map/ppermute | solution.py:665
  57.6 1.9 collective-permute-start.4
  60.0 1.6 collective-permute-start.18
  61.6 8.2 %collective-permute-done.4.refs_5_ = bf16[1984,128]{1,0:T(8,128)(2,1)S(1)} collective-permute-done((bf16[1984,128]{1,0:T(8,128)(2,1)S(1)}, bf16[1984,128]{1,0:T(8,128)(2,1)S(1)}, u32[]{:S(2)}, u32[]{:S(2)}) %collective-permute-start.4) | collective-permute-done | bytes 507936 | tf_op jit(solution)/shard_map/ppermute | solution.py:659
  70.4 7.1 %collective-permute-done.19.refs_20_ = bf16[1984,128]{1,0:T(8,128)(2,1)S(1)} collective-permute-done((bf16[1984,128]{1,0:T(8,128)(2,1)S(1)}, bf16[1984,128]{1,0:T(8,128)(2,1)S(1)}, u32[]{:S(2)}, u32[]{:S(2)}) %collective-permute-start.19) | collective-permute-done | bytes 507936 | tf_op jit(solution)/shard_map/ppermute | solution.py:659
  77.5 1.9 collective-permute-start.12
  79.6 1.9 collective-permute-start.22
  81.5 5.0 %collective-permute-done.12.refs_13_ = bf16[1984,128]{1,0:T(8,128)(2,1)S(1)} collective-permute-done((bf16[1984,128]{1,0:T(8,128)(2,1)S(1)}, bf16[1984,128]{1,0:T(8,128)(2,1)S(1)}, u32[]{:S(2)}, u32[]{:S(2)}) %collective-permute-start.12) | collective-permute-done | bytes 507936 | tf_op jit(solution)/shard_map/ppermute | solution.py:659
  87.0 4.9 %collective-permute-done.20.refs_21_ = bf16[1984,128]{1,0:T(8,128)(2,1)S(1)} collective-permute-done((bf16[1984,128]{1,0:T(8,128)(2,1)S(1)}, bf16[1984,128]{1,0:T(8,128)(2,1)S(1)}, u32[]{:S(2)}, u32[]{:S(2)}) %collective-permute-start.20) | collective-permute-done | bytes 507936 | tf_op jit(solution)/shard_map/ppermute | solution.py:659
  92.9 1.0 collective-permute-done.24.refs_25_
  94.8 37.0 %model_step.1 = (bf16[256,768]{1,0:T(8,128)(2,1)}, f32[256,768]{1,0:T(8,128)}, bf16[7936,128]{1,0:T(8,128)(2,1)}, bf16[7936,128]{1,0:T(8,128)(2,1)}, bf16[7936,1...) custom-call(s32[2]{0:T(128)} %copy-done.7, ...), custom_call_target="tpu_custom_call" | custom-call | tf_op jit(solution)/shard_map/model_step/pallas_call | solution.py:536
  132.9 3.3 %collective-permute-done.34.got_ref = bf16[7936,128]{1,0:T(8,128)(2,1)S(1)} collective-permute-done((bf16[7936,128]{1,0:T(8,128)(2,1)}, bf16[7936,128]{1,0:T(8,128)(2,1)S(1)}, u32[]{:S(2)}, u32[]{:S(2)}) %collective-permute-start.34) | collective-permute-done | bytes 2031648 | tf_op jit(solution)/shard_map/ppermute | solution.py:662
  136.2 1.6 copy-done.6
  138.4 1.0 add_cores.7
  139.4 1.9 collective-permute-start.35
  141.3 1.0 add_cores.6
  142.9 1.0 add_cores.5
  143.9 1.6 collective-permute-start.29
  145.5 8.4 %collective-permute-done.35.got_ref = bf16[2,1984,128]{2,1,0:T(8,128)(2,1)S(1)} collective-permute-done((bf16[2,1984,128]{2,1,0:T(8,128)(2,1)S(1)}, bf16[2,1984,128]{2,1,0:T(8,128)(2,1)S(1)}, u32[]{:S(2)}, u32[]{:S(2)}) %collective-permute-start.35) | collective-permute-done | bytes 1015840 | tf_op jit(solution)/shard_map/ppermute | solution.py:659
  154.2 1.8 collective-permute-start.36
  156.0 1.0 add_cores.4
  157.0 2.0 collective-permute-start.26
  159.0 11.2 %collective-permute-done.32.got_ref = bf16[2,1984,128]{2,1,0:T(8,128)(2,1)S(1)} collective-permute-done((bf16[2,1984,128]{2,1,0:T(8,128)(2,1)S(1)}, bf16[2,1984,128]{2,1,0:T(8,128)(2,1)S(1)}, u32[]{:S(2)}, u32[]{:S(2)}) %collective-permute-start.32) | collective-permute-done | bytes 1015840 | tf_op jit(solution)/shard_map/ppermute | solution.py:659
  170.5 1.8 collective-permute-start.33
  172.5 3.5 %collective-permute-start.37 = (bf16[1984,128]{1,0:T(8,128)(2,1)S(1)}, bf16[1984,128]{1,0:T(8,128)(2,1)S(1)}, u32[]{:S(2)}, u32[]{:S(2)}) collective-permute-start(bf16[1984,128]{1,0:T(8,128)(2,1)S(1)} %add_all.4), channel_id=1, source_target_pairs={{4,0},{5,1},{0,2},{1,3},{6,4},{7,5},{2,6},{3,7},{12,8},{13,9},{8,1... | collective-permute-start | bytes 1523720 | tf_op jit(solution)/shard_map/ppermute | solution.py:665
  175.9 10.7 %collective-permute-done.29.got_ref = bf16[2,1984,128]{2,1,0:T(8,128)(2,1)S(1)} collective-permute-done((bf16[2,1984,128]{2,1,0:T(8,128)(2,1)S(1)}, bf16[2,1984,128]{2,1,0:T(8,128)(2,1)S(1)}, u32[]{:S(2)}, u32[]{:S(2)}) %collective-permute-start.29) | collective-permute-done | bytes 1015840 | tf_op jit(solution)/shard_map/ppermute | solution.py:659
  186.8 1.8 collective-permute-start.30
  188.8 3.5 %collective-permute-start.38 = (bf16[1984,128]{1,0:T(8,128)(2,1)S(1)}, bf16[1984,128]{1,0:T(8,128)(2,1)S(1)}, u32[]{:S(2)}, u32[]{:S(2)}) collective-permute-start(bf16[1984,128]{1,0:T(8,128)(2,1)S(1)} %add_all.5), channel_id=1, source_target_pairs={{4,0},{5,1},{0,2},{1,3},{6,4},{7,5},{2,6},{3,7},{12,8},{13,9},{8,1... | collective-permute-start | bytes 1523720 | tf_op jit(solution)/shard_map/ppermute | solution.py:665
  192.3 10.6 %collective-permute-done.26.got_ref = bf16[2,1984,128]{2,1,0:T(8,128)(2,1)S(1)} collective-permute-done((bf16[2,1984,128]{2,1,0:T(8,128)(2,1)S(1)}, bf16[2,1984,128]{2,1,0:T(8,128)(2,1)S(1)}, u32[]{:S(2)}, u32[]{:S(2)}) %collective-permute-start.26) | collective-permute-done | bytes 1015840 | tf_op jit(solution)/shard_map/ppermute | solution.py:659
  203.1 1.8 collective-permute-start.27
  205.2 3.5 %collective-permute-start.39 = (bf16[1984,128]{1,0:T(8,128)(2,1)S(1)}, bf16[1984,128]{1,0:T(8,128)(2,1)S(1)}, u32[]{:S(2)}, u32[]{:S(2)}) collective-permute-start(bf16[1984,128]{1,0:T(8,128)(2,1)S(1)} %add_all.6), channel_id=1, source_target_pairs={{4,0},{5,1},{0,2},{1,3},{6,4},{7,5},{2,6},{3,7},{12,8},{13,9},{8,1... | collective-permute-start | bytes 1523720 | tf_op jit(solution)/shard_map/ppermute | solution.py:665
  208.6 3.6 %collective-permute-done.27.refs_1_ = bf16[1984,128]{1,0:T(8,128)(2,1)S(1)} collective-permute-done((bf16[1984,128]{1,0:T(8,128)(2,1)S(1)}, bf16[1984,128]{1,0:T(8,128)(2,1)S(1)}, u32[]{:S(2)}, u32[]{:S(2)}) %collective-permute-start.27) | collective-permute-done | bytes 507936 | tf_op jit(solution)/shard_map/ppermute | solution.py:659
  212.2 6.9 %collective-permute-done.39.refs_2_ = bf16[1984,128]{1,0:T(8,128)(2,1)S(1)} collective-permute-done((bf16[1984,128]{1,0:T(8,128)(2,1)S(1)}, bf16[1984,128]{1,0:T(8,128)(2,1)S(1)}, u32[]{:S(2)}, u32[]{:S(2)}) %collective-permute-start.39) | collective-permute-done | bytes 507936 | tf_op jit(solution)/shard_map/ppermute | solution.py:665
  219.3 1.8 collective-permute-start.40
  221.4 11.6 %collective-permute-done.40.refs_1_ = bf16[1984,128]{1,0:T(8,128)(2,1)S(1)} collective-permute-done((bf16[1984,128]{1,0:T(8,128)(2,1)S(1)}, bf16[1984,128]{1,0:T(8,128)(2,1)S(1)}, u32[]{:S(2)}, u32[]{:S(2)}) %collective-permute-start.40) | collective-permute-done | bytes 507936 | tf_op jit(solution)/shard_map/ppermute | solution.py:659
  233.0 0.8 collective-permute-start.42
  233.8 8.2 %collective-permute-done.42.refs_3_ = bf16[1984,128]{1,0:T(8,128)(2,1)S(1)} collective-permute-done((bf16[1984,128]{1,0:T(8,128)(2,1)S(1)}, bf16[1984,128]{1,0:T(8,128)(2,1)S(1)}, u32[]{:S(2)}, u32[]{:S(2)}) %collective-permute-start.42) | collective-permute-done | bytes 507936 | tf_op jit(solution)/shard_map/ppermute | solution.py:659
  242.0 18.2 %optimizer_step.1 = (f32[943392]{0:T(1024)}, f32[943392]{0:T(1024)}, f32[943392]{0:T(1024)}) custom-call(s32[2]{0:T(128)S(1)} %copy-done.9, s32[168]{0:T(256)S(1)} %copy-done.11, bf16[1984,128]{1,0:T(8,128)(2,1)S(1)} %add_all.7.refs_0_, bf16[1984,128]{1,0:T(8,128)(2,1)S(1)} %collective-permute-done.40.refs_1_, ...), custom_call_target="tpu_custom_call" | custom-call | tf_op jit(solution)/shard_map/optimizer_step/pallas_call | solution.py:261
  (134 shorter events, 10.3 us)
Async XLA Ops:
  0.6 91.3 %copy-start.37 = (s32[2]{0:T(128)S(1)}, s32[2]{0:T(128)}, u32[]{:S(2)}) copy-start(s32[2]{0:T(128)} %param.11) | copy-start | bytes 28
  3.5 91.3 %copy-start.7 = (s32[2]{0:T(128)}, s32[2]{0:T(128)S(1)}, u32[]{:S(2)}) copy-start(s32[2]{0:T(128)S(1)} %pad_add_fusion.where_ref) | copy-start | bytes 28
  14.3 80.5 %copy-start.2 = (bf16[7936,128]{1,0:T(8,128)(2,1)}, bf16[7936,128]{1,0:T(8,128)(2,1)S(1)}, u32[]{:S(2)}) copy-start(bf16[7936,128]{1,0:T(8,128)(2,1)S(1)} %get-tuple-element.36.refs_0_) | copy-start | bytes 6094852
  14.3 15.6 %collective-permute-start.1 = (bf16[1984,128]{1,0:T(8,128)(2,1)S(1)}, bf16[1984,128]{1,0:T(8,128)(2,1)S(1)}, u32[]{:S(2)}, u32[]{:S(2)}) collective-permute-start(bf16[1984,128]{1,0:T(8,128)(2,1)S(1)} %get-tuple-element.37), channel_id=1, source_target_pairs={{4,0},{5,1},{0,2},{1,3},{6,4},{7,5},{2,6},{3,7},{12,8},{13,9},{8,1... | collective-permute-start | bytes 1523720 | tf_op jit(solution)/shard_map/ppermute | solution.py:665
  29.9 62.9 %copy-start.13 = (bf16[1984,128]{1,0:T(8,128)(2,1)}, bf16[1984,128]{1,0:T(8,128)(2,1)S(1)}, u32[]{:S(2)}) copy-start(bf16[1984,128]{1,0:T(8,128)(2,1)S(1)} %collective-permute-done.1.refs_2_) | copy-start | bytes 1523716
  29.9 13.8 %collective-permute-start.9 = (bf16[1984,128]{1,0:T(8,128)(2,1)S(1)}, bf16[1984,128]{1,0:T(8,128)(2,1)S(1)}, u32[]{:S(2)}, u32[]{:S(2)}) collective-permute-start(bf16[1984,128]{1,0:T(8,128)(2,1)S(1)} %collective-permute-done.1.refs_2_), channel_id=1, source_target_pairs={{4,0},{5,1},{0,2},{1,3},{6,4},{7,5},{2,6},{3,7},{12,8},{13,9},{8,1... | collective-permute-start | bytes 1523720 | tf_op jit(solution)/shard_map/ppermute | solution.py:665
  30.8 13.3 %collective-permute-start.5 = (bf16[1984,128]{1,0:T(8,128)(2,1)S(1)}, bf16[1984,128]{1,0:T(8,128)(2,1)S(1)}, u32[]{:S(2)}, u32[]{:S(2)}) collective-permute-start(bf16[1984,128]{1,0:T(8,128)(2,1)S(1)} %collective-permute-done.1.refs_2_), channel_id=1, source_target_pairs={{0,1},{1,0},{2,3},{3,2},{4,5},{5,4},{6,7},{7,6},{8,9},{9,8},{10,11... | collective-permute-start | bytes 1523720 | tf_op jit(solution)/shard_map/ppermute | solution.py:662
  30.8 14.9 %collective-permute-start.3 = (bf16[1984,128]{1,0:T(8,128)(2,1)S(1)}, bf16[1984,128]{1,0:T(8,128)(2,1)S(1)}, u32[]{:S(2)}, u32[]{:S(2)}) collective-permute-start(bf16[1984,128]{1,0:T(8,128)(2,1)S(1)} %collective-permute-done.1.refs_2_), channel_id=1, source_target_pairs={{0,16},{1,9},{2,18},{3,11},{4,20},{5,13},{6,22},{7,15},{8,24},{9,1... | collective-permute-start | bytes 1523720 | tf_op jit(solution)/shard_map/ppermute | solution.py:659
  32.3 13.6 %collective-permute-start.2 = (bf16[1984,128]{1,0:T(8,128)(2,1)S(1)}, bf16[1984,128]{1,0:T(8,128)(2,1)S(1)}, u32[]{:S(2)}, u32[]{:S(2)}) collective-permute-start(bf16[1984,128]{1,0:T(8,128)(2,1)S(1)} %collective-permute-done.1.refs_2_), channel_id=1, source_target_pairs={{0,8},{1,17},{2,10},{3,19},{4,12},{5,21},{6,14},{7,23},{8,0},{9,25... | collective-permute-start | bytes 1523720 | tf_op jit(solution)/shard_map/ppermute | solution.py:659
  43.7 49.1 %copy-start.14 = (bf16[1984,128]{1,0:T(8,128)(2,1)}, bf16[1984,128]{1,0:T(8,128)(2,1)S(1)}, u32[]{:S(2)}) copy-start(bf16[1984,128]{1,0:T(8,128)(2,1)S(1)} %collective-permute-done.9.refs_10_) | copy-start | bytes 1523716
  43.7 12.8 %collective-permute-start.17 = (bf16[1984,128]{1,0:T(8,128)(2,1)S(1)}, bf16[1984,128]{1,0:T(8,128)(2,1)S(1)}, u32[]{:S(2)}, u32[]{:S(2)}) collective-permute-start(bf16[1984,128]{1,0:T(8,128)(2,1)S(1)} %collective-permute-done.9.refs_10_), channel_id=1, source_target_pairs={{4,0},{5,1},{0,2},{1,3},{6,4},{7,5},{2,6},{3,7},{12,8},{13,9},{8,1... | collective-permute-start | bytes 1523720 | tf_op jit(solution)/shard_map/ppermute | solution.py:665
  44.2 12.4 %collective-permute-start.13 = (bf16[1984,128]{1,0:T(8,128)(2,1)S(1)}, bf16[1984,128]{1,0:T(8,128)(2,1)S(1)}, u32[]{:S(2)}, u32[]{:S(2)}) collective-permute-start(bf16[1984,128]{1,0:T(8,128)(2,1)S(1)} %collective-permute-done.9.refs_10_), channel_id=1, source_target_pairs={{0,1},{1,0},{2,3},{3,2},{4,5},{5,4},{6,7},{7,6},{8,9},{9,8},{10,11... | collective-permute-start | bytes 1523720 | tf_op jit(solution)/shard_map/ppermute | solution.py:662
  44.2 13.4 %collective-permute-start.11 = (bf16[1984,128]{1,0:T(8,128)(2,1)S(1)}, bf16[1984,128]{1,0:T(8,128)(2,1)S(1)}, u32[]{:S(2)}, u32[]{:S(2)}) collective-permute-start(bf16[1984,128]{1,0:T(8,128)(2,1)S(1)} %collective-permute-done.9.refs_10_), channel_id=1, source_target_pairs={{0,16},{1,9},{2,18},{3,11},{4,20},{5,13},{6,22},{7,15},{8,24},{9,1... | collective-permute-start | bytes 1523720 | tf_op jit(solution)/shard_map/ppermute | solution.py:659
  45.8 47.0 %collective-permute-start = (bf16[7936,128]{1,0:T(8,128)(2,1)S(1)}, bf16[7936,128]{1,0:T(8,128)(2,1)S(1)}, u32[]{:S(2)}, u32[]{:S(2)}) collective-permute-start(bf16[7936,128]{1,0:T(8,128)(2,1)S(1)} %get-tuple-element.36.refs_0_), channel_id=1, source_target_pairs={{0,1},{1,0},{2,3},{3,2},{4,5},{5,4},{6,7},{7,6},{8,9},{9,8},{10,11... | collective-permute-start | bytes 6094856 | tf_op jit(solution)/shard_map/ppermute | solution.py:662
  45.9 13.6 %collective-permute-start.10 = (bf16[1984,128]{1,0:T(8,128)(2,1)S(1)}, bf16[1984,128]{1,0:T(8,128)(2,1)S(1)}, u32[]{:S(2)}, u32[]{:S(2)}) collective-permute-start(bf16[1984,128]{1,0:T(8,128)(2,1)S(1)} %collective-permute-done.9.refs_10_), channel_id=1, source_target_pairs={{0,8},{1,17},{2,10},{3,19},{4,12},{5,21},{6,14},{7,23},{8,0},{9,25... | collective-permute-start | bytes 1523720 | tf_op jit(solution)/shard_map/ppermute | solution.py:659
  56.5 2.9 %collective-permute-start.7 = (bf16[1984,128]{1,0:T(8,128)(2,1)S(1)}, bf16[1984,128]{1,0:T(8,128)(2,1)S(1)}, u32[]{:S(2)}, u32[]{:S(2)}) collective-permute-start(bf16[1984,128]{1,0:T(8,128)(2,1)S(1)} %collective-permute-done.3.refs_4_), channel_id=1, source_target_pairs={{0,1},{1,0},{2,3},{3,2},{4,5},{5,4},{6,7},{7,6},{8,9},{9,8},{10,11... | collective-permute-start | bytes 1523720 | tf_op jit(solution)/shard_map/ppermute | solution.py:662
  56.6 3.5 %collective-permute-start.6 = (bf16[1984,128]{1,0:T(8,128)(2,1)S(1)}, bf16[1984,128]{1,0:T(8,128)(2,1)S(1)}, u32[]{:S(2)}, u32[]{:S(2)}) collective-permute-start(bf16[1984,128]{1,0:T(8,128)(2,1)S(1)} %collective-permute-done.2.refs_3_), channel_id=1, source_target_pairs={{0,1},{1,0},{2,3},{3,2},{4,5},{5,4},{6,7},{7,6},{8,9},{9,8},{10,11... | collective-permute-start | bytes 1523720 | tf_op jit(solution)/shard_map/ppermute | solution.py:662
  57.6 12.2 %collective-permute-start.4 = (bf16[1984,128]{1,0:T(8,128)(2,1)S(1)}, bf16[1984,128]{1,0:T(8,128)(2,1)S(1)}, u32[]{:S(2)}, u32[]{:S(2)}) collective-permute-start(bf16[1984,128]{1,0:T(8,128)(2,1)S(1)} %collective-permute-done.2.refs_3_), channel_id=1, source_target_pairs={{0,16},{1,9},{2,18},{3,11},{4,20},{5,13},{6,22},{7,15},{8,24},{9,1... | collective-permute-start | bytes 1523720 | tf_op jit(solution)/shard_map/ppermute | solution.py:659
  59.5 10.4 %collective-permute-start.21 = (bf16[1984,128]{1,0:T(8,128)(2,1)S(1)}, bf16[1984,128]{1,0:T(8,128)(2,1)S(1)}, u32[]{:S(2)}, u32[]{:S(2)}) collective-permute-start(bf16[1984,128]{1,0:T(8,128)(2,1)S(1)} %collective-permute-done.17.refs_18_), channel_id=1, source_target_pairs={{0,1},{1,0},{2,3},{3,2},{4,5},{5,4},{6,7},{7,6},{8,9},{9,8},{10,11... | collective-permute-start | bytes 1523720 | tf_op jit(solution)/shard_map/ppermute | solution.py:662
  59.5 18.0 %collective-permute-start.19 = (bf16[1984,128]{1,0:T(8,128)(2,1)S(1)}, bf16[1984,128]{1,0:T(8,128)(2,1)S(1)}, u32[]{:S(2)}, u32[]{:S(2)}) collective-permute-start(bf16[1984,128]{1,0:T(8,128)(2,1)S(1)} %collective-permute-done.17.refs_18_), channel_id=1, source_target_pairs={{0,16},{1,9},{2,18},{3,11},{4,20},{5,13},{6,22},{7,15},{8,24},{9,1... | collective-permute-start | bytes 1523720 | tf_op jit(solution)/shard_map/ppermute | solution.py:659
  60.0 19.3 %collective-permute-start.18 = (bf16[1984,128]{1,0:T(8,128)(2,1)S(1)}, bf16[1984,128]{1,0:T(8,128)(2,1)S(1)}, u32[]{:S(2)}, u32[]{:S(2)}) collective-permute-start(bf16[1984,128]{1,0:T(8,128)(2,1)S(1)} %collective-permute-done.17.refs_18_), channel_id=1, source_target_pairs={{0,8},{1,17},{2,10},{3,19},{4,12},{5,21},{6,14},{7,23},{8,0},{9,25... | collective-permute-start | bytes 1523720 | tf_op jit(solution)/shard_map/ppermute | solution.py:659
  69.8 9.5 %collective-permute-start.15 = (bf16[1984,128]{1,0:T(8,128)(2,1)S(1)}, bf16[1984,128]{1,0:T(8,128)(2,1)S(1)}, u32[]{:S(2)}, u32[]{:S(2)}) collective-permute-start(bf16[1984,128]{1,0:T(8,128)(2,1)S(1)} %collective-permute-done.11.refs_12_), channel_id=1, source_target_pairs={{0,1},{1,0},{2,3},{3,2},{4,5},{5,4},{6,7},{7,6},{8,9},{9,8},{10,11... | collective-permute-start | bytes 1523720 | tf_op jit(solution)/shard_map/ppermute | solution.py:662
  69.9 9.8 %collective-permute-start.14 = (bf16[1984,128]{1,0:T(8,128)(2,1)S(1)}, bf16[1984,128]{1,0:T(8,128)(2,1)S(1)}, u32[]{:S(2)}, u32[]{:S(2)}) collective-permute-start(bf16[1984,128]{1,0:T(8,128)(2,1)S(1)} %collective-permute-done.10.refs_11_), channel_id=1, source_target_pairs={{0,1},{1,0},{2,3},{3,2},{4,5},{5,4},{6,7},{7,6},{8,9},{9,8},{10,11... | collective-permute-start | bytes 1523720 | tf_op jit(solution)/shard_map/ppermute | solution.py:662
  77.5 9.0 %collective-permute-start.12 = (bf16[1984,128]{1,0:T(8,128)(2,1)S(1)}, bf16[1984,128]{1,0:T(8,128)(2,1)S(1)}, u32[]{:S(2)}, u32[]{:S(2)}) collective-permute-start(bf16[1984,128]{1,0:T(8,128)(2,1)S(1)} %collective-permute-done.10.refs_11_), channel_id=1, source_target_pairs={{0,16},{1,9},{2,18},{3,11},{4,20},{5,13},{6,22},{7,15},{8,24},{9,1... | collective-permute-start | bytes 1523720 | tf_op jit(solution)/shard_map/ppermute | solution.py:659
  79.4 7.2 %collective-permute-start.8 = (bf16[1984,128]{1,0:T(8,128)(2,1)S(1)}, bf16[1984,128]{1,0:T(8,128)(2,1)S(1)}, u32[]{:S(2)}, u32[]{:S(2)}) collective-permute-start(bf16[1984,128]{1,0:T(8,128)(2,1)S(1)} %collective-permute-done.4.refs_5_), channel_id=1, source_target_pairs={{0,1},{1,0},{2,3},{3,2},{4,5},{5,4},{6,7},{7,6},{8,9},{9,8},{10,11... | collective-permute-start | bytes 1523720 | tf_op jit(solution)/shard_map/ppermute | solution.py:662
  79.4 12.6 %collective-permute-start.20 = (bf16[1984,128]{1,0:T(8,128)(2,1)S(1)}, bf16[1984,128]{1,0:T(8,128)(2,1)S(1)}, u32[]{:S(2)}, u32[]{:S(2)}) collective-permute-start(bf16[1984,128]{1,0:T(8,128)(2,1)S(1)} %collective-permute-done.18.refs_19_), channel_id=1, source_target_pairs={{0,16},{1,9},{2,18},{3,11},{4,20},{5,13},{6,22},{7,15},{8,24},{9,1... | collective-permute-start | bytes 1523720 | tf_op jit(solution)/shard_map/ppermute | solution.py:659
  79.6 13.2 %collective-permute-start.22 = (bf16[1984,128]{1,0:T(8,128)(2,1)S(1)}, bf16[1984,128]{1,0:T(8,128)(2,1)S(1)}, u32[]{:S(2)}, u32[]{:S(2)}) collective-permute-start(bf16[1984,128]{1,0:T(8,128)(2,1)S(1)} %collective-permute-done.18.refs_19_), channel_id=1, source_target_pairs={{0,1},{1,0},{2,3},{3,2},{4,5},{5,4},{6,7},{7,6},{8,9},{9,8},{10,11... | collective-permute-start | bytes 1523720 | tf_op jit(solution)/shard_map/ppermute | solution.py:662
  86.5 6.3 %collective-permute-start.23 = (bf16[1984,128]{1,0:T(8,128)(2,1)S(1)}, bf16[1984,128]{1,0:T(8,128)(2,1)S(1)}, u32[]{:S(2)}, u32[]{:S(2)}) collective-permute-start(bf16[1984,128]{1,0:T(8,128)(2,1)S(1)} %collective-permute-done.19.refs_20_), channel_id=1, source_target_pairs={{0,1},{1,0},{2,3},{3,2},{4,5},{5,4},{6,7},{7,6},{8,9},{9,8},{10,11... | collective-permute-start | bytes 1523720 | tf_op jit(solution)/shard_map/ppermute | solution.py:662
  86.5 6.3 %collective-permute-start.16 = (bf16[1984,128]{1,0:T(8,128)(2,1)S(1)}, bf16[1984,128]{1,0:T(8,128)(2,1)S(1)}, u32[]{:S(2)}, u32[]{:S(2)}) collective-permute-start(bf16[1984,128]{1,0:T(8,128)(2,1)S(1)} %collective-permute-done.12.refs_13_), channel_id=1, source_target_pairs={{0,1},{1,0},{2,3},{3,2},{4,5},{5,4},{6,7},{7,6},{8,9},{9,8},{10,11... | collective-permute-start | bytes 1523720 | tf_op jit(solution)/shard_map/ppermute | solution.py:662
  91.9 1.9 collective-permute-start.24
  131.7 4.5 %collective-permute-start.34 = (bf16[7936,128]{1,0:T(8,128)(2,1)}, bf16[7936,128]{1,0:T(8,128)(2,1)S(1)}, u32[]{:S(2)}, u32[]{:S(2)}) collective-permute-start(bf16[7936,128]{1,0:T(8,128)(2,1)} %get-tuple-element.59), channel_id=1, source_target_pairs={{0,1},{1,0},{2,3},{3,2},{4,5},{5,4},{6,7},{7,6},{8,9},{9,8},{10,11... | collective-permute-start | bytes 6094856 | tf_op jit(solution)/shard_map/ppermute | solution.py:662
  132.3 9.0 %collective-permute-start.31 = (bf16[7936,128]{1,0:T(8,128)(2,1)}, bf16[7936,128]{1,0:T(8,128)(2,1)S(1)}, u32[]{:S(2)}, u32[]{:S(2)}) collective-permute-start(bf16[7936,128]{1,0:T(8,128)(2,1)} %get-tuple-element.53), channel_id=1, source_target_pairs={{0,1},{1,0},{2,3},{3,2},{4,5},{5,4},{6,7},{7,6},{8,9},{9,8},{10,11... | collective-permute-start | bytes 6094856 | tf_op jit(solution)/shard_map/ppermute | solution.py:662
  132.4 10.5 %collective-permute-start.28 = (bf16[7936,128]{1,0:T(8,128)(2,1)}, bf16[7936,128]{1,0:T(8,128)(2,1)S(1)}, u32[]{:S(2)}, u32[]{:S(2)}) collective-permute-start(bf16[7936,128]{1,0:T(8,128)(2,1)} %get-tuple-element.47), channel_id=1, source_target_pairs={{0,1},{1,0},{2,3},{3,2},{4,5},{5,4},{6,7},{7,6},{8,9},{9,8},{10,11... | collective-permute-start | bytes 6094856 | tf_op jit(solution)/shard_map/ppermute | solution.py:662
  132.8 23.2 %collective-permute-start.25 = (bf16[7936,128]{1,0:T(8,128)(2,1)}, bf16[7936,128]{1,0:T(8,128)(2,1)S(1)}, u32[]{:S(2)}, u32[]{:S(2)}) collective-permute-start(bf16[7936,128]{1,0:T(8,128)(2,1)} %get-tuple-element.41), channel_id=1, source_target_pairs={{0,1},{1,0},{2,3},{3,2},{4,5},{5,4},{6,7},{7,6},{8,9},{9,8},{10,11... | collective-permute-start | bytes 6094856 | tf_op jit(solution)/shard_map/ppermute | solution.py:662
  139.4 14.5 %collective-permute-start.35 = (bf16[2,1984,128]{2,1,0:T(8,128)(2,1)S(1)}, bf16[2,1984,128]{2,1,0:T(8,128)(2,1)S(1)}, u32[]{:S(2)}, u32[]{:S(2)}) collective-permute-start(bf16[2,1984,128]{2,1,0:T(8,128)(2,1)S(1)} %get-tuple-element.61), channel_id=1, source_target_pairs={{0,16},{1,9},{2,18},{3,11},{4,20},{5,13},{6,22},{7,15},{8,24},{9,1... | collective-permute-start | bytes 3047432 | tf_op jit(solution)/shard_map/ppermute | solution.py:659
  142.4 27.9 %collective-permute-start.32 = (bf16[2,1984,128]{2,1,0:T(8,128)(2,1)S(1)}, bf16[2,1984,128]{2,1,0:T(8,128)(2,1)S(1)}, u32[]{:S(2)}, u32[]{:S(2)}) collective-permute-start(bf16[2,1984,128]{2,1,0:T(8,128)(2,1)S(1)} %get-tuple-element.55), channel_id=1, source_target_pairs={{0,16},{1,9},{2,18},{3,11},{4,20},{5,13},{6,22},{7,15},{8,24},{9,1... | collective-permute-start | bytes 3047432 | tf_op jit(solution)/shard_map/ppermute | solution.py:659
  143.9 42.7 %collective-permute-start.29 = (bf16[2,1984,128]{2,1,0:T(8,128)(2,1)S(1)}, bf16[2,1984,128]{2,1,0:T(8,128)(2,1)S(1)}, u32[]{:S(2)}, u32[]{:S(2)}) collective-permute-start(bf16[2,1984,128]{2,1,0:T(8,128)(2,1)S(1)} %get-tuple-element.49), channel_id=1, source_target_pairs={{0,16},{1,9},{2,18},{3,11},{4,20},{5,13},{6,22},{7,15},{8,24},{9,1... | collective-permute-start | bytes 3047432 | tf_op jit(solution)/shard_map/ppermute | solution.py:659
  154.2 18.1 %collective-permute-start.36 = (bf16[1984,128]{1,0:T(8,128)(2,1)S(1)}, bf16[1984,128]{1,0:T(8,128)(2,1)S(1)}, u32[]{:S(2)}, u32[]{:S(2)}) collective-permute-start(bf16[1984,128]{1,0:T(8,128)(2,1)S(1)} %get-tuple-element.63), channel_id=1, source_target_pairs={{0,8},{1,17},{2,10},{3,19},{4,12},{5,21},{6,14},{7,23},{8,0},{9,25... | collective-permute-start | bytes 1523720 | tf_op jit(solution)/shard_map/ppermute | solution.py:659
  157.0 45.9 %collective-permute-start.26 = (bf16[2,1984,128]{2,1,0:T(8,128)(2,1)S(1)}, bf16[2,1984,128]{2,1,0:T(8,128)(2,1)S(1)}, u32[]{:S(2)}, u32[]{:S(2)}) collective-permute-start(bf16[2,1984,128]{2,1,0:T(8,128)(2,1)S(1)} %get-tuple-element.43), channel_id=1, source_target_pairs={{0,16},{1,9},{2,18},{3,11},{4,20},{5,13},{6,22},{7,15},{8,24},{9,1... | collective-permute-start | bytes 3047432 | tf_op jit(solution)/shard_map/ppermute | solution.py:659
  170.5 18.1 %collective-permute-start.33 = (bf16[1984,128]{1,0:T(8,128)(2,1)S(1)}, bf16[1984,128]{1,0:T(8,128)(2,1)S(1)}, u32[]{:S(2)}, u32[]{:S(2)}) collective-permute-start(bf16[1984,128]{1,0:T(8,128)(2,1)S(1)} %get-tuple-element.57), channel_id=1, source_target_pairs={{0,8},{1,17},{2,10},{3,19},{4,12},{5,21},{6,14},{7,23},{8,0},{9,25... | collective-permute-start | bytes 1523720 | tf_op jit(solution)/shard_map/ppermute | solution.py:659
  172.5 16.2 %collective-permute-start.37 = (bf16[1984,128]{1,0:T(8,128)(2,1)S(1)}, bf16[1984,128]{1,0:T(8,128)(2,1)S(1)}, u32[]{:S(2)}, u32[]{:S(2)}) collective-permute-start(bf16[1984,128]{1,0:T(8,128)(2,1)S(1)} %add_all.4), channel_id=1, source_target_pairs={{4,0},{5,1},{0,2},{1,3},{6,4},{7,5},{2,6},{3,7},{12,8},{13,9},{8,1... | collective-permute-start | bytes 1523720 | tf_op jit(solution)/shard_map/ppermute | solution.py:665
  186.8 18.1 %collective-permute-start.30 = (bf16[1984,128]{1,0:T(8,128)(2,1)S(1)}, bf16[1984,128]{1,0:T(8,128)(2,1)S(1)}, u32[]{:S(2)}, u32[]{:S(2)}) collective-permute-start(bf16[1984,128]{1,0:T(8,128)(2,1)S(1)} %get-tuple-element.51), channel_id=1, source_target_pairs={{0,8},{1,17},{2,10},{3,19},{4,12},{5,21},{6,14},{7,23},{8,0},{9,25... | collective-permute-start | bytes 1523720 | tf_op jit(solution)/shard_map/ppermute | solution.py:659
  188.8 16.1 %collective-permute-start.38 = (bf16[1984,128]{1,0:T(8,128)(2,1)S(1)}, bf16[1984,128]{1,0:T(8,128)(2,1)S(1)}, u32[]{:S(2)}, u32[]{:S(2)}) collective-permute-start(bf16[1984,128]{1,0:T(8,128)(2,1)S(1)} %add_all.5), channel_id=1, source_target_pairs={{4,0},{5,1},{0,2},{1,3},{6,4},{7,5},{2,6},{3,7},{12,8},{13,9},{8,1... | collective-permute-start | bytes 1523720 | tf_op jit(solution)/shard_map/ppermute | solution.py:665
  203.1 9.1 %collective-permute-start.27 = (bf16[1984,128]{1,0:T(8,128)(2,1)S(1)}, bf16[1984,128]{1,0:T(8,128)(2,1)S(1)}, u32[]{:S(2)}, u32[]{:S(2)}) collective-permute-start(bf16[1984,128]{1,0:T(8,128)(2,1)S(1)} %get-tuple-element.45), channel_id=1, source_target_pairs={{0,8},{1,17},{2,10},{3,19},{4,12},{5,21},{6,14},{7,23},{8,0},{9,25... | collective-permute-start | bytes 1523720 | tf_op jit(solution)/shard_map/ppermute | solution.py:659
  205.2 13.9 %collective-permute-start.39 = (bf16[1984,128]{1,0:T(8,128)(2,1)S(1)}, bf16[1984,128]{1,0:T(8,128)(2,1)S(1)}, u32[]{:S(2)}, u32[]{:S(2)}) collective-permute-start(bf16[1984,128]{1,0:T(8,128)(2,1)S(1)} %add_all.6), channel_id=1, source_target_pairs={{4,0},{5,1},{0,2},{1,3},{6,4},{7,5},{2,6},{3,7},{12,8},{13,9},{8,1... | collective-permute-start | bytes 1523720 | tf_op jit(solution)/shard_map/ppermute | solution.py:665
  219.3 13.7 %collective-permute-start.40 = (bf16[1984,128]{1,0:T(8,128)(2,1)S(1)}, bf16[1984,128]{1,0:T(8,128)(2,1)S(1)}, u32[]{:S(2)}, u32[]{:S(2)}) collective-permute-start(bf16[1984,128]{1,0:T(8,128)(2,1)S(1)} %add_all.7.refs_0_), channel_id=1, source_target_pairs={{0,8},{1,17},{2,10},{3,19},{4,12},{5,21},{6,14},{7,23},{8,0},{9,25... | collective-permute-start | bytes 1523720 | tf_op jit(solution)/shard_map/ppermute | solution.py:659
  221.1 12.8 %collective-permute-start.41 = (bf16[1984,128]{1,0:T(8,128)(2,1)S(1)}, bf16[1984,128]{1,0:T(8,128)(2,1)S(1)}, u32[]{:S(2)}, u32[]{:S(2)}) collective-permute-start(bf16[1984,128]{1,0:T(8,128)(2,1)S(1)} %add_all.7.refs_0_), channel_id=1, source_target_pairs={{0,16},{1,9},{2,18},{3,11},{4,20},{5,13},{6,22},{7,15},{8,24},{9,1... | collective-permute-start | bytes 1523720 | tf_op jit(solution)/shard_map/ppermute | solution.py:659
  233.0 9.0 %collective-permute-start.42 = (bf16[1984,128]{1,0:T(8,128)(2,1)S(1)}, bf16[1984,128]{1,0:T(8,128)(2,1)S(1)}, u32[]{:S(2)}, u32[]{:S(2)}) collective-permute-start(bf16[1984,128]{1,0:T(8,128)(2,1)S(1)} %collective-permute-done.40.refs_1_), channel_id=1, source_target_pairs={{0,16},{1,9},{2,18},{3,11},{4,20},{5,13},{6,22},{7,15},{8,24},{9,1... | collective-permute-start | bytes 1523720 | tf_op jit(solution)/shard_map/ppermute | solution.py:659
  (33 other events, 621.2 us)

commit v2 on v1

--- a/solution.py
+++ b/solution.py
@@ -91,6 +91,8 @@
                 else:
                     runs.append([row, row + ROUND, places])
             self.runs.append([tuple(run) for run in runs])
+        self.attention_blocks = max(i for i, found in enumerate(self.regions) if found[0][0] < UP)
+        self.vector_blocks = min(i for i, found in enumerate(self.regions) if found[-1][0] == VEC)
         self.margin = ROUND * (FF // LANES)
         self.flat_rows = up_to(up_to(self.length, LANES) // LANES + 1, 8)
         self.buffer_rows = self.margin + self.flat_rows + self.margin + 8
@@ -161,7 +163,7 @@
             buffer[pl.ds(at, 64), :] = pltpu.roll(value, shift, 1)
             return carry
 
-        lax.fori_loop(0, chunk // 8192, roll_in, 0)
+        lax.fori_loop(0, chunk // 8192, roll_in, 0, unroll=True)
 
         @pl.when(step == steps - 1)
         def _():
@@ -253,7 +255,7 @@
             new_two_ref[span] = new_two.reshape(8192)
             return carry
 
-        lax.fori_loop(0, chunk // 8192, update, 0)
+        lax.fori_loop(0, chunk // 8192, update, 0, unroll=True)
 
     buffer_rows = geo.margin + max(steps * rows, geo.flat_rows) + geo.margin + 8
     flat_spec = pl.BlockSpec((chunk,), lambda i: (i,))
@@ -317,14 +319,23 @@
         ) = refs[2 + len(grad_refs) :]
 
         index, replica = where_ref[0], where_ref[1]
-        copies = []
+        arrivals = []
         for i, (ref, (block, at)) in enumerate(zip(weight_refs, weight_places(index, replica))):
             target = store if block is None else store.at[block, pl.ds(aligned(at), ref.shape[0]), :]
-            copies.append(pltpu.make_async_copy(ref, target, in_sems.at[i]))
-        for copy in copies:
-            copy.start()
-        for copy in copies:
-            copy.wait()
+            arrivals.append((block, pltpu.make_async_copy(ref, target, in_sems.at[i])))
+
+        def each_arrival(early, act):
+            for block, copy in arrivals:
+                if block is None:
+                    if early:
+                        act(copy)
+                else:
+                    first = (block <= geo.attention_blocks) | (block >= geo.vector_blocks)
+                    pl.when(first if early else jnp.logical_not(first))(lambda copy=copy: act(copy))
+
+        each_arrival(True, lambda copy: copy.start())
+        each_arrival(False, lambda copy: copy.start())
+        each_arrival(True, lambda copy: copy.wait())
 
         def spans(matrix, low, high):
             for first, last, places in geo.runs[matrix]:
@@ -427,6 +438,8 @@
         hidden_low[...] = value.astype(BF16)
         hidden_t[...] = value.astype(BF16).T
 
+        each_arrival(False, lambda copy: copy.wait())
+
         def up_step(tile, carry):
             pre = nn(hidden_low[...], load_wide(UP, 2 * tile, 2)) + vec(V_UP + 2 * tile, 2)
             below = 0.5 * (1.0 + lax.erf(pre * (0.5**0.5)))
@@ -461,6 +474,25 @@
             vec_grad(V_UP + 2 * tile, d_up.astype(F32))
             d_hidden[...] += nt(d_up, load_wide(UP, 2 * tile, 2))
             save_wide(UP, 2 * tile, nn(hidden_t[...], d_up))
+
+        if outs_of:
+            departures = [
+                (block, pltpu.make_async_copy(store.at[block], ref, out_sems.at[i]))
+                for i, (ref, block) in enumerate(zip(grad_refs, outs_of(index)))
+            ]
+        else:
+            departures = [(None, pltpu.make_async_copy(store, grad_refs[0], out_sems.at[0]))]
+
+        def each_departure(early, act):
+            for block, copy in departures:
+                if block is None:
+                    if not early:
+                        act(copy)
+                else:
+                    first = (block > geo.attention_blocks) & (block < geo.vector_blocks)
+                    pl.when(first if early else jnp.logical_not(first))(lambda copy=copy: act(copy))
+
+        each_departure(True, lambda copy: copy.start())
 
         d_out = d_hidden[...]
         hat = hat_one[...]
@@ -516,17 +548,9 @@
         save_wide(TIME_IN, 0, nn(sines.T, d_time_pre))
         save(VEC, 0, vec_grads[...].astype(BF16))
 
-        if outs_of:
-            copies = [
-                pltpu.make_async_copy(store.at[block], ref, out_sems.at[i])
-                for i, (ref, block) in enumerate(zip(grad_refs, outs_of(index)))
-            ]
-        else:
-            copies = [pltpu.make_async_copy(store, grad_refs[0], out_sems.at[0])]
-        for copy in copies:
-            copy.start()
-        for copy in copies:
-            copy.wait()
+        each_departure(False, lambda copy: copy.start())
+        each_departure(True, lambda copy: copy.wait())
+        each_departure(False, lambda copy: copy.wait())
 
     if outs_of:
         grad_shapes = [jax.ShapeDtypeStruct((geo.rows, LANES), BF16)] * grads
@@ -687,10 +711,14 @@
 
         if direct:
             weights = [block, core_swap(block)]
+            one = None
             for _ in range(1, chips):
                 quarter = ring_hop(quarter)
-                one = first_way(quarter)
-                two = second_way(quarter)
+                ready = quarter
+                if one is not None:
+                    ready, one = lax.optimization_barrier((quarter, one))
+                one = first_way(ready)
+                two = second_way(ready)
                 three = second_way(one)
                 four = [quarter, one, two, three]
                 weights += four + [core_swap(item) for item in four]

time: 261 us -> 241 us (0.923)
  Pallas kernels: 71.6 us -> 52.8 us
    pallas_call x1, Pallas kernels: 10.8 us -> 3.14 us  [pack_block(): pl.pallas_call(kernel, grid=(steps,), in_specs=[pl.BlockSpec(memory_space...]
    pallas_call x1, Pallas kernels: 18.2 us -> 11.8 us  [optimizer_step(): pl.pallas_call(kernel, grid=(steps,), in_specs=[pl.BlockSpec(memory_space...]
    pallas_call x1, Pallas kernels: 37 us -> 32.2 us  [model_step(): pl.pallas_call(kernel, in_specs=[pl.BlockSpec(memory_space=pltpu.SMEM)] *...]
  transfers between devices with their start and end apart: 43 -> 43, of which waited for: 18 -> 20; matrix products, arithmetic and copies ran while one was open for 0% -> 0% of each run, Pallas kernels for 2% -> 2%
where the time goes in v2:
time: 241 us
  waiting for transfers between devices  133 us (55%)
  Pallas kernels  52.8 us (22%)
  starting transfers between devices  46.9 us (19%)
  local copies, waits for them, and re-layouts  6.29 us (3%)
    ppermute x20, waiting for transfers between devices, permute(): return lax.ppermute(value, axes, pairs)  92.4 us
    ppermute x6, waiting for transfers between devices, ring_hop(): lax.ppermute(value, 'fsdp', [(before[chip] * 2 + core, chip * 2 + core) f...  36.3 us
    pallas_call x1, Pallas kernels, model_step(): pl.pallas_call(kernel, in_specs=[pl.BlockSpec(memory_space=pltpu.SMEM)] *...  32.2 us
    ppermute x20, starting transfers between devices, permute(): return lax.ppermute(value, axes, pairs)  29.1 us
    ppermute x6, starting transfers between devices, ring_hop(): lax.ppermute(value, 'fsdp', [(before[chip] * 2 + core, chip * 2 + core) f...  15.1 us
    pallas_call x1, Pallas kernels, optimizer_step(): pl.pallas_call(kernel, grid=(steps,), in_specs=[pl.BlockSpec(memory_space...  11.8 us
    unnamed x76, local copies, waits for them, and re-layouts  6.29 us
  transfers between devices with their start and end apart: 43, of which 20 were waited for; matrix products, arithmetic and copies ran while one was open for 0% of the time, Pallas kernels for 2%

profile of v2, /device:TPU:0, one launch (start us, length us, event | category | flops | bytes accessed | tf_op | source)
XLA Modules:
  0.0 241.1 jit_solution(13399859494587802199)
XLA Ops:
  0.7 2.1 copy-done
  3.5 3.1 %pack_block.1 = (bf16[7936,128]{1,0:T(8,128)(2,1)S(1)}, bf16[1984,128]{1,0:T(8,128)(2,1)S(1)}) custom-call(s32[2]{0:T(128)S(1)} %pad_add_fusion.where_ref, s32[168]{0:T(256)S(1)} %copy-done.10, f32[943392]{0:T(1024)S(1)} %copy-done), custom_call_target="tpu_custom_call" | custom-call | tf_op jit(solution)/shard_map/pack_block/pallas_call | solution.py:182
  6.6 3.1 %collective-permute-start.1 = (bf16[1984,128]{1,0:T(8,128)(2,1)S(1)}, bf16[1984,128]{1,0:T(8,128)(2,1)S(1)}, u32[]{:S(2)}, u32[]{:S(2)}) collective-permute-start(bf16[1984,128]{1,0:T(8,128)(2,1)S(1)} %get-tuple-element.39), channel_id=1, source_target_pairs={{4,0},{5,1},{0,2},{1,3},{6,4},{7,5},{2,6},{3,7},{12,8},{13,9},{8,1... | collective-permute-start | bytes 1523720 | tf_op jit(solution)/shard_map/ppermute | solution.py:689
  9.8 12.5 %collective-permute-done.1.refs_2_ = bf16[1984,128]{1,0:T(8,128)(2,1)S(1)} collective-permute-done((bf16[1984,128]{1,0:T(8,128)(2,1)S(1)}, bf16[1984,128]{1,0:T(8,128)(2,1)S(1)}, u32[]{:S(2)}, u32[]{:S(2)}) %collective-permute-start.1) | collective-permute-done | bytes 507936 | tf_op jit(solution)/shard_map/ppermute | solution.py:689
  22.3 0.9 collective-permute-start.9
  23.2 1.5 collective-permute-start.2
  24.7 1.5 collective-permute-start.3
  26.2 9.8 %collective-permute-done.9.refs_10_ = bf16[1984,128]{1,0:T(8,128)(2,1)S(1)} collective-permute-done((bf16[1984,128]{1,0:T(8,128)(2,1)S(1)}, bf16[1984,128]{1,0:T(8,128)(2,1)S(1)}, u32[]{:S(2)}, u32[]{:S(2)}) %collective-permute-start.9) | collective-permute-done | bytes 507936 | tf_op jit(solution)/shard_map/ppermute | solution.py:689
  36.6 2.5 %collective-permute-start.10 = (bf16[1984,128]{1,0:T(8,128)(2,1)S(1)}, bf16[1984,128]{1,0:T(8,128)(2,1)S(1)}, u32[]{:S(2)}, u32[]{:S(2)}) collective-permute-start(bf16[1984,128]{1,0:T(8,128)(2,1)S(1)} %collective-permute-done.9.refs_10_), channel_id=1, source_target_pairs={{0,8},{1,17},{2,10},{3,19},{4,12},{5,21},{6,14},{7,23},{8,0},{9,25... | collective-permute-start | bytes 1523720 | tf_op jit(solution)/shard_map/ppermute | solution.py:683
  39.1 1.5 collective-permute-start.11
  40.6 8.3 %collective-permute-done.17.refs_18_ = bf16[1984,128]{1,0:T(8,128)(2,1)S(1)} collective-permute-done((bf16[1984,128]{1,0:T(8,128)(2,1)S(1)}, bf16[1984,128]{1,0:T(8,128)(2,1)S(1)}, u32[]{:S(2)}, u32[]{:S(2)}) %collective-permute-start.17) | collective-permute-done | bytes 507936 | tf_op jit(solution)/shard_map/ppermute | solution.py:689
  49.4 1.8 collective-permute-done.10.refs_11_
  51.2 1.1 collective-permute-start.4
  52.8 0.9 collective-permute-start.19
  53.8 6.5 %collective-permute-done.4.refs_5_ = bf16[1984,128]{1,0:T(8,128)(2,1)S(1)} collective-permute-done((bf16[1984,128]{1,0:T(8,128)(2,1)S(1)}, bf16[1984,128]{1,0:T(8,128)(2,1)S(1)}, u32[]{:S(2)}, u32[]{:S(2)}) %collective-permute-start.4) | collective-permute-done | bytes 507936 | tf_op jit(solution)/shard_map/ppermute | solution.py:683
  60.2 3.1 %collective-permute-start.18 = (bf16[1984,128]{1,0:T(8,128)(2,1)S(1)}, bf16[1984,128]{1,0:T(8,128)(2,1)S(1)}, u32[]{:S(2)}, u32[]{:S(2)}) collective-permute-start(bf16[1984,128]{1,0:T(8,128)(2,1)S(1)} %collective-permute-done.17.refs_18_), channel_id=1, source_target_pairs={{0,8},{1,17},{2,10},{3,19},{4,12},{5,21},{6,14},{7,23},{8,0},{9,25... | collective-permute-start | bytes 1523720 | tf_op jit(solution)/shard_map/ppermute | solution.py:683
  63.4 7.6 %collective-permute-done.19.refs_20_ = bf16[1984,128]{1,0:T(8,128)(2,1)S(1)} collective-permute-done((bf16[1984,128]{1,0:T(8,128)(2,1)S(1)}, bf16[1984,128]{1,0:T(8,128)(2,1)S(1)}, u32[]{:S(2)}, u32[]{:S(2)}) %collective-permute-start.19) | collective-permute-done | bytes 507936 | tf_op jit(solution)/shard_map/ppermute | solution.py:683
  71.0 4.3 %collective-permute-done.18.refs_19_ = bf16[1984,128]{1,0:T(8,128)(2,1)S(1)} collective-permute-done((bf16[1984,128]{1,0:T(8,128)(2,1)S(1)}, bf16[1984,128]{1,0:T(8,128)(2,1)S(1)}, u32[]{:S(2)}, u32[]{:S(2)}) %collective-permute-start.18) | collective-permute-done | bytes 507936 | tf_op jit(solution)/shard_map/ppermute | solution.py:683
  75.3 1.2 collective-permute-done.12.refs_13_
  77.1 7.2 %collective-permute-done.20.refs_21_ = bf16[1984,128]{1,0:T(8,128)(2,1)S(1)} collective-permute-done((bf16[1984,128]{1,0:T(8,128)(2,1)S(1)}, bf16[1984,128]{1,0:T(8,128)(2,1)S(1)}, u32[]{:S(2)}, u32[]{:S(2)}) %collective-permute-start.20) | collective-permute-done | bytes 507936 | tf_op jit(solution)/shard_map/ppermute | solution.py:683
  85.2 1.0 collective-permute-done.24.refs_25_
  87.1 32.2 %model_step.1 = (bf16[256,768]{1,0:T(8,128)(2,1)}, f32[256,768]{1,0:T(8,128)}, bf16[7936,128]{1,0:T(8,128)(2,1)}, bf16[7936,128]{1,0:T(8,128)(2,1)}, bf16[7936,1...) custom-call(s32[2]{0:T(128)} %copy-done.7, ...), custom_call_target="tpu_custom_call" | custom-call | tf_op jit(solution)/shard_map/model_step/pallas_call | solution.py:560
  120.4 3.3 %collective-permute-done.34.got_ref = bf16[7936,128]{1,0:T(8,128)(2,1)S(1)} collective-permute-done((bf16[7936,128]{1,0:T(8,128)(2,1)}, bf16[7936,128]{1,0:T(8,128)(2,1)S(1)}, u32[]{:S(2)}, u32[]{:S(2)}) %collective-permute-start.34) | collective-permute-done | bytes 2031648 | tf_op jit(solution)/shard_map/ppermute | solution.py:686
  123.7 1.6 copy-done.6
  125.9 1.0 add_cores.7
  127.5 1.0 add_cores.6
  128.5 1.6 collective-permute-start.32
  130.1 1.0 add_cores.5
  131.7 9.8 %collective-permute-done.35.got_ref = bf16[2,1984,128]{2,1,0:T(8,128)(2,1)S(1)} collective-permute-done((bf16[2,1984,128]{2,1,0:T(8,128)(2,1)S(1)}, bf16[2,1984,128]{2,1,0:T(8,128)(2,1)S(1)}, u32[]{:S(2)}, u32[]{:S(2)}) %collective-permute-start.35) | collective-permute-done | bytes 1015840 | tf_op jit(solution)/shard_map/ppermute | solution.py:683
  141.7 2.5 %collective-permute-start.36 = (bf16[1984,128]{1,0:T(8,128)(2,1)S(1)}, bf16[1984,128]{1,0:T(8,128)(2,1)S(1)}, u32[]{:S(2)}, u32[]{:S(2)}) collective-permute-start(bf16[1984,128]{1,0:T(8,128)(2,1)S(1)} %get-tuple-element.67), channel_id=1, source_target_pairs={{0,8},{1,17},{2,10},{3,19},{4,12},{5,21},{6,14},{7,23},{8,0},{9,25... | collective-permute-start | bytes 1523720 | tf_op jit(solution)/shard_map/ppermute | solution.py:683
  144.3 1.0 add_cores.4
  145.4 12.4 %collective-permute-done.32.got_ref = bf16[2,1984,128]{2,1,0:T(8,128)(2,1)S(1)} collective-permute-done((bf16[2,1984,128]{2,1,0:T(8,128)(2,1)S(1)}, bf16[2,1984,128]{2,1,0:T(8,128)(2,1)S(1)}, u32[]{:S(2)}, u32[]{:S(2)}) %collective-permute-start.32) | collective-permute-done | bytes 1015840 | tf_op jit(solution)/shard_map/ppermute | solution.py:683
  158.1 2.5 %collective-permute-start.33 = (bf16[1984,128]{1,0:T(8,128)(2,1)S(1)}, bf16[1984,128]{1,0:T(8,128)(2,1)S(1)}, u32[]{:S(2)}, u32[]{:S(2)}) collective-permute-start(bf16[1984,128]{1,0:T(8,128)(2,1)S(1)} %get-tuple-element.61), channel_id=1, source_target_pairs={{0,8},{1,17},{2,10},{3,19},{4,12},{5,21},{6,14},{7,23},{8,0},{9,25... | collective-permute-start | bytes 1523720 | tf_op jit(solution)/shard_map/ppermute | solution.py:683
  160.7 3.5 %collective-permute-start.37 = (bf16[1984,128]{1,0:T(8,128)(2,1)S(1)}, bf16[1984,128]{1,0:T(8,128)(2,1)S(1)}, u32[]{:S(2)}, u32[]{:S(2)}) collective-permute-start(bf16[1984,128]{1,0:T(8,128)(2,1)S(1)} %add_all.4), channel_id=1, source_target_pairs={{4,0},{5,1},{0,2},{1,3},{6,4},{7,5},{2,6},{3,7},{12,8},{13,9},{8,1... | collective-permute-start | bytes 1523720 | tf_op jit(solution)/shard_map/ppermute | solution.py:689
  164.2 9.9 %collective-permute-done.29.got_ref = bf16[2,1984,128]{2,1,0:T(8,128)(2,1)S(1)} collective-permute-done((bf16[2,1984,128]{2,1,0:T(8,128)(2,1)S(1)}, bf16[2,1984,128]{2,1,0:T(8,128)(2,1)S(1)}, u32[]{:S(2)}, u32[]{:S(2)}) %collective-permute-start.29) | collective-permute-done | bytes 1015840 | tf_op jit(solution)/shard_map/ppermute | solution.py:683
  174.4 2.5 %collective-permute-start.30 = (bf16[1984,128]{1,0:T(8,128)(2,1)S(1)}, bf16[1984,128]{1,0:T(8,128)(2,1)S(1)}, u32[]{:S(2)}, u32[]{:S(2)}) collective-permute-start(bf16[1984,128]{1,0:T(8,128)(2,1)S(1)} %get-tuple-element.55), channel_id=1, source_target_pairs={{0,8},{1,17},{2,10},{3,19},{4,12},{5,21},{6,14},{7,23},{8,0},{9,25... | collective-permute-start | bytes 1523720 | tf_op jit(solution)/shard_map/ppermute | solution.py:683
  177.1 3.5 %collective-permute-start.38 = (bf16[1984,128]{1,0:T(8,128)(2,1)S(1)}, bf16[1984,128]{1,0:T(8,128)(2,1)S(1)}, u32[]{:S(2)}, u32[]{:S(2)}) collective-permute-start(bf16[1984,128]{1,0:T(8,128)(2,1)S(1)} %add_all.5), channel_id=1, source_target_pairs={{4,0},{5,1},{0,2},{1,3},{6,4},{7,5},{2,6},{3,7},{12,8},{13,9},{8,1... | collective-permute-start | bytes 1523720 | tf_op jit(solution)/shard_map/ppermute | solution.py:689
  180.6 9.8 %collective-permute-done.26.got_ref = bf16[2,1984,128]{2,1,0:T(8,128)(2,1)S(1)} collective-permute-done((bf16[2,1984,128]{2,1,0:T(8,128)(2,1)S(1)}, bf16[2,1984,128]{2,1,0:T(8,128)(2,1)S(1)}, u32[]{:S(2)}, u32[]{:S(2)}) %collective-permute-start.26) | collective-permute-done | bytes 1015840 | tf_op jit(solution)/shard_map/ppermute | solution.py:683
  190.7 2.5 %collective-permute-start.27 = (bf16[1984,128]{1,0:T(8,128)(2,1)S(1)}, bf16[1984,128]{1,0:T(8,128)(2,1)S(1)}, u32[]{:S(2)}, u32[]{:S(2)}) collective-permute-start(bf16[1984,128]{1,0:T(8,128)(2,1)S(1)} %get-tuple-element.49), channel_id=1, source_target_pairs={{0,8},{1,17},{2,10},{3,19},{4,12},{5,21},{6,14},{7,23},{8,0},{9,25... | collective-permute-start | bytes 1523720 | tf_op jit(solution)/shard_map/ppermute | solution.py:683
  193.4 3.5 %collective-permute-start.39 = (bf16[1984,128]{1,0:T(8,128)(2,1)S(1)}, bf16[1984,128]{1,0:T(8,128)(2,1)S(1)}, u32[]{:S(2)}, u32[]{:S(2)}) collective-permute-start(bf16[1984,128]{1,0:T(8,128)(2,1)S(1)} %add_all.6), channel_id=1, source_target_pairs={{4,0},{5,1},{0,2},{1,3},{6,4},{7,5},{2,6},{3,7},{12,8},{13,9},{8,1... | collective-permute-start | bytes 1523720 | tf_op jit(solution)/shard_map/ppermute | solution.py:689
  197.0 3.2 %collective-permute-done.27.refs_1_ = bf16[1984,128]{1,0:T(8,128)(2,1)S(1)} collective-permute-done((bf16[1984,128]{1,0:T(8,128)(2,1)S(1)}, bf16[1984,128]{1,0:T(8,128)(2,1)S(1)}, u32[]{:S(2)}, u32[]{:S(2)}) %collective-permute-start.27) | collective-permute-done | bytes 507936 | tf_op jit(solution)/shard_map/ppermute | solution.py:683
  200.2 5.6 %collective-permute-done.39.refs_2_ = bf16[1984,128]{1,0:T(8,128)(2,1)S(1)} collective-permute-done((bf16[1984,128]{1,0:T(8,128)(2,1)S(1)}, bf16[1984,128]{1,0:T(8,128)(2,1)S(1)}, u32[]{:S(2)}, u32[]{:S(2)}) %collective-permute-start.39) | collective-permute-done | bytes 507936 | tf_op jit(solution)/shard_map/ppermute | solution.py:689
  205.9 1.8 collective-permute-start.40
  207.8 1.6 collective-permute-start.41
  209.4 10.7 %collective-permute-done.40.refs_1_ = bf16[1984,128]{1,0:T(8,128)(2,1)S(1)} collective-permute-done((bf16[1984,128]{1,0:T(8,128)(2,1)S(1)}, bf16[1984,128]{1,0:T(8,128)(2,1)S(1)}, u32[]{:S(2)}, u32[]{:S(2)}) %collective-permute-start.40) | collective-permute-done | bytes 507936 | tf_op jit(solution)/shard_map/ppermute | solution.py:683
  220.1 1.1 collective-permute-start.42
  221.2 7.9 %collective-permute-done.42.refs_3_ = bf16[1984,128]{1,0:T(8,128)(2,1)S(1)} collective-permute-done((bf16[1984,128]{1,0:T(8,128)(2,1)S(1)}, bf16[1984,128]{1,0:T(8,128)(2,1)S(1)}, u32[]{:S(2)}, u32[]{:S(2)}) %collective-permute-start.42) | collective-permute-done | bytes 507936 | tf_op jit(solution)/shard_map/ppermute | solution.py:683
  229.2 11.8 %optimizer_step.1 = (f32[943392]{0:T(1024)}, f32[943392]{0:T(1024)}, f32[943392]{0:T(1024)}) custom-call(s32[2]{0:T(128)S(1)} %copy-done.9, s32[168]{0:T(256)S(1)} %copy-done.11, bf16[1984,128]{1,0:T(8,128)(2,1)S(1)} %add_all.7.refs_0_, bf16[1984,128]{1,0:T(8,128)(2,1)S(1)} %collective-permute-done.40.refs_1_, ...), custom_call_target="tpu_custom_call" | custom-call | tf_op jit(solution)/shard_map/optimizer_step/pallas_call | solution.py:263
  (134 shorter events, 9.3 us)
Async XLA Ops:
  0.6 83.6 %copy-start.37 = (s32[2]{0:T(128)S(1)}, s32[2]{0:T(128)}, u32[]{:S(2)}) copy-start(s32[2]{0:T(128)} %param.11) | copy-start | bytes 28
  3.5 83.6 %copy-start.7 = (s32[2]{0:T(128)}, s32[2]{0:T(128)S(1)}, u32[]{:S(2)}) copy-start(s32[2]{0:T(128)S(1)} %pad_add_fusion.where_ref) | copy-start | bytes 28
  6.6 80.5 %copy-start.2 = (bf16[7936,128]{1,0:T(8,128)(2,1)}, bf16[7936,128]{1,0:T(8,128)(2,1)S(1)}, u32[]{:S(2)}) copy-start(bf16[7936,128]{1,0:T(8,128)(2,1)S(1)} %get-tuple-element.38.refs_0_) | copy-start | bytes 6094852
  6.6 15.7 %collective-permute-start.1 = (bf16[1984,128]{1,0:T(8,128)(2,1)S(1)}, bf16[1984,128]{1,0:T(8,128)(2,1)S(1)}, u32[]{:S(2)}, u32[]{:S(2)}) collective-permute-start(bf16[1984,128]{1,0:T(8,128)(2,1)S(1)} %get-tuple-element.39), channel_id=1, source_target_pairs={{4,0},{5,1},{0,2},{1,3},{6,4},{7,5},{2,6},{3,7},{12,8},{13,9},{8,1... | collective-permute-start | bytes 1523720 | tf_op jit(solution)/shard_map/ppermute | solution.py:689
  22.3 62.8 %copy-start.13 = (bf16[1984,128]{1,0:T(8,128)(2,1)}, bf16[1984,128]{1,0:T(8,128)(2,1)S(1)}, u32[]{:S(2)}) copy-start(bf16[1984,128]{1,0:T(8,128)(2,1)S(1)} %collective-permute-done.1.refs_2_) | copy-start | bytes 1523716
  22.3 13.8 %collective-permute-start.9 = (bf16[1984,128]{1,0:T(8,128)(2,1)S(1)}, bf16[1984,128]{1,0:T(8,128)(2,1)S(1)}, u32[]{:S(2)}, u32[]{:S(2)}) collective-permute-start(bf16[1984,128]{1,0:T(8,128)(2,1)S(1)} %collective-permute-done.1.refs_2_), channel_id=1, source_target_pairs={{4,0},{5,1},{0,2},{1,3},{6,4},{7,5},{2,6},{3,7},{12,8},{13,9},{8,1... | collective-permute-start | bytes 1523720 | tf_op jit(solution)/shard_map/ppermute | solution.py:689
  23.2 13.4 %collective-permute-start.2 = (bf16[1984,128]{1,0:T(8,128)(2,1)S(1)}, bf16[1984,128]{1,0:T(8,128)(2,1)S(1)}, u32[]{:S(2)}, u32[]{:S(2)}) collective-permute-start(bf16[1984,128]{1,0:T(8,128)(2,1)S(1)} %collective-permute-done.1.refs_2_), channel_id=1, source_target_pairs={{0,8},{1,17},{2,10},{3,19},{4,12},{5,21},{6,14},{7,23},{8,0},{9,25... | collective-permute-start | bytes 1523720 | tf_op jit(solution)/shard_map/ppermute | solution.py:683
  24.7 14.4 %collective-permute-start.5 = (bf16[1984,128]{1,0:T(8,128)(2,1)S(1)}, bf16[1984,128]{1,0:T(8,128)(2,1)S(1)}, u32[]{:S(2)}, u32[]{:S(2)}) collective-permute-start(bf16[1984,128]{1,0:T(8,128)(2,1)S(1)} %collective-permute-done.1.refs_2_), channel_id=1, source_target_pairs={{0,1},{1,0},{2,3},{3,2},{4,5},{5,4},{6,7},{7,6},{8,9},{9,8},{10,11... | collective-permute-start | bytes 1523720 | tf_op jit(solution)/shard_map/ppermute | solution.py:686
  24.7 15.9 %collective-permute-start.3 = (bf16[1984,128]{1,0:T(8,128)(2,1)S(1)}, bf16[1984,128]{1,0:T(8,128)(2,1)S(1)}, u32[]{:S(2)}, u32[]{:S(2)}) collective-permute-start(bf16[1984,128]{1,0:T(8,128)(2,1)S(1)} %collective-permute-done.1.refs_2_), channel_id=1, source_target_pairs={{0,16},{1,9},{2,18},{3,11},{4,20},{5,13},{6,22},{7,15},{8,24},{9,1... | collective-permute-start | bytes 1523720 | tf_op jit(solution)/shard_map/ppermute | solution.py:683
  36.1 49.0 %copy-start.14 = (bf16[1984,128]{1,0:T(8,128)(2,1)}, bf16[1984,128]{1,0:T(8,128)(2,1)S(1)}, u32[]{:S(2)}) copy-start(bf16[1984,128]{1,0:T(8,128)(2,1)S(1)} %collective-permute-done.9.refs_10_) | copy-start | bytes 1523716
  36.1 12.8 %collective-permute-start.17 = (bf16[1984,128]{1,0:T(8,128)(2,1)S(1)}, bf16[1984,128]{1,0:T(8,128)(2,1)S(1)}, u32[]{:S(2)}, u32[]{:S(2)}) collective-permute-start(bf16[1984,128]{1,0:T(8,128)(2,1)S(1)} %collective-permute-done.9.refs_10_), channel_id=1, source_target_pairs={{4,0},{5,1},{0,2},{1,3},{6,4},{7,5},{2,6},{3,7},{12,8},{13,9},{8,1... | collective-permute-start | bytes 1523720 | tf_op jit(solution)/shard_map/ppermute | solution.py:689
  36.6 12.4 %collective-permute-start.13 = (bf16[1984,128]{1,0:T(8,128)(2,1)S(1)}, bf16[1984,128]{1,0:T(8,128)(2,1)S(1)}, u32[]{:S(2)}, u32[]{:S(2)}) collective-permute-start(bf16[1984,128]{1,0:T(8,128)(2,1)S(1)} %collective-permute-done.9.refs_10_), channel_id=1, source_target_pairs={{0,1},{1,0},{2,3},{3,2},{4,5},{5,4},{6,7},{7,6},{8,9},{9,8},{10,11... | collective-permute-start | bytes 1523720 | tf_op jit(solution)/shard_map/ppermute | solution.py:686
  36.6 14.6 %collective-permute-start.10 = (bf16[1984,128]{1,0:T(8,128)(2,1)S(1)}, bf16[1984,128]{1,0:T(8,128)(2,1)S(1)}, u32[]{:S(2)}, u32[]{:S(2)}) collective-permute-start(bf16[1984,128]{1,0:T(8,128)(2,1)S(1)} %collective-permute-done.9.refs_10_), channel_id=1, source_target_pairs={{0,8},{1,17},{2,10},{3,19},{4,12},{5,21},{6,14},{7,23},{8,0},{9,25... | collective-permute-start | bytes 1523720 | tf_op jit(solution)/shard_map/ppermute | solution.py:683
  39.1 13.2 %collective-permute-start.11 = (bf16[1984,128]{1,0:T(8,128)(2,1)S(1)}, bf16[1984,128]{1,0:T(8,128)(2,1)S(1)}, u32[]{:S(2)}, u32[]{:S(2)}) collective-permute-start(bf16[1984,128]{1,0:T(8,128)(2,1)S(1)} %collective-permute-done.9.refs_10_), channel_id=1, source_target_pairs={{0,16},{1,9},{2,18},{3,11},{4,20},{5,13},{6,22},{7,15},{8,24},{9,1... | collective-permute-start | bytes 1523720 | tf_op jit(solution)/shard_map/ppermute | solution.py:683
  40.6 11.7 %collective-permute-start.7 = (bf16[1984,128]{1,0:T(8,128)(2,1)S(1)}, bf16[1984,128]{1,0:T(8,128)(2,1)S(1)}, u32[]{:S(2)}, u32[]{:S(2)}) collective-permute-start(bf16[1984,128]{1,0:T(8,128)(2,1)S(1)} %collective-permute-done.3.refs_4_), channel_id=1, source_target_pairs={{0,1},{1,0},{2,3},{3,2},{4,5},{5,4},{6,7},{7,6},{8,9},{9,8},{10,11... | collective-permute-start | bytes 1523720 | tf_op jit(solution)/shard_map/ppermute | solution.py:686
  48.9 3.9 %collective-permute-start.6 = (bf16[1984,128]{1,0:T(8,128)(2,1)S(1)}, bf16[1984,128]{1,0:T(8,128)(2,1)S(1)}, u32[]{:S(2)}, u32[]{:S(2)}) collective-permute-start(bf16[1984,128]{1,0:T(8,128)(2,1)S(1)} %collective-permute-done.2.refs_3_), channel_id=1, source_target_pairs={{0,1},{1,0},{2,3},{3,2},{4,5},{5,4},{6,7},{7,6},{8,9},{9,8},{10,11... | collective-permute-start | bytes 1523720 | tf_op jit(solution)/shard_map/ppermute | solution.py:686
  49.0 36.1 %collective-permute-start = (bf16[7936,128]{1,0:T(8,128)(2,1)S(1)}, bf16[7936,128]{1,0:T(8,128)(2,1)S(1)}, u32[]{:S(2)}, u32[]{:S(2)}) collective-permute-start(bf16[7936,128]{1,0:T(8,128)(2,1)S(1)} %get-tuple-element.38.refs_0_), channel_id=1, source_target_pairs={{0,1},{1,0},{2,3},{3,2},{4,5},{5,4},{6,7},{7,6},{8,9},{9,8},{10,11... | collective-permute-start | bytes 6094856 | tf_op jit(solution)/shard_map/ppermute | solution.py:686
  51.2 9.0 %collective-permute-start.4 = (bf16[1984,128]{1,0:T(8,128)(2,1)S(1)}, bf16[1984,128]{1,0:T(8,128)(2,1)S(1)}, u32[]{:S(2)}, u32[]{:S(2)}) collective-permute-start(bf16[1984,128]{1,0:T(8,128)(2,1)S(1)} %collective-permute-done.2.refs_3_), channel_id=1, source_target_pairs={{0,16},{1,9},{2,18},{3,11},{4,20},{5,13},{6,22},{7,15},{8,24},{9,1... | collective-permute-start | bytes 1523720 | tf_op jit(solution)/shard_map/ppermute | solution.py:683
  52.3 11.0 %collective-permute-start.21 = (bf16[1984,128]{1,0:T(8,128)(2,1)S(1)}, bf16[1984,128]{1,0:T(8,128)(2,1)S(1)}, u32[]{:S(2)}, u32[]{:S(2)}) collective-permute-start(bf16[1984,128]{1,0:T(8,128)(2,1)S(1)} %collective-permute-done.17.refs_18_), channel_id=1, source_target_pairs={{0,1},{1,0},{2,3},{3,2},{4,5},{5,4},{6,7},{7,6},{8,9},{9,8},{10,11... | collective-permute-start | bytes 1523720 | tf_op jit(solution)/shard_map/ppermute | solution.py:686
  52.3 11.0 %collective-permute-start.15 = (bf16[1984,128]{1,0:T(8,128)(2,1)S(1)}, bf16[1984,128]{1,0:T(8,128)(2,1)S(1)}, u32[]{:S(2)}, u32[]{:S(2)}) collective-permute-start(bf16[1984,128]{1,0:T(8,128)(2,1)S(1)} %collective-permute-done.11.refs_12_), channel_id=1, source_target_pairs={{0,1},{1,0},{2,3},{3,2},{4,5},{5,4},{6,7},{7,6},{8,9},{9,8},{10,11... | collective-permute-start | bytes 1523720 | tf_op jit(solution)/shard_map/ppermute | solution.py:686
  52.8 18.1 %collective-permute-start.19 = (bf16[1984,128]{1,0:T(8,128)(2,1)S(1)}, bf16[1984,128]{1,0:T(8,128)(2,1)S(1)}, u32[]{:S(2)}, u32[]{:S(2)}) collective-permute-start(bf16[1984,128]{1,0:T(8,128)(2,1)S(1)} %collective-permute-done.17.refs_18_), channel_id=1, source_target_pairs={{0,16},{1,9},{2,18},{3,11},{4,20},{5,13},{6,22},{7,15},{8,24},{9,1... | collective-permute-start | bytes 1523720 | tf_op jit(solution)/shard_map/ppermute | solution.py:683
  60.2 15.0 %collective-permute-start.18 = (bf16[1984,128]{1,0:T(8,128)(2,1)S(1)}, bf16[1984,128]{1,0:T(8,128)(2,1)S(1)}, u32[]{:S(2)}, u32[]{:S(2)}) collective-permute-start(bf16[1984,128]{1,0:T(8,128)(2,1)S(1)} %collective-permute-done.17.refs_18_), channel_id=1, source_target_pairs={{0,8},{1,17},{2,10},{3,19},{4,12},{5,21},{6,14},{7,23},{8,0},{9,25... | collective-permute-start | bytes 1523720 | tf_op jit(solution)/shard_map/ppermute | solution.py:683
  63.3 12.0 %collective-permute-start.14 = (bf16[1984,128]{1,0:T(8,128)(2,1)S(1)}, bf16[1984,128]{1,0:T(8,128)(2,1)S(1)}, u32[]{:S(2)}, u32[]{:S(2)}) collective-permute-start(bf16[1984,128]{1,0:T(8,128)(2,1)S(1)} %collective-permute-done.10.refs_11_), channel_id=1, source_target_pairs={{0,1},{1,0},{2,3},{3,2},{4,5},{5,4},{6,7},{7,6},{8,9},{9,8},{10,11... | collective-permute-start | bytes 1523720 | tf_op jit(solution)/shard_map/ppermute | solution.py:686
  63.3 13.2 %collective-permute-start.12 = (bf16[1984,128]{1,0:T(8,128)(2,1)S(1)}, bf16[1984,128]{1,0:T(8,128)(2,1)S(1)}, u32[]{:S(2)}, u32[]{:S(2)}) collective-permute-start(bf16[1984,128]{1,0:T(8,128)(2,1)S(1)} %collective-permute-done.10.refs_11_), channel_id=1, source_target_pairs={{0,16},{1,9},{2,18},{3,11},{4,20},{5,13},{6,22},{7,15},{8,24},{9,1... | collective-permute-start | bytes 1523720 | tf_op jit(solution)/shard_map/ppermute | solution.py:683
  71.0 5.6 %collective-permute-start.8 = (bf16[1984,128]{1,0:T(8,128)(2,1)S(1)}, bf16[1984,128]{1,0:T(8,128)(2,1)S(1)}, u32[]{:S(2)}, u32[]{:S(2)}) collective-permute-start(bf16[1984,128]{1,0:T(8,128)(2,1)S(1)} %collective-permute-done.4.refs_5_), channel_id=1, source_target_pairs={{0,1},{1,0},{2,3},{3,2},{4,5},{5,4},{6,7},{7,6},{8,9},{9,8},{10,11... | collective-permute-start | bytes 1523720 | tf_op jit(solution)/shard_map/ppermute | solution.py:686
  75.3 9.0 %collective-permute-start.20 = (bf16[1984,128]{1,0:T(8,128)(2,1)S(1)}, bf16[1984,128]{1,0:T(8,128)(2,1)S(1)}, u32[]{:S(2)}, u32[]{:S(2)}) collective-permute-start(bf16[1984,128]{1,0:T(8,128)(2,1)S(1)} %collective-permute-done.18.refs_19_), channel_id=1, source_target_pairs={{0,16},{1,9},{2,18},{3,11},{4,20},{5,13},{6,22},{7,15},{8,24},{9,1... | collective-permute-start | bytes 1523720 | tf_op jit(solution)/shard_map/ppermute | solution.py:683
  75.3 9.9 %collective-permute-start.22 = (bf16[1984,128]{1,0:T(8,128)(2,1)S(1)}, bf16[1984,128]{1,0:T(8,128)(2,1)S(1)}, u32[]{:S(2)}, u32[]{:S(2)}) collective-permute-start(bf16[1984,128]{1,0:T(8,128)(2,1)S(1)} %collective-permute-done.18.refs_19_), channel_id=1, source_target_pairs={{0,1},{1,0},{2,3},{3,2},{4,5},{5,4},{6,7},{7,6},{8,9},{9,8},{10,11... | collective-permute-start | bytes 1523720 | tf_op jit(solution)/shard_map/ppermute | solution.py:686
  76.6 8.5 %collective-permute-start.23 = (bf16[1984,128]{1,0:T(8,128)(2,1)S(1)}, bf16[1984,128]{1,0:T(8,128)(2,1)S(1)}, u32[]{:S(2)}, u32[]{:S(2)}) collective-permute-start(bf16[1984,128]{1,0:T(8,128)(2,1)S(1)} %collective-permute-done.19.refs_20_), channel_id=1, source_target_pairs={{0,1},{1,0},{2,3},{3,2},{4,5},{5,4},{6,7},{7,6},{8,9},{9,8},{10,11... | collective-permute-start | bytes 1523720 | tf_op jit(solution)/shard_map/ppermute | solution.py:686
  76.6 8.6 %collective-permute-start.16 = (bf16[1984,128]{1,0:T(8,128)(2,1)S(1)}, bf16[1984,128]{1,0:T(8,128)(2,1)S(1)}, u32[]{:S(2)}, u32[]{:S(2)}) collective-permute-start(bf16[1984,128]{1,0:T(8,128)(2,1)S(1)} %collective-permute-done.12.refs_13_), channel_id=1, source_target_pairs={{0,1},{1,0},{2,3},{3,2},{4,5},{5,4},{6,7},{7,6},{8,9},{9,8},{10,11... | collective-permute-start | bytes 1523720 | tf_op jit(solution)/shard_map/ppermute | solution.py:686
  84.3 1.9 collective-permute-start.24
  119.3 4.5 %collective-permute-start.34 = (bf16[7936,128]{1,0:T(8,128)(2,1)}, bf16[7936,128]{1,0:T(8,128)(2,1)S(1)}, u32[]{:S(2)}, u32[]{:S(2)}) collective-permute-start(bf16[7936,128]{1,0:T(8,128)(2,1)} %get-tuple-element.63), channel_id=1, source_target_pairs={{0,1},{1,0},{2,3},{3,2},{4,5},{5,4},{6,7},{7,6},{8,9},{9,8},{10,11... | collective-permute-start | bytes 6094856 | tf_op jit(solution)/shard_map/ppermute | solution.py:686
  119.8 7.2 %collective-permute-start.31 = (bf16[7936,128]{1,0:T(8,128)(2,1)}, bf16[7936,128]{1,0:T(8,128)(2,1)S(1)}, u32[]{:S(2)}, u32[]{:S(2)}) collective-permute-start(bf16[7936,128]{1,0:T(8,128)(2,1)} %get-tuple-element.57), channel_id=1, source_target_pairs={{0,1},{1,0},{2,3},{3,2},{4,5},{5,4},{6,7},{7,6},{8,9},{9,8},{10,11... | collective-permute-start | bytes 6094856 | tf_op jit(solution)/shard_map/ppermute | solution.py:686
  119.9 10.2 %collective-permute-start.28 = (bf16[7936,128]{1,0:T(8,128)(2,1)}, bf16[7936,128]{1,0:T(8,128)(2,1)S(1)}, u32[]{:S(2)}, u32[]{:S(2)}) collective-permute-start(bf16[7936,128]{1,0:T(8,128)(2,1)} %get-tuple-element.51), channel_id=1, source_target_pairs={{0,1},{1,0},{2,3},{3,2},{4,5},{5,4},{6,7},{7,6},{8,9},{9,8},{10,11... | collective-permute-start | bytes 6094856 | tf_op jit(solution)/shard_map/ppermute | solution.py:686
  120.4 23.9 %collective-permute-start.25 = (bf16[7936,128]{1,0:T(8,128)(2,1)}, bf16[7936,128]{1,0:T(8,128)(2,1)S(1)}, u32[]{:S(2)}, u32[]{:S(2)}) collective-permute-start(bf16[7936,128]{1,0:T(8,128)(2,1)} %get-tuple-element.45), channel_id=1, source_target_pairs={{0,1},{1,0},{2,3},{3,2},{4,5},{5,4},{6,7},{7,6},{8,9},{9,8},{10,11... | collective-permute-start | bytes 6094856 | tf_op jit(solution)/shard_map/ppermute | solution.py:686
  127.0 14.5 %collective-permute-start.35 = (bf16[2,1984,128]{2,1,0:T(8,128)(2,1)S(1)}, bf16[2,1984,128]{2,1,0:T(8,128)(2,1)S(1)}, u32[]{:S(2)}, u32[]{:S(2)}) collective-permute-start(bf16[2,1984,128]{2,1,0:T(8,128)(2,1)S(1)} %get-tuple-element.65), channel_id=1, source_target_pairs={{0,16},{1,9},{2,18},{3,11},{4,20},{5,13},{6,22},{7,15},{8,24},{9,1... | collective-permute-start | bytes 3047432 | tf_op jit(solution)/shard_map/ppermute | solution.py:683
  128.5 29.3 %collective-permute-start.32 = (bf16[2,1984,128]{2,1,0:T(8,128)(2,1)S(1)}, bf16[2,1984,128]{2,1,0:T(8,128)(2,1)S(1)}, u32[]{:S(2)}, u32[]{:S(2)}) collective-permute-start(bf16[2,1984,128]{2,1,0:T(8,128)(2,1)S(1)} %get-tuple-element.59), channel_id=1, source_target_pairs={{0,16},{1,9},{2,18},{3,11},{4,20},{5,13},{6,22},{7,15},{8,24},{9,1... | collective-permute-start | bytes 3047432 | tf_op jit(solution)/shard_map/ppermute | solution.py:683
  131.2 43.0 %collective-permute-start.29 = (bf16[2,1984,128]{2,1,0:T(8,128)(2,1)S(1)}, bf16[2,1984,128]{2,1,0:T(8,128)(2,1)S(1)}, u32[]{:S(2)}, u32[]{:S(2)}) collective-permute-start(bf16[2,1984,128]{2,1,0:T(8,128)(2,1)S(1)} %get-tuple-element.53), channel_id=1, source_target_pairs={{0,16},{1,9},{2,18},{3,11},{4,20},{5,13},{6,22},{7,15},{8,24},{9,1... | collective-permute-start | bytes 3047432 | tf_op jit(solution)/shard_map/ppermute | solution.py:683
  141.7 18.9 %collective-permute-start.36 = (bf16[1984,128]{1,0:T(8,128)(2,1)S(1)}, bf16[1984,128]{1,0:T(8,128)(2,1)S(1)}, u32[]{:S(2)}, u32[]{:S(2)}) collective-permute-start(bf16[1984,128]{1,0:T(8,128)(2,1)S(1)} %get-tuple-element.67), channel_id=1, source_target_pairs={{0,8},{1,17},{2,10},{3,19},{4,12},{5,21},{6,14},{7,23},{8,0},{9,25... | collective-permute-start | bytes 1523720 | tf_op jit(solution)/shard_map/ppermute | solution.py:683
  145.3 45.2 %collective-permute-start.26 = (bf16[2,1984,128]{2,1,0:T(8,128)(2,1)S(1)}, bf16[2,1984,128]{2,1,0:T(8,128)(2,1)S(1)}, u32[]{:S(2)}, u32[]{:S(2)}) collective-permute-start(bf16[2,1984,128]{2,1,0:T(8,128)(2,1)S(1)} %get-tuple-element.47), channel_id=1, source_target_pairs={{0,16},{1,9},{2,18},{3,11},{4,20},{5,13},{6,22},{7,15},{8,24},{9,1... | collective-permute-start | bytes 3047432 | tf_op jit(solution)/shard_map/ppermute | solution.py:683
  158.1 18.8 %collective-permute-start.33 = (bf16[1984,128]{1,0:T(8,128)(2,1)S(1)}, bf16[1984,128]{1,0:T(8,128)(2,1)S(1)}, u32[]{:S(2)}, u32[]{:S(2)}) collective-permute-start(bf16[1984,128]{1,0:T(8,128)(2,1)S(1)} %get-tuple-element.61), channel_id=1, source_target_pairs={{0,8},{1,17},{2,10},{3,19},{4,12},{5,21},{6,14},{7,23},{8,0},{9,25... | collective-permute-start | bytes 1523720 | tf_op jit(solution)/shard_map/ppermute | solution.py:683
  160.7 16.2 %collective-permute-start.37 = (bf16[1984,128]{1,0:T(8,128)(2,1)S(1)}, bf16[1984,128]{1,0:T(8,128)(2,1)S(1)}, u32[]{:S(2)}, u32[]{:S(2)}) collective-permute-start(bf16[1984,128]{1,0:T(8,128)(2,1)S(1)} %add_all.4), channel_id=1, source_target_pairs={{4,0},{5,1},{0,2},{1,3},{6,4},{7,5},{2,6},{3,7},{12,8},{13,9},{8,1... | collective-permute-start | bytes 1523720 | tf_op jit(solution)/shard_map/ppermute | solution.py:689
  174.4 18.9 %collective-permute-start.30 = (bf16[1984,128]{1,0:T(8,128)(2,1)S(1)}, bf16[1984,128]{1,0:T(8,128)(2,1)S(1)}, u32[]{:S(2)}, u32[]{:S(2)}) collective-permute-start(bf16[1984,128]{1,0:T(8,128)(2,1)S(1)} %get-tuple-element.55), channel_id=1, source_target_pairs={{0,8},{1,17},{2,10},{3,19},{4,12},{5,21},{6,14},{7,23},{8,0},{9,25... | collective-permute-start | bytes 1523720 | tf_op jit(solution)/shard_map/ppermute | solution.py:683
  177.1 16.1 %collective-permute-start.38 = (bf16[1984,128]{1,0:T(8,128)(2,1)S(1)}, bf16[1984,128]{1,0:T(8,128)(2,1)S(1)}, u32[]{:S(2)}, u32[]{:S(2)}) collective-permute-start(bf16[1984,128]{1,0:T(8,128)(2,1)S(1)} %add_all.5), channel_id=1, source_target_pairs={{4,0},{5,1},{0,2},{1,3},{6,4},{7,5},{2,6},{3,7},{12,8},{13,9},{8,1... | collective-permute-start | bytes 1523720 | tf_op jit(solution)/shard_map/ppermute | solution.py:689
  190.7 9.5 %collective-permute-start.27 = (bf16[1984,128]{1,0:T(8,128)(2,1)S(1)}, bf16[1984,128]{1,0:T(8,128)(2,1)S(1)}, u32[]{:S(2)}, u32[]{:S(2)}) collective-permute-start(bf16[1984,128]{1,0:T(8,128)(2,1)S(1)} %get-tuple-element.49), channel_id=1, source_target_pairs={{0,8},{1,17},{2,10},{3,19},{4,12},{5,21},{6,14},{7,23},{8,0},{9,25... | collective-permute-start | bytes 1523720 | tf_op jit(solution)/shard_map/ppermute | solution.py:683
  193.4 12.3 %collective-permute-start.39 = (bf16[1984,128]{1,0:T(8,128)(2,1)S(1)}, bf16[1984,128]{1,0:T(8,128)(2,1)S(1)}, u32[]{:S(2)}, u32[]{:S(2)}) collective-permute-start(bf16[1984,128]{1,0:T(8,128)(2,1)S(1)} %add_all.6), channel_id=1, source_target_pairs={{4,0},{5,1},{0,2},{1,3},{6,4},{7,5},{2,6},{3,7},{12,8},{13,9},{8,1... | collective-permute-start | bytes 1523720 | tf_op jit(solution)/shard_map/ppermute | solution.py:689
  205.9 14.2 %collective-permute-start.40 = (bf16[1984,128]{1,0:T(8,128)(2,1)S(1)}, bf16[1984,128]{1,0:T(8,128)(2,1)S(1)}, u32[]{:S(2)}, u32[]{:S(2)}) collective-permute-start(bf16[1984,128]{1,0:T(8,128)(2,1)S(1)} %add_all.7.refs_0_), channel_id=1, source_target_pairs={{0,8},{1,17},{2,10},{3,19},{4,12},{5,21},{6,14},{7,23},{8,0},{9,25... | collective-permute-start | bytes 1523720 | tf_op jit(solution)/shard_map/ppermute | solution.py:683
  207.8 13.5 %collective-permute-start.41 = (bf16[1984,128]{1,0:T(8,128)(2,1)S(1)}, bf16[1984,128]{1,0:T(8,128)(2,1)S(1)}, u32[]{:S(2)}, u32[]{:S(2)}) collective-permute-start(bf16[1984,128]{1,0:T(8,128)(2,1)S(1)} %add_all.7.refs_0_), channel_id=1, source_target_pairs={{0,16},{1,9},{2,18},{3,11},{4,20},{5,13},{6,22},{7,15},{8,24},{9,1... | collective-permute-start | bytes 1523720 | tf_op jit(solution)/shard_map/ppermute | solution.py:683
  220.1 9.0 %collective-permute-start.42 = (bf16[1984,128]{1,0:T(8,128)(2,1)S(1)}, bf16[1984,128]{1,0:T(8,128)(2,1)S(1)}, u32[]{:S(2)}, u32[]{:S(2)}) collective-permute-start(bf16[1984,128]{1,0:T(8,128)(2,1)S(1)} %collective-permute-done.40.refs_1_), channel_id=1, source_target_pairs={{0,16},{1,9},{2,18},{3,11},{4,20},{5,13},{6,22},{7,15},{8,24},{9,1... | collective-permute-start | bytes 1523720 | tf_op jit(solution)/shard_map/ppermute | solution.py:683
  (33 other events, 617.5 us)

commit v3 on v1

--- a/solution.py
+++ b/solution.py
@@ -37,6 +37,8 @@
 
 F32 = jnp.float32
 BF16 = jnp.bfloat16
+TOKEN = (8, LANES)
+HEAD = 0.50
 
 
 def up_to(value, step):
@@ -72,6 +74,7 @@
         ]
         self.rows = up_to(max(used), 8 * ROUND)
         self.quarter = self.rows // 4
+        self.head = up_to(int(self.quarter * HEAD), ROUND)
         self.runs = []
         for matrix, (rows, cols) in enumerate(MATRICES):
             groups = []
@@ -91,6 +94,8 @@
                 else:
                     runs.append([row, row + ROUND, places])
             self.runs.append([tuple(run) for run in runs])
+        self.attention_blocks = max(i for i, found in enumerate(self.regions) if found[0][0] < UP)
+        self.vector_blocks = min(i for i, found in enumerate(self.regions) if found[-1][0] == VEC)
         self.margin = ROUND * (FF // LANES)
         self.flat_rows = up_to(up_to(self.length, LANES) // LANES + 1, 8)
         self.buffer_rows = self.margin + self.flat_rows + self.margin + 8
@@ -161,7 +166,7 @@
             buffer[pl.ds(at, 64), :] = pltpu.roll(value, shift, 1)
             return carry
 
-        lax.fori_loop(0, chunk // 8192, roll_in, 0)
+        lax.fori_loop(0, chunk // 8192, roll_in, 0, unroll=True)
 
         @pl.when(step == steps - 1)
         def _():
@@ -177,6 +182,7 @@
             quarter_ref[...] = block_ref[pl.ds(mine, geo.quarter), :]
 
     buffer_rows = geo.margin + max(steps * rows, geo.flat_rows) + geo.margin + 8
+    sizes = [geo.rows, geo.quarter]
     return pl.pallas_call(
         kernel,
         grid=(steps,),
@@ -185,16 +191,10 @@
             pl.BlockSpec(memory_space=pltpu.SMEM),
             pl.BlockSpec((chunk,), lambda i: (i,)),
         ],
-        out_specs=[
-            pl.BlockSpec((geo.rows, LANES), lambda i: (0, 0)),
-            pl.BlockSpec((geo.quarter, LANES), lambda i: (0, 0)),
-        ],
-        out_shape=[
-            jax.ShapeDtypeStruct((geo.rows, LANES), BF16),
-            jax.ShapeDtypeStruct((geo.quarter, LANES), BF16),
-        ],
+        out_specs=[pl.BlockSpec(memory_space=pltpu.VMEM)] * len(sizes),
+        out_shape=[jax.ShapeDtypeStruct((size, LANES), BF16) for size in sizes],
         scratch_shapes=[pltpu.VMEM((buffer_rows, LANES), F32)],
-        compiler_params=pltpu.CompilerParams(vmem_limit_bytes=32 * 2**20),
+        compiler_params=pltpu.CompilerParams(vmem_limit_bytes=16 * 2**20),
         name="pack_block",
     )(where, geo.table(), params)
 
@@ -208,22 +208,15 @@
 
     def kernel(where_ref, table_ref, *refs):
         piece_refs = refs[:count]
-        params_ref, one_ref, two_ref, new_params_ref, new_one_ref, new_two_ref, block, buffer, sems = refs[count:]
+        params_ref, one_ref, two_ref, new_params_ref, new_one_ref, new_two_ref, block, buffer = refs[count:]
         step = pl.program_id(0)
         index = where_ref[0]
         shift = (index * geo.length) % LANES
 
         @pl.when(step == 0)
         def _():
-            places = piece_places(index, where_ref[1])
-            copies = [
-                pltpu.make_async_copy(ref, block.at[pl.ds(aligned(at), ref.shape[0]), :], sems.at[i])
-                for i, (ref, at) in enumerate(zip(piece_refs, places))
-            ]
-            for copy in copies:
-                copy.start()
-            for copy in copies:
-                copy.wait()
+            for piece, start, length, at in piece_places(index, where_ref[1]):
+                block[pl.ds(aligned(at), length), :] = piece_refs[piece][pl.ds(start, length), :]
 
             def move(flat, width, place):
                 buffer[pl.ds(flat, ROUND, stride=width), :] = block[pl.ds(place, ROUND), :].astype(F32)
@@ -253,7 +246,7 @@
             new_two_ref[span] = new_two.reshape(8192)
             return carry
 
-        lax.fori_loop(0, chunk // 8192, update, 0)
+        lax.fori_loop(0, chunk // 8192, update, 0, unroll=True)
 
     buffer_rows = geo.margin + max(steps * rows, geo.flat_rows) + geo.margin + 8
     flat_spec = pl.BlockSpec((chunk,), lambda i: (i,))
@@ -262,16 +255,15 @@
         kernel,
         grid=(steps,),
         in_specs=[pl.BlockSpec(memory_space=pltpu.SMEM)] * 2
-        + [pl.BlockSpec(memory_space=pl.ANY)] * count
+        + [pl.BlockSpec(memory_space=pltpu.VMEM)] * count
         + [flat_spec] * 3,
         out_specs=[flat_spec] * 3,
         out_shape=[flat_shape] * 3,
         scratch_shapes=[
             pltpu.VMEM((geo.rows, LANES), BF16),
             pltpu.VMEM((buffer_rows, LANES), F32),
-            pltpu.SemaphoreType.DMA((count,)),
         ],
-        compiler_params=pltpu.CompilerParams(vmem_limit_bytes=48 * 2**20),
+        compiler_params=pltpu.CompilerParams(vmem_limit_bytes=24 * 2**20),
         name="optimizer_step",
     )(where, geo.table(), *pieces, params, moment_one, moment_two)
 
@@ -298,33 +290,55 @@
     )
 
 
-def model_step(geo, tokens, cotangent, lengths, sinusoid, where, weights, weight_places, outs_of):
+def model_step(geo, tokens, cotangent, lengths, sinusoid, where, pieces, piece_places, grad_parts):
     seqs = tokens.shape[0] // L
     rows = tokens.shape[0]
-    count = len(weights)
+    count = len(pieces)
     pairs = HEADS // 2
-    grads = geo.shards
     scale = HEAD_DIM ** (-0.5)
+    grad_shapes = [
+        ((geo.shards if blocks is None else len(blocks), length, LANES)) for blocks, _, length in grad_parts(0)
+    ]
+    in_count = sum(geo.shards if isinstance(runs, int) else len(runs) for runs in piece_places(0, 0))
+    out_count = sum(shape[0] for shape in grad_shapes)
 
     def kernel(where_ref, lengths_ref, tokens_ref, cotangent_ref, sinusoid_ref, *refs):
-        weight_refs = refs[:count]
+        piece_refs = refs[:count]
         refs = refs[count:]
         output_ref, token_grad_ref = refs[:2]
-        grad_refs = refs[2 : 2 + grads] if outs_of else refs[2:3]
+        grad_refs = refs[2 : 2 + len(grad_shapes)]
         (
             store, vecs, vec_grads, rows_zero, rows_low, qkv, probs, context, hat_one, hidden, hidden_low, hidden_t,
             act, slope, total, d_hidden, d_qkv, in_sems, out_sems,
-        ) = refs[2 + len(grad_refs) :]
+        ) = refs[2 + len(grad_shapes) :]
 
         index, replica = where_ref[0], where_ref[1]
-        copies = []
-        for i, (ref, (block, at)) in enumerate(zip(weight_refs, weight_places(index, replica))):
-            target = store if block is None else store.at[block, pl.ds(aligned(at), ref.shape[0]), :]
-            copies.append(pltpu.make_async_copy(ref, target, in_sems.at[i]))
-        for copy in copies:
-            copy.start()
-        for copy in copies:
-            copy.wait()
+
+        def in_waves(copies, is_early, early, act):
+            for block, copy in copies:
+                now = is_early(block)
+                if isinstance(block, int):
+                    if early == now:
+                        act(copy)
+                else:
+                    pl.when(now if early else jnp.logical_not(now))(lambda copy=copy: act(copy))
+
+        arrivals = []
+        for ref, runs in zip(piece_refs, piece_places(index, replica)):
+            if isinstance(runs, int):
+                runs = [(block, None, ref.shape[1], runs) for block in range(geo.shards)]
+            for block, start, length, at in runs:
+                source = ref.at[block] if start is None else ref.at[pl.ds(start, length), :]
+                target = store.at[block, pl.ds(aligned(at), length), :]
+                arrivals.append((block, pltpu.make_async_copy(source, target, in_sems.at[len(arrivals)])))
+
+        def read_first(block):
+            early, late = block <= geo.attention_blocks, block >= geo.vector_blocks
+            return early or late if isinstance(block, int) else early | late
+
+        in_waves(arrivals, read_first, True, lambda copy: copy.start())
+        in_waves(arrivals, read_first, False, lambda copy: copy.start())
+        in_waves(arrivals, read_first, True, lambda copy: copy.wait())
 
         def spans(matrix, low, high):
             for first, last, places in geo.runs[matrix]:
@@ -427,6 +441,8 @@
         hidden_low[...] = value.astype(BF16)
         hidden_t[...] = value.astype(BF16).T
 
+        in_waves(arrivals, read_first, False, lambda copy: copy.wait())
+
         def up_step(tile, carry):
             pre = nn(hidden_low[...], load_wide(UP, 2 * tile, 2)) + vec(V_UP + 2 * tile, 2)
             below = 0.5 * (1.0 + lax.erf(pre * (0.5**0.5)))
@@ -461,6 +477,18 @@
             vec_grad(V_UP + 2 * tile, d_up.astype(F32))
             d_hidden[...] += nt(d_up, load_wide(UP, 2 * tile, 2))
             save_wide(UP, 2 * tile, nn(hidden_t[...], d_up))
+
+        departures = []
+        for ref, (blocks, at, length) in zip(grad_refs, grad_parts(index)):
+            for i, block in enumerate(range(geo.shards) if blocks is None else blocks):
+                source = store.at[block, pl.ds(at, length), :]
+                departures.append((block, pltpu.make_async_copy(source, ref.at[i], out_sems.at[len(departures)])))
+
+        def done_first(block):
+            late, early = block > geo.attention_blocks, block < geo.vector_blocks
+            return early and late if isinstance(block, int) else early & late
+
+        in_waves(departures, done_first, True, lambda copy: copy.start())
 
         d_out = d_hidden[...]
         hat = hat_one[...]
@@ -516,22 +544,10 @@
         save_wide(TIME_IN, 0, nn(sines.T, d_time_pre))
         save(VEC, 0, vec_grads[...].astype(BF16))
 
-        if outs_of:
-            copies = [
-                pltpu.make_async_copy(store.at[block], ref, out_sems.at[i])
-                for i, (ref, block) in enumerate(zip(grad_refs, outs_of(index)))
-            ]
-        else:
-            copies = [pltpu.make_async_copy(store, grad_refs[0], out_sems.at[0])]
-        for copy in copies:
-            copy.start()
-        for copy in copies:
-            copy.wait()
-
-    if outs_of:
-        grad_shapes = [jax.ShapeDtypeStruct((geo.rows, LANES), BF16)] * grads
-    else:
-        grad_shapes = [jax.ShapeDtypeStruct((geo.shards, geo.rows, LANES), BF16)]
+        in_waves(departures, done_first, False, lambda copy: copy.start())
+        in_waves(departures, done_first, True, lambda copy: copy.wait())
+        in_waves(departures, done_first, False, lambda copy: copy.wait())
+
     whole = pl.BlockSpec(memory_space=pltpu.VMEM)
     return pl.pallas_call(
         kernel,
@@ -539,7 +555,11 @@
         + [whole] * 3
         + [pl.BlockSpec(memory_space=pl.ANY)] * count,
         out_specs=[whole] * 2 + [pl.BlockSpec(memory_space=pl.ANY)] * len(grad_shapes),
-        out_shape=[jax.ShapeDtypeStruct((rows, D), BF16), jax.ShapeDtypeStruct((rows, D), F32)] + grad_shapes,
+        out_shape=[
+            jax.ShapeDtypeStruct((rows, D), BF16),
+            jax.ShapeDtypeStruct((rows, D), F32),
+        ]
+        + [jax.ShapeDtypeStruct(shape, BF16) for shape in grad_shapes],
         scratch_shapes=[
             pltpu.VMEM((geo.shards, geo.rows, LANES), BF16),
             pltpu.VMEM((VEC_ROWS, LANES), F32),
@@ -558,12 +578,12 @@
             pltpu.VMEM((rows, D), F32),
             pltpu.VMEM((rows, D), F32),
             pltpu.VMEM((rows, 3 * D), BF16),
-            pltpu.SemaphoreType.DMA((count,)),
-            pltpu.SemaphoreType.DMA((len(grad_shapes),)),
+            pltpu.SemaphoreType.DMA((in_count,)),
+            pltpu.SemaphoreType.DMA((out_count,)),
         ],
-        compiler_params=pltpu.CompilerParams(vmem_limit_bytes=60 * 2**20),
+        compiler_params=pltpu.CompilerParams(vmem_limit_bytes=18 * 2**20 + geo.shards * geo.rows * LANES * 2),
         name="model_step",
-    )(where, lengths, tokens, cotangent, sinusoid, *weights)
+    )(where, lengths, tokens, cotangent, sinusoid, *pieces)
 
 
 def neighbor_quarters(index, replica):
@@ -571,61 +591,100 @@
     return replica, replica ^ (1 + core), replica ^ (2 - core), replica ^ 3
 
 
-def add_cores(geo, keep, got, where):
-    size = geo.quarter
-
-    def kernel(where_ref, keep_ref, got_ref, near_ref, far_ref):
-        order = neighbor_quarters(where_ref[0], where_ref[1])
-        for i, quarter in enumerate(order):
-            span = pl.ds(pl.multiple_of(quarter * size, ROUND), size)
-            value = (keep_ref[span, :].astype(F32) + got_ref[span, :].astype(F32)).astype(BF16)
-            (near_ref if i < 2 else far_ref)[i % 2] = value
+def small_step(name, body, scalars, inputs, shapes, after):
+    def kernel(*refs):
+        first, last = len(scalars), len(scalars) + len(inputs)
+        body(refs[:first], refs[first:last], refs[last + len(after) : -1])
+        refs[-1][...] = jnp.zeros(TOKEN, F32)
 
     whole = pl.BlockSpec(memory_space=pltpu.VMEM)
     return pl.pallas_call(
         kernel,
-        in_specs=[pl.BlockSpec(memory_space=pltpu.SMEM), whole, whole],
-        out_specs=[whole, whole],
-        out_shape=[jax.ShapeDtypeStruct((2, size, LANES), BF16)] * 2,
-        compiler_params=pltpu.CompilerParams(vmem_limit_bytes=32 * 2**20),
-        name="add_cores",
-    )(where, keep, got)
-
-
-def add_pair(near, got):
-    size = near.shape[1]
-
-    def kernel(near_ref, got_ref, own_ref, next_ref):
-        for i, ref in enumerate((own_ref, next_ref)):
-            ref[...] = (near_ref[i].astype(F32) + got_ref[i].astype(F32)).astype(BF16)
-
-    whole = pl.BlockSpec(memory_space=pltpu.VMEM)
-    return pl.pallas_call(
-        kernel,
-        in_specs=[whole, whole],
-        out_specs=[whole, whole],
-        out_shape=[jax.ShapeDtypeStruct((size, LANES), BF16)] * 2,
-        compiler_params=pltpu.CompilerParams(vmem_limit_bytes=32 * 2**20),
-        name="add_pair",
-    )(near, got)
-
-
-def add_all(*items):
-    def kernel(*refs):
-        value = refs[0][...].astype(F32)
-        for ref in refs[1:-1]:
-            value = value + ref[...].astype(F32)
-        refs[-1][...] = value.astype(BF16)
-
-    whole = pl.BlockSpec(memory_space=pltpu.VMEM)
-    return pl.pallas_call(
-        kernel,
-        in_specs=[whole] * len(items),
-        out_specs=whole,
-        out_shape=jax.ShapeDtypeStruct(items[0].shape, BF16),
-        compiler_params=pltpu.CompilerParams(vmem_limit_bytes=32 * 2**20),
-        name="add_all",
-    )(*items)
+        in_specs=[pl.BlockSpec(memory_space=pltpu.SMEM)] * len(scalars)
+        + [whole] * len(inputs)
+        + [pl.BlockSpec(memory_space=pl.ANY)] * len(after),
+        out_specs=[whole] * (len(shapes) + 1),
+        out_shape=[jax.ShapeDtypeStruct(shape, BF16) for shape in shapes] + [jax.ShapeDtypeStruct(TOKEN, F32)],
+        compiler_params=pltpu.CompilerParams(vmem_limit_bytes=12 * 2**20),
+        name=name,
+    )(*scalars, *inputs, *after)
+
+
+def stack_up(after, items):
+    def body(scalars, inputs, outs):
+        at = 0
+        for ref in inputs:
+            outs[0][pl.ds(at, ref.shape[0]), :] = ref[...]
+            at += ref.shape[0]
+
+    return small_step("stack_up", body, [], items, [(sum(item.shape[0] for item in items), LANES)], after)
+
+
+def join_block(geo, where, after, quarters):
+    def body(scalars, inputs, outs):
+        for ref, quarter in zip(inputs, neighbor_quarters(scalars[0][0], scalars[0][1])):
+            outs[0][pl.ds(aligned(quarter * geo.quarter), geo.quarter), :] = ref[...]
+
+    return small_step("join_block", body, [where], quarters, [(geo.rows, LANES)], after)
+
+
+def reduce_step(geo, where, after, cores=None, pair=None, items=None, head=None, tails=None, halves=False):
+    size = geo.quarter
+    inputs, shapes = [], []
+    if cores is not None:
+        inputs += cores + [tails] * (tails is not None)
+        shapes += [(2, head or size, LANES)] * 2 + [(4 * (size - (head or 0)), LANES)] * (head is not None)
+    if pair is not None:
+        inputs += pair
+        rows = pair[0].shape[1]
+        shapes += [(rows // 2, LANES)] * 4 if halves else [(rows, LANES)] * 2
+    if items is not None:
+        inputs += items
+        rows = items[0].shape[0]
+        shapes += [(rows // 2, LANES)] * 2 if halves else [(rows, LANES)]
+
+    def body(scalars, inputs, outs):
+        inputs, outs = list(inputs), list(outs)
+
+        def save(value):
+            start = 0
+            while start < value.shape[0]:
+                out = outs.pop(0)
+                out[...] = value[start : start + out.shape[0], :].astype(BF16)
+                start += out.shape[0]
+
+        if cores is not None:
+            keep, got = inputs[:2]
+            for i, quarter in enumerate(neighbor_quarters(scalars[0][0], scalars[0][1])):
+                span = pl.ds(aligned(quarter * size), head or size)
+                value = keep[span, :].astype(F32) + got[span, :].astype(F32)
+                if tails is not None:
+                    more = inputs[2].shape[0] // 4
+                    tail = inputs[2][pl.ds(aligned(quarter * more), more), :].astype(F32)
+                    value = jnp.concatenate([value[: size - more], value[size - more :] + tail], axis=0)
+                outs[i // 2][i % 2] = value.astype(BF16)
+            if head is not None:
+                more = size - head
+                for i in range(4):
+                    span = pl.ds(i * size + head, more)
+                    value = keep[span, :].astype(F32) + got[span, :].astype(F32)
+                    outs[2][pl.ds(i * more, more), :] = value.astype(BF16)
+            inputs = inputs[2 + (tails is not None) :]
+            del outs[: 2 + (head is not None)]
+        if pair is not None:
+            near, got = inputs[:2]
+            for i in range(2):
+                save(near[i].astype(F32) + got[i].astype(F32))
+            inputs = inputs[2:]
+        if items is not None:
+            edges = sorted({0} | {ref.shape[0] for ref in inputs})
+            values = []
+            for low, high in zip(edges, edges[1:]):
+                parts = [ref[pl.ds(low, high - low), :].astype(F32) for ref in inputs if ref.shape[0] > low]
+                values.append(sum(parts[1:], parts[0]))
+            save(values[0] if len(values) == 1 else jnp.concatenate(values, axis=0))
+
+    return small_step("reduce_step", body, [where], inputs, shapes, after)
 
 
 def ring_order(size):
@@ -640,7 +699,7 @@
 
 
 def make_local(dp, fsdp):
-    direct = dp == 4 and fsdp == 8
+    direct_links = dp == 4 and fsdp == 8
     chips = fsdp // 2
     order = ring_order(chips)
     before = [order[order.index(chip) - 1] for chip in range(chips)]
@@ -661,10 +720,12 @@
     def core_swap(value):
         return lax.ppermute(value, "fsdp", [(index, index ^ 1) for index in range(fsdp)])
 
-    def ring_hop(value):
-        return lax.ppermute(
-            value, "fsdp", [(before[chip] * 2 + core, chip * 2 + core) for chip in range(chips) for core in range(2)]
-        )
+    def ring_hop(value, hops=1):
+        pairs = []
+        for place, chip in enumerate(order):
+            target = order[(place + hops) % chips]
+            pairs += [(chip * 2 + core, target * 2 + core) for core in range(2)]
+        return lax.ppermute(value, "fsdp", pairs)
 
     def first_way(value):
         return permute(value, ("dp", "fsdp"), lambda r, i: (r ^ (1 + i % 2)) * fsdp + i)
@@ -685,40 +746,63 @@
 
         block, quarter = pack_block(geo, params, where)
 
-        if direct:
-            weights = [block, core_swap(block)]
-            for _ in range(1, chips):
-                quarter = ring_hop(quarter)
-                one = first_way(quarter)
-                two = second_way(quarter)
-                three = second_way(one)
-                four = [quarter, one, two, three]
-                weights += four + [core_swap(item) for item in four]
+        def block_of(hops, other=0):
+            return lambda index: chip_before(index // 2, hops) * 2 + (index % 2 ^ other)
+
+        if direct_links:
+            swapped = core_swap(block)
+            pieces = [block, swapped]
+            quarter_1, token = stack_up([], [ring_hop(quarter)])
+            hop, one_1, two_1 = ring_hop(quarter_1), first_way(quarter_1), second_way(quarter_1)
+            quarter_2, token = stack_up([token, swapped], [hop])
+            hop, one_2, two_2 = ring_hop(quarter_2), first_way(quarter_2), second_way(quarter_2)
+            passed, token = stack_up([token, two_1], [one_1])
+            three_1 = second_way(passed)
+            quarter_3, token = stack_up([token], [hop])
+            one_3, two_3 = first_way(quarter_3), second_way(quarter_3)
+            passed, token = stack_up([token, two_2], [one_2])
+            three_2 = second_way(passed)
+            block, token = join_block(geo, where, [token], [quarter_1, one_1, two_1, three_1])
+            swapped = core_swap(block)
+            pieces += [block, swapped]
+            passed, token = stack_up([token, two_3], [one_3])
+            three_3 = second_way(passed)
+            stack, token = stack_up([token], [quarter_2, one_2, two_2, quarter_3, one_3, two_3])
+            stack_swapped = core_swap(stack)
+            pieces += [stack, stack_swapped]
+            last_2, token = stack_up([token], [three_2])
+            last_3, token = stack_up([token, swapped, stack_swapped], [three_3])
+            for item in (last_2, last_3):
+                pieces += [item, core_swap(item)]
 
             def weight_places(index, replica):
-                chip, core = index // 2, index % 2
-                places = [(index, 0), (index ^ 1, 0)]
-                for hops in range(1, chips):
-                    for whose in (index, index ^ 1):
-                        source = chip_before(chip, hops) * 2 + whose % 2
-                        places += [(source, item * geo.quarter) for item in neighbor_quarters(whose, replica)]
+                places = []
+                for hops in range(2):
+                    for other in range(2):
+                        places.append([(block_of(hops, other)(index), 0, geo.rows, 0)])
+                size = geo.quarter
+                for which in ((0, 2), (1, 2), (2, 2), (0, 3), (1, 3), (2, 3)), ((3, 2),), ((3, 3),):
+                    for other in range(2):
+                        quarters = neighbor_quarters(index ^ other, replica)
+                        places.append([
+                            (block_of(hops, other)(index), i * size, size, quarters[quarter] * size)
+                            for i, (quarter, hops) in enumerate(which)
+                        ])
                 return places
 
-            def outs_of(index):
-                chip, core = index // 2, index % 2
-                out = []
-                for hops in range(1, chips + 1):
-                    other = chip_before(chip, hops)
-                    out += [other * 2 + core, other * 2 + 1 - core]
-                return out
+            def grad_parts(index):
+                kept = [block_of(hops)(index) for hops in range(1, chips + 1)]
+                sent = [block_of(hops, 1)(index) for hops in range(1, chips + 1)]
+                return [([block], 0, geo.rows) for block in kept + sent]
 
         else:
-            weights = [lax.all_gather(block, "fsdp", axis=0)]
+            pieces = [lax.all_gather(block, "fsdp", axis=0)]
 
             def weight_places(index, replica):
-                return [(None, 0)]
-
-            outs_of = None
+                return [0]
+
+            def grad_parts(index):
+                return [(None, 0, geo.rows)]
 
         output, token_grad, *grads = model_step(
             geo,
@@ -727,32 +811,54 @@
             lengths,
             sinusoid,
             where,
-            weights,
+            pieces,
             weight_places,
-            outs_of,
+            grad_parts,
         )
 
-        if direct:
-            passed = []
-            for hops in range(chips):
-                keep, send = grads[2 * hops], grads[2 * hops + 1]
-                near, far = add_cores(geo, keep, core_swap(send), where)
-                own, other = add_pair(near, second_way(far))
-                quarter = add_all(own, first_way(other), *passed)
-                if hops < chips - 1:
-                    passed = [ring_hop(quarter)]
-            one = first_way(quarter)
-            pieces = [quarter, one, second_way(quarter), second_way(one)]
+        if direct_links:
+            grads = [item[0] for item in grads]
+            cores = [[grads[hops], core_swap(grads[chips + hops])] for hops in range(chips)]
+            near_1, far_1, tails, token = reduce_step(geo, where, [], cores=cores[0], head=geo.head)
+            far_1, tails = second_way(far_1), ring_hop(tails, -1)
+            near_2, far_2, token = reduce_step(geo, where, [token], cores=cores[1])
+            far_2 = second_way(far_2)
+            near_3, far_3, own_1, next_1, token = reduce_step(geo, where, [token], cores=cores[2], pair=[near_1, far_1])
+            next_1, far_3 = first_way(next_1), second_way(far_3)
+            quarter, token = reduce_step(geo, where, [token], items=[own_1, next_1])
+            passed = ring_hop(quarter)
+            near_4, far_4, own_2, next_2, token = reduce_step(
+                geo, where, [token], cores=cores[3], pair=[near_2, far_2], tails=tails
+            )
+            next_2, far_4 = first_way(next_2), second_way(far_4)
+            own_3, next_3, token = reduce_step(geo, where, [token], pair=[near_3, far_3])
+            next_3 = first_way(next_3)
+            quarter, token = reduce_step(geo, where, [token], items=[own_2, next_2, passed])
+            passed = ring_hop(quarter)
+            own_a, own_b, next_a, next_b, token = reduce_step(geo, where, [token], pair=[near_4, far_4], halves=True)
+            next_a, next_b = first_way(next_a), first_way(next_b)
+            passed_a, passed_b, token = reduce_step(geo, where, [token], items=[own_3, next_3, passed], halves=True)
+            passed_a, passed_b = ring_hop(passed_a), ring_hop(passed_b)
+            half_a, token = reduce_step(geo, where, [token], items=[own_a, next_a, passed_a])
+            one_a, two_a = first_way(half_a), second_way(half_a)
+            half_b, token = reduce_step(geo, where, [token], items=[own_b, next_b, passed_b])
+            one_b, two_b = first_way(half_b), second_way(half_b)
+            pieces = [half_a, half_b, one_a, one_b, two_a, two_b, second_way(one_a), second_way(one_b)]
 
             def piece_places(index, replica):
-                return [item * geo.quarter for item in neighbor_quarters(index, replica)]
+                half = geo.quarter // 2
+                return [
+                    (2 * i + j, 0, half, item * geo.quarter + j * half)
+                    for i, item in enumerate(neighbor_quarters(index, replica))
+                    for j in range(2)
+                ]
 
         else:
             mine = lax.psum_scatter(grads[0], "fsdp", scatter_dimension=0)
             pieces = [lax.psum(mine, "dp")]
 
             def piece_places(index, replica):
-                return [0]
+                return [(0, 0, geo.rows, 0)]
 
         new_params, new_one, new_two = optimizer_step(
             geo, params, moment_one, moment_two, where, pieces, piece_places

time: 261 us -> 220 us (0.84)
  waiting for transfers between devices: 133 us -> 110 us
  Pallas kernels: 71.6 us -> 54 us
    ppermute x20 -> x24, waiting for transfers between devices: 90.1 us -> 58.1 us  [permute(): return lax.ppermute(value, axes, pairs)]
    pallas_call x1, Pallas kernels: 18.2 us -> 7.8 us  [optimizer_step(): pl.pallas_call(kernel, grid=(steps,), in_specs=[pl.BlockSpec(memory_space...]
    ppermute x6 -> x8, waiting for transfers between devices: 38.5 us -> 46.8 us  [ring_hop(): return lax.ppermute(value, 'fsdp', pairs)]
    pallas_call x1, Pallas kernels: 10.8 us -> 3.14 us  [pack_block(): pl.pallas_call(kernel, grid=(steps,), in_specs=[pl.BlockSpec(memory_space...]
    pallas_call x12 -> x21, Pallas kernels: 5.69 us -> 11.7 us  [small_step(): pl.pallas_call(kernel, in_specs=[pl.BlockSpec(memory_space=pltpu.SMEM)] *...]
    pallas_call x1, Pallas kernels: 37 us -> 31.3 us  [model_step(): pl.pallas_call(kernel, in_specs=[pl.BlockSpec(memory_space=pltpu.SMEM)] *...]
    ppermute x20 -> x24, starting transfers between devices: 28.4 us -> 30.7 us  [permute(): return lax.ppermute(value, axes, pairs)]
    ppermute x6 -> x8, starting transfers between devices: 14.9 us -> 16.7 us  [ring_hop(): return lax.ppermute(value, 'fsdp', pairs)]
  transfers between devices with their start and end apart: 43 -> 41, of which waited for: 18 -> 23; matrix products, arithmetic and copies ran while one was open for 0% -> 0% of each run, Pallas kernels for 2% -> 5%
where the time goes in v3:
time: 220 us; the launch traced here: 219 us
  waiting for transfers between devices  110 us (50%)
  Pallas kernels  54 us (25%)
  starting transfers between devices  49.5 us (22%)
  local copies, waits for them, and re-layouts  4.42 us (2%)
    ppermute x24, waiting for transfers between devices, permute(): return lax.ppermute(value, axes, pairs)  58.1 us
    ppermute x8, waiting for transfers between devices, ring_hop(): return lax.ppermute(value, 'fsdp', pairs)  46.8 us
    pallas_call x1, Pallas kernels, model_step(): pl.pallas_call(kernel, in_specs=[pl.BlockSpec(memory_space=pltpu.SMEM)] *...  31.3 us
    ppermute x24, starting transfers between devices, permute(): return lax.ppermute(value, axes, pairs)  30.7 us
    ppermute x8, starting transfers between devices, ring_hop(): return lax.ppermute(value, 'fsdp', pairs)  16.7 us
    pallas_call x21, Pallas kernels, small_step(): pl.pallas_call(kernel, in_specs=[pl.BlockSpec(memory_space=pltpu.SMEM)] *...  11.7 us
    pallas_call x1, Pallas kernels, optimizer_step(): pl.pallas_call(kernel, grid=(steps,), in_specs=[pl.BlockSpec(memory_space...  7.8 us
    ppermute x9, waiting for transfers between devices, core_swap(): lax.ppermute(value, 'fsdp', [(index, index ^ 1) for index in range(fsdp)])  4.73 us
  transfers between devices with their start and end apart: 41, of which 23 were waited for; matrix products, arithmetic and copies ran while one was open for 0% of the time, Pallas kernels for 5%

profile of v3, /device:TPU:0, one launch (start us, length us, event | category | flops | bytes accessed | tf_op | source)
XLA Modules:
  0.0 218.7 jit_solution(397510933752348831)
XLA Ops:
  0.7 2.1 copy-done
  3.5 3.1 %pack_block.1 = (bf16[7936,128]{1,0:T(8,128)(2,1)S(1)}, bf16[1984,128]{1,0:T(8,128)(2,1)S(1)}) custom-call(s32[2]{0:T(128)S(1)} %pad_add_fusion.where_ref.refs_0_, s32[168]{0:T(256)S(1)} %copy-done.11, f32[943392]{0:T(1024)S(1)} %copy-done), custom_call_target="tpu_custom_call" | custom-call | tf_op jit(solution)/shard_map/pack_block/pallas_call | solution.py:186
  7.0 2.8 %collective-permute-start.1 = (bf16[1984,128]{1,0:T(8,128)(2,1)S(1)}, bf16[1984,128]{1,0:T(8,128)(2,1)S(1)}, u32[]{:S(2)}, u32[]{:S(2)}) collective-permute-start(bf16[1984,128]{1,0:T(8,128)(2,1)S(1)} %get-tuple-element.75), channel_id=1, source_target_pairs={{0,2},{1,3},{2,6},{3,7},{6,4},{7,5},{4,0},{5,1},{8,10},{9,11},{10,... | collective-permute-start | bytes 1523720 | tf_op jit(solution)/shard_map/ppermute | solution.py:728
  9.8 13.1 %collective-permute-done.1.refs_0_ = bf16[1984,128]{1,0:T(8,128)(2,1)S(1)} collective-permute-done((bf16[1984,128]{1,0:T(8,128)(2,1)S(1)}, bf16[1984,128]{1,0:T(8,128)(2,1)S(1)}, u32[]{:S(2)}, u32[]{:S(2)}) %collective-permute-start.1) | collective-permute-done | bytes 507936 | tf_op jit(solution)/shard_map/ppermute | solution.py:728
  24.0 1.5 collective-permute-start.3
  25.5 1.5 collective-permute-start.2
  27.0 10.2 %collective-permute-done.4.refs_0_ = bf16[1984,128]{1,0:T(8,128)(2,1)S(1)} collective-permute-done((bf16[1984,128]{1,0:T(8,128)(2,1)S(1)}, bf16[1984,128]{1,0:T(8,128)(2,1)S(1)}, u32[]{:S(2)}, u32[]{:S(2)}) %collective-permute-start.4) | collective-permute-done | bytes 507936 | tf_op jit(solution)/shard_map/ppermute | solution.py:728
  38.1 1.5 collective-permute-start.8
  39.6 1.5 collective-permute-start.6
  41.7 8.9 %collective-permute-done.7.refs_0_ = bf16[1984,128]{1,0:T(8,128)(2,1)S(1)} collective-permute-done((bf16[1984,128]{1,0:T(8,128)(2,1)S(1)}, bf16[1984,128]{1,0:T(8,128)(2,1)S(1)}, u32[]{:S(2)}, u32[]{:S(2)}) %collective-permute-start.7) | collective-permute-done | bytes 507936 | tf_op jit(solution)/shard_map/ppermute | solution.py:728
  50.7 1.3 collective-permute-start.11
  52.0 1.5 collective-permute-start.10
  54.2 7.1 %collective-permute-done.5.refs_4_ = bf16[1984,128]{1,0:T(8,128)(2,1)S(1)} collective-permute-done((bf16[1984,128]{1,0:T(8,128)(2,1)S(1)}, bf16[1984,128]{1,0:T(8,128)(2,1)S(1)}, u32[]{:S(2)}, u32[]{:S(2)}) %collective-permute-start.5) | collective-permute-done | bytes 507936 | tf_op jit(solution)/shard_map/ppermute | solution.py:718
  61.9 5.7 %collective-permute-done.11.refs_2_.refs_5_ = bf16[1984,128]{1,0:T(8,128)(2,1)S(1)} collective-permute-done((bf16[1984,128]{1,0:T(8,128)(2,1)S(1)}, bf16[1984,128]{1,0:T(8,128)(2,1)S(1)}, u32[]{:S(2)}, u32[]{:S(2)}) %collective-permute-start.11) | collective-permute-done | bytes 507936 | tf_op jit(solution)/shard_map/ppermute | solution.py:718
  68.4 1.5 collective-permute-start.13
  70.5 7.0 %collective-permute-done.13.refs_0_ = bf16[1984,128]{1,0:T(8,128)(2,1)S(1)} collective-permute-done((bf16[1984,128]{1,0:T(8,128)(2,1)S(1)}, bf16[1984,128]{1,0:T(8,128)(2,1)S(1)}, u32[]{:S(2)}, u32[]{:S(2)}) %collective-permute-start.13) | collective-permute-done | bytes 507936 | tf_op jit(solution)/shard_map/ppermute | solution.py:718
  77.6 5.3 %collective-permute-done.15.refs_0_ = bf16[1984,128]{1,0:T(8,128)(2,1)S(1)} collective-permute-done((bf16[1984,128]{1,0:T(8,128)(2,1)S(1)}, bf16[1984,128]{1,0:T(8,128)(2,1)S(1)}, u32[]{:S(2)}, u32[]{:S(2)}) %collective-permute-start.15) | collective-permute-done | bytes 507936 | tf_op jit(solution)/shard_map/ppermute | solution.py:718
  85.4 1.7 collective-permute-done.16.refs_9_
  87.1 31.3 %model_step.1 = (bf16[256,768]{1,0:T(8,128)(2,1)}, f32[256,768]{1,0:T(8,128)}, bf16[1,7936,128]{2,1,0:T(8,128)(2,1)S(1)}, bf16[1,7936,128]{2,1,0:T(8,128)(2,1)S(...) custom-call(s32[2]{0:T(128)S(1)} %pad_add_fusion.where_ref.refs_0_, ...), custom_call_target="tpu_custom_call" | custom-call | tf_op jit(solution)/shard_map/model_step/pallas_call | solution.py:552
  119.5 3.0 %collective-permute-done.18.refs_2_ = bf16[7936,128]{1,0:T(8,128)(2,1)S(1)} collective-permute-done((bf16[7936,128]{1,0:T(8,128)(2,1)S(1)}, bf16[7936,128]{1,0:T(8,128)(2,1)S(1)}, u32[]{:S(2)}, u32[]{:S(2)}) %collective-permute-start.18) | collective-permute-done | bytes 2031648 | tf_op jit(solution)/shard_map/ppermute | solution.py:721
  123.6 1.5 collective-permute-start.23
  125.1 2.1 collective-permute-start.19
  128.8 3.8 %collective-permute-done.23.refs_4_ = bf16[2,992,128]{2,1,0:T(8,128)(2,1)S(1)} collective-permute-done((bf16[2,992,128]{2,1,0:T(8,128)(2,1)S(1)}, bf16[2,992,128]{2,1,0:T(8,128)(2,1)S(1)}, u32[]{:S(2)}, u32[]{:S(2)}) %collective-permute-start.23) | collective-permute-done | bytes 507936 | tf_op jit(solution)/shard_map/ppermute | solution.py:718
  133.9 1.5 collective-permute-start.28
  136.0 8.5 %collective-permute-done.24.refs_2_ = bf16[992,128]{1,0:T(8,128)(2,1)S(1)} collective-permute-done((bf16[992,128]{1,0:T(8,128)(2,1)S(1)}, bf16[992,128]{1,0:T(8,128)(2,1)S(1)}, u32[]{:S(2)}, u32[]{:S(2)}) %collective-permute-start.24) | collective-permute-done | bytes 253984 | tf_op jit(solution)/shard_map/ppermute | solution.py:718
  145.1 5.2 %collective-permute-done.19.refs_3_ = bf16[3968,128]{1,0:T(8,128)(2,1)S(1)} collective-permute-done((bf16[3968,128]{1,0:T(8,128)(2,1)S(1)}, bf16[3968,128]{1,0:T(8,128)(2,1)S(1)}, u32[]{:S(2)}, u32[]{:S(2)}) %collective-permute-start.19) | collective-permute-done | bytes 1015840 | tf_op jit(solution)/shard_map/ppermute | solution.py:728
  150.3 1.4 reduce_step.15
  151.8 1.6 collective-permute-start.26
  154.2 3.2 %collective-permute-start.27 = (bf16[992,128]{1,0:T(8,128)(2,1)S(1)}, bf16[992,128]{1,0:T(8,128)(2,1)S(1)}, u32[]{:S(2)}, u32[]{:S(2)}) collective-permute-start(bf16[992,128]{1,0:T(8,128)(2,1)S(1)} %get-tuple-element.120), channel_id=1, source_target_pairs={{0,2},{1,3},{2,6},{3,7},{6,4},{7,5},{4,0},{5,1},{8,10},{9,11},{10,... | collective-permute-start | bytes 761864 | tf_op jit(solution)/shard_map/ppermute | solution.py:728
  157.4 3.1 %collective-permute-done.28.refs_2_ = bf16[2,1984,128]{2,1,0:T(8,128)(2,1)S(1)} collective-permute-done((bf16[2,1984,128]{2,1,0:T(8,128)(2,1)S(1)}, bf16[2,1984,128]{2,1,0:T(8,128)(2,1)S(1)}, u32[]{:S(2)}, u32[]{:S(2)}) %collective-permute-start.28) | collective-permute-done | bytes 1015840 | tf_op jit(solution)/shard_map/ppermute | solution.py:718
  161.3 1.7 collective-permute-done.27.refs_3_
  163.1 3.3 %collective-permute-done.26.refs_2_ = bf16[1984,128]{1,0:T(8,128)(2,1)S(1)} collective-permute-done((bf16[1984,128]{1,0:T(8,128)(2,1)S(1)}, bf16[1984,128]{1,0:T(8,128)(2,1)S(1)}, u32[]{:S(2)}, u32[]{:S(2)}) %collective-permute-start.26) | collective-permute-done | bytes 507936 | tf_op jit(solution)/shard_map/ppermute | solution.py:718
  167.0 2.7 %collective-permute-start.31 = (bf16[1984,128]{1,0:T(8,128)(2,1)S(1)}, bf16[1984,128]{1,0:T(8,128)(2,1)S(1)}, u32[]{:S(2)}, u32[]{:S(2)}) collective-permute-start(bf16[1984,128]{1,0:T(8,128)(2,1)S(1)} %get-tuple-element.130), channel_id=1, source_target_pairs={{0,2},{1,3},{2,6},{3,7},{6,4},{7,5},{4,0},{5,1},{8,10},{9,11},{10,... | collective-permute-start | bytes 1523720 | tf_op jit(solution)/shard_map/ppermute | solution.py:728
  169.7 1.5 collective-permute-start.30
  171.2 5.5 %collective-permute-done.25.refs_2_ = bf16[2,1984,128]{2,1,0:T(8,128)(2,1)S(1)} collective-permute-done((bf16[2,1984,128]{2,1,0:T(8,128)(2,1)S(1)}, bf16[2,1984,128]{2,1,0:T(8,128)(2,1)S(1)}, u32[]{:S(2)}, u32[]{:S(2)}) %collective-permute-start.25) | collective-permute-done | bytes 1015840 | tf_op jit(solution)/shard_map/ppermute | solution.py:718
  177.6 2.3 %collective-permute-done.31.refs_3_ = bf16[1984,128]{1,0:T(8,128)(2,1)S(1)} collective-permute-done((bf16[1984,128]{1,0:T(8,128)(2,1)S(1)}, bf16[1984,128]{1,0:T(8,128)(2,1)S(1)}, u32[]{:S(2)}, u32[]{:S(2)}) %collective-permute-start.31) | collective-permute-done | bytes 507936 | tf_op jit(solution)/shard_map/ppermute | solution.py:728
  180.6 3.5 %collective-permute-start.32 = (bf16[992,128]{1,0:T(8,128)(2,1)S(1)}, bf16[992,128]{1,0:T(8,128)(2,1)S(1)}, u32[]{:S(2)}, u32[]{:S(2)}) collective-permute-start(bf16[992,128]{1,0:T(8,128)(2,1)S(1)} %get-tuple-element.132), channel_id=1, source_target_pairs={{0,2},{1,3},{2,6},{3,7},{6,4},{7,5},{4,0},{5,1},{8,10},{9,11},{10,... | collective-permute-start | bytes 761864 | tf_op jit(solution)/shard_map/ppermute | solution.py:728
  184.2 2.0 collective-permute-start.33
  186.7 4.0 %collective-permute-done.32.refs_3_ = bf16[992,128]{1,0:T(8,128)(2,1)S(1)} collective-permute-done((bf16[992,128]{1,0:T(8,128)(2,1)S(1)}, bf16[992,128]{1,0:T(8,128)(2,1)S(1)}, u32[]{:S(2)}, u32[]{:S(2)}) %collective-permute-start.32) | collective-permute-done | bytes 253984 | tf_op jit(solution)/shard_map/ppermute | solution.py:728
  191.3 1.6 collective-permute-start.35
  192.9 1.3 collective-permute-done.34.refs_3_
  196.3 2.2 collective-permute-start.37
  198.5 2.4 %collective-permute-start.39 = (bf16[992,128]{1,0:T(8,128)(2,1)S(1)}, bf16[992,128]{1,0:T(8,128)(2,1)S(1)}, u32[]{:S(2)}, u32[]{:S(2)}) collective-permute-start(bf16[992,128]{1,0:T(8,128)(2,1)S(1)} %collective-permute-done.35.refs_2_), channel_id=1, source_target_pairs={{0,16},{1,9},{2,18},{3,11},{4,20},{5,13},{6,22},{7,15},{8,24},{9,1... | collective-permute-start | bytes 761864 | tf_op jit(solution)/shard_map/ppermute | solution.py:718
  200.9 3.6 %collective-permute-done.36.refs_3_ = bf16[992,128]{1,0:T(8,128)(2,1)S(1)} collective-permute-done((bf16[992,128]{1,0:T(8,128)(2,1)S(1)}, bf16[992,128]{1,0:T(8,128)(2,1)S(1)}, u32[]{:S(2)}, u32[]{:S(2)}) %collective-permute-start.36) | collective-permute-done | bytes 253984 | tf_op jit(solution)/shard_map/ppermute | solution.py:718
  204.4 1.9 collective-permute-start.40
  206.3 1.8 collective-permute-done.39.refs_6_
  208.1 2.7 %collective-permute-done.40.refs_7_ = bf16[992,128]{1,0:T(8,128)(2,1)S(1)} collective-permute-done((bf16[992,128]{1,0:T(8,128)(2,1)S(1)}, bf16[992,128]{1,0:T(8,128)(2,1)S(1)}, u32[]{:S(2)}, u32[]{:S(2)}) %collective-permute-start.40) | collective-permute-done | bytes 253984 | tf_op jit(solution)/shard_map/ppermute | solution.py:718
  210.9 7.8 %optimizer_step.1 = (f32[943392]{0:T(1024)}, f32[943392]{0:T(1024)}, f32[943392]{0:T(1024)}) custom-call(s32[2]{0:T(128)S(1)} %pad_add_fusion.where_ref.refs_0_, s32[168]{0:T(256)S(1)} %copy-done.12, bf16[992,128]{1,0:T(8,128)(2,1)S(1)} %get-tuple-element.134.refs_0_, bf16[992,128]{1,0:T(8,128)(2,1)S(1)} %get-tuple-element.139.refs_1_, ...), custom_call_target="tpu_custom_call" | custom-call | tf_op jit(solution)/shard_map/optimizer_step/pallas_call | solution.py:254
  (93 shorter events, 22.3 us)
Async XLA Ops:
  6.6 30.6 %collective-permute-start = (bf16[7936,128]{1,0:T(8,128)(2,1)S(1)}, bf16[7936,128]{1,0:T(8,128)(2,1)S(1)}, u32[]{:S(2)}, u32[]{:S(2)}) collective-permute-start(bf16[7936,128]{1,0:T(8,128)(2,1)S(1)} %get-tuple-element.74.refs_0_), channel_id=1, source_target_pairs={{0,1},{1,0},{2,3},{3,2},{4,5},{5,4},{6,7},{7,6},{8,9},{9,8},{10,11... | collective-permute-start | bytes 6094856 | tf_op jit(solution)/shard_map/ppermute | solution.py:721
  7.0 15.9 %collective-permute-start.1 = (bf16[1984,128]{1,0:T(8,128)(2,1)S(1)}, bf16[1984,128]{1,0:T(8,128)(2,1)S(1)}, u32[]{:S(2)}, u32[]{:S(2)}) collective-permute-start(bf16[1984,128]{1,0:T(8,128)(2,1)S(1)} %get-tuple-element.75), channel_id=1, source_target_pairs={{0,2},{1,3},{2,6},{3,7},{6,4},{7,5},{4,0},{5,1},{8,10},{9,11},{10,... | collective-permute-start | bytes 1523720 | tf_op jit(solution)/shard_map/ppermute | solution.py:728
  22.9 14.3 %collective-permute-start.4 = (bf16[1984,128]{1,0:T(8,128)(2,1)S(1)}, bf16[1984,128]{1,0:T(8,128)(2,1)S(1)}, u32[]{:S(2)}, u32[]{:S(2)}) collective-permute-start(bf16[1984,128]{1,0:T(8,128)(2,1)S(1)} %get-tuple-element.76.refs_1_), channel_id=1, source_target_pairs={{0,2},{1,3},{2,6},{3,7},{6,4},{7,5},{4,0},{5,1},{8,10},{9,11},{10,... | collective-permute-start | bytes 1523720 | tf_op jit(solution)/shard_map/ppermute | solution.py:728
  24.0 17.1 %collective-permute-start.3 = (bf16[1984,128]{1,0:T(8,128)(2,1)S(1)}, bf16[1984,128]{1,0:T(8,128)(2,1)S(1)}, u32[]{:S(2)}, u32[]{:S(2)}) collective-permute-start(bf16[1984,128]{1,0:T(8,128)(2,1)S(1)} %get-tuple-element.76.refs_1_), channel_id=1, source_target_pairs={{0,16},{1,9},{2,18},{3,11},{4,20},{5,13},{6,22},{7,15},{8,24},{9,1... | collective-permute-start | bytes 1523720 | tf_op jit(solution)/shard_map/ppermute | solution.py:718
  25.5 15.6 %collective-permute-start.2 = (bf16[1984,128]{1,0:T(8,128)(2,1)S(1)}, bf16[1984,128]{1,0:T(8,128)(2,1)S(1)}, u32[]{:S(2)}, u32[]{:S(2)}) collective-permute-start(bf16[1984,128]{1,0:T(8,128)(2,1)S(1)} %get-tuple-element.76.refs_1_), channel_id=1, source_target_pairs={{0,8},{1,17},{2,10},{3,19},{4,12},{5,21},{6,14},{7,23},{8,0},{9,25... | collective-permute-start | bytes 1523720 | tf_op jit(solution)/shard_map/ppermute | solution.py:718
  37.2 13.5 %copy-start.3 = (bf16[7936,128]{1,0:T(8,128)(2,1)}, bf16[7936,128]{1,0:T(8,128)(2,1)S(1)}, u32[]{:S(2)}) copy-start(bf16[7936,128]{1,0:T(8,128)(2,1)S(1)} %collective-permute-done.refs_2_.refs_1_) | copy-start | bytes 6094852
  37.2 13.4 %collective-permute-start.7 = (bf16[1984,128]{1,0:T(8,128)(2,1)S(1)}, bf16[1984,128]{1,0:T(8,128)(2,1)S(1)}, u32[]{:S(2)}, u32[]{:S(2)}) collective-permute-start(bf16[1984,128]{1,0:T(8,128)(2,1)S(1)} %get-tuple-element.80.refs_0_), channel_id=1, source_target_pairs={{0,2},{1,3},{2,6},{3,7},{6,4},{7,5},{4,0},{5,1},{8,10},{9,11},{10,... | collective-permute-start | bytes 1523720 | tf_op jit(solution)/shard_map/ppermute | solution.py:728
  38.1 15.4 %collective-permute-start.8 = (bf16[1984,128]{1,0:T(8,128)(2,1)S(1)}, bf16[1984,128]{1,0:T(8,128)(2,1)S(1)}, u32[]{:S(2)}, u32[]{:S(2)}) collective-permute-start(bf16[1984,128]{1,0:T(8,128)(2,1)S(1)} %get-tuple-element.80.refs_0_), channel_id=1, source_target_pairs={{0,16},{1,9},{2,18},{3,11},{4,20},{5,13},{6,22},{7,15},{8,24},{9,1... | collective-permute-start | bytes 1523720 | tf_op jit(solution)/shard_map/ppermute | solution.py:718
  39.6 14.5 %collective-permute-start.6 = (bf16[1984,128]{1,0:T(8,128)(2,1)S(1)}, bf16[1984,128]{1,0:T(8,128)(2,1)S(1)}, u32[]{:S(2)}, u32[]{:S(2)}) collective-permute-start(bf16[1984,128]{1,0:T(8,128)(2,1)S(1)} %get-tuple-element.80.refs_0_), channel_id=1, source_target_pairs={{0,8},{1,17},{2,10},{3,19},{4,12},{5,21},{6,14},{7,23},{8,0},{9,25... | collective-permute-start | bytes 1523720 | tf_op jit(solution)/shard_map/ppermute | solution.py:718
  41.2 20.1 %collective-permute-start.5 = (bf16[1984,128]{1,0:T(8,128)(2,1)S(1)}, bf16[1984,128]{1,0:T(8,128)(2,1)S(1)}, u32[]{:S(2)}, u32[]{:S(2)}) collective-permute-start(bf16[1984,128]{1,0:T(8,128)(2,1)S(1)} %get-tuple-element.79), channel_id=1, source_target_pairs={{0,16},{1,9},{2,18},{3,11},{4,20},{5,13},{6,22},{7,15},{8,24},{9,1... | collective-permute-start | bytes 1523720 | tf_op jit(solution)/shard_map/ppermute | solution.py:718
  50.7 16.9 %collective-permute-start.11 = (bf16[1984,128]{1,0:T(8,128)(2,1)S(1)}, bf16[1984,128]{1,0:T(8,128)(2,1)S(1)}, u32[]{:S(2)}, u32[]{:S(2)}) collective-permute-start(bf16[1984,128]{1,0:T(8,128)(2,1)S(1)} %get-tuple-element.85.refs_3_), channel_id=1, source_target_pairs={{0,16},{1,9},{2,18},{3,11},{4,20},{5,13},{6,22},{7,15},{8,24},{9,1... | collective-permute-start | bytes 1523720 | tf_op jit(solution)/shard_map/ppermute | solution.py:718
  52.0 15.6 %collective-permute-start.10 = (bf16[1984,128]{1,0:T(8,128)(2,1)S(1)}, bf16[1984,128]{1,0:T(8,128)(2,1)S(1)}, u32[]{:S(2)}, u32[]{:S(2)}) collective-permute-start(bf16[1984,128]{1,0:T(8,128)(2,1)S(1)} %get-tuple-element.85.refs_3_), channel_id=1, source_target_pairs={{0,8},{1,17},{2,10},{3,19},{4,12},{5,21},{6,14},{7,23},{8,0},{9,25... | collective-permute-start | bytes 1523720 | tf_op jit(solution)/shard_map/ppermute | solution.py:718
  61.9 6.0 %copy-start.8 = (bf16[7936,128]{1,0:T(8,128)(2,1)}, bf16[7936,128]{1,0:T(8,128)(2,1)S(1)}, u32[]{:S(2)}) copy-start(bf16[7936,128]{1,0:T(8,128)(2,1)S(1)} %get-tuple-element.84.refs_2_) | copy-start | bytes 6094852
  67.9 19.2 %copy-start.7 = (bf16[11904,128]{1,0:T(8,128)(2,1)}, bf16[11904,128]{1,0:T(8,128)(2,1)S(1)}, u32[]{:S(2)}) copy-start(bf16[11904,128]{1,0:T(8,128)(2,1)S(1)} %get-tuple-element.88.refs_4_) | copy-start | bytes 9142276
  67.9 15.0 %collective-permute-start.12 = (bf16[11904,128]{1,0:T(8,128)(2,1)S(1)}, bf16[11904,128]{1,0:T(8,128)(2,1)S(1)}, u32[]{:S(2)}, u32[]{:S(2)}) collective-permute-start(bf16[11904,128]{1,0:T(8,128)(2,1)S(1)} %get-tuple-element.88.refs_4_), channel_id=1, source_target_pairs={{0,1},{1,0},{2,3},{3,2},{4,5},{5,4},{6,7},{7,6},{8,9},{9,8},{10,11... | collective-permute-start | bytes 9142280 | tf_op jit(solution)/shard_map/ppermute | solution.py:721
  68.0 14.9 %collective-permute-start.9 = (bf16[7936,128]{1,0:T(8,128)(2,1)S(1)}, bf16[7936,128]{1,0:T(8,128)(2,1)S(1)}, u32[]{:S(2)}, u32[]{:S(2)}) collective-permute-start(bf16[7936,128]{1,0:T(8,128)(2,1)S(1)} %get-tuple-element.84.refs_2_), channel_id=1, source_target_pairs={{0,1},{1,0},{2,3},{3,2},{4,5},{5,4},{6,7},{7,6},{8,9},{9,8},{10,11... | collective-permute-start | bytes 6094856 | tf_op jit(solution)/shard_map/ppermute | solution.py:721
  68.4 9.0 %collective-permute-start.13 = (bf16[1984,128]{1,0:T(8,128)(2,1)S(1)}, bf16[1984,128]{1,0:T(8,128)(2,1)S(1)}, u32[]{:S(2)}, u32[]{:S(2)}) collective-permute-start(bf16[1984,128]{1,0:T(8,128)(2,1)S(1)} %get-tuple-element.89), channel_id=1, source_target_pairs={{0,16},{1,9},{2,18},{3,11},{4,20},{5,13},{6,22},{7,15},{8,24},{9,1... | collective-permute-start | bytes 1523720 | tf_op jit(solution)/shard_map/ppermute | solution.py:718
  70.0 12.9 %collective-permute-start.15 = (bf16[1984,128]{1,0:T(8,128)(2,1)S(1)}, bf16[1984,128]{1,0:T(8,128)(2,1)S(1)}, u32[]{:S(2)}, u32[]{:S(2)}) collective-permute-start(bf16[1984,128]{1,0:T(8,128)(2,1)S(1)} %get-tuple-element.92), channel_id=1, source_target_pairs={{0,16},{1,9},{2,18},{3,11},{4,20},{5,13},{6,22},{7,15},{8,24},{9,1... | collective-permute-start | bytes 1523720 | tf_op jit(solution)/shard_map/ppermute | solution.py:718
  77.5 7.9 %collective-permute-start.14 = (bf16[1984,128]{1,0:T(8,128)(2,1)S(1)}, bf16[1984,128]{1,0:T(8,128)(2,1)S(1)}, u32[]{:S(2)}, u32[]{:S(2)}) collective-permute-start(bf16[1984,128]{1,0:T(8,128)(2,1)S(1)} %get-tuple-element.91.refs_6_), channel_id=1, source_target_pairs={{0,1},{1,0},{2,3},{3,2},{4,5},{5,4},{6,7},{7,6},{8,9},{9,8},{10,11... | collective-permute-start | bytes 1523720 | tf_op jit(solution)/shard_map/ppermute | solution.py:721
  85.2 1.9 collective-permute-start.16
  118.5 4.1 %collective-permute-start.18 = (bf16[7936,128]{1,0:T(8,128)(2,1)S(1)}, bf16[7936,128]{1,0:T(8,128)(2,1)S(1)}, u32[]{:S(2)}, u32[]{:S(2)}) collective-permute-start(bf16[7936,128]{1,0:T(8,128)(2,1)S(1)} %bitcast.23), channel_id=1, source_target_pairs={{0,1},{1,0},{2,3},{3,2},{4,5},{5,4},{6,7},{7,6},{8,9},{9,8},{10,11... | collective-permute-start | bytes 6094856 | tf_op jit(solution)/shard_map/ppermute | solution.py:721
  118.6 8.6 %collective-permute-start.20 = (bf16[7936,128]{1,0:T(8,128)(2,1)S(1)}, bf16[7936,128]{1,0:T(8,128)(2,1)S(1)}, u32[]{:S(2)}, u32[]{:S(2)}) collective-permute-start(bf16[7936,128]{1,0:T(8,128)(2,1)S(1)} %bitcast.22), channel_id=1, source_target_pairs={{0,1},{1,0},{2,3},{3,2},{4,5},{5,4},{6,7},{7,6},{8,9},{9,8},{10,11... | collective-permute-start | bytes 6094856 | tf_op jit(solution)/shard_map/ppermute | solution.py:721
  119.0 9.8 %collective-permute-start.22 = (bf16[7936,128]{1,0:T(8,128)(2,1)S(1)}, bf16[7936,128]{1,0:T(8,128)(2,1)S(1)}, u32[]{:S(2)}, u32[]{:S(2)}) collective-permute-start(bf16[7936,128]{1,0:T(8,128)(2,1)S(1)} %bitcast.21), channel_id=1, source_target_pairs={{0,1},{1,0},{2,3},{3,2},{4,5},{5,4},{6,7},{7,6},{8,9},{9,8},{10,11... | collective-permute-start | bytes 6094856 | tf_op jit(solution)/shard_map/ppermute | solution.py:721
  119.1 26.0 %collective-permute-start.17 = (bf16[7936,128]{1,0:T(8,128)(2,1)S(1)}, bf16[7936,128]{1,0:T(8,128)(2,1)S(1)}, u32[]{:S(2)}, u32[]{:S(2)}) collective-permute-start(bf16[7936,128]{1,0:T(8,128)(2,1)S(1)} %bitcast.20), channel_id=1, source_target_pairs={{0,1},{1,0},{2,3},{3,2},{4,5},{5,4},{6,7},{7,6},{8,9},{9,8},{10,11... | collective-permute-start | bytes 6094856 | tf_op jit(solution)/shard_map/ppermute | solution.py:721
  123.6 9.1 %collective-permute-start.23 = (bf16[2,992,128]{2,1,0:T(8,128)(2,1)S(1)}, bf16[2,992,128]{2,1,0:T(8,128)(2,1)S(1)}, u32[]{:S(2)}, u32[]{:S(2)}) collective-permute-start(bf16[2,992,128]{2,1,0:T(8,128)(2,1)S(1)} %get-tuple-element.110), channel_id=1, source_target_pairs={{0,16},{1,9},{2,18},{3,11},{4,20},{5,13},{6,22},{7,15},{8,24},{9,1... | collective-permute-start | bytes 1523720 | tf_op jit(solution)/shard_map/ppermute | solution.py:718
  125.1 25.2 %collective-permute-start.19 = (bf16[3968,128]{1,0:T(8,128)(2,1)S(1)}, bf16[3968,128]{1,0:T(8,128)(2,1)S(1)}, u32[]{:S(2)}, u32[]{:S(2)}) collective-permute-start(bf16[3968,128]{1,0:T(8,128)(2,1)S(1)} %get-tuple-element.101), channel_id=1, source_target_pairs={{0,4},{1,5},{2,0},{3,1},{6,2},{7,3},{4,6},{5,7},{8,12},{9,13},{10,... | collective-permute-start | bytes 3047432 | tf_op jit(solution)/shard_map/ppermute | solution.py:728
  128.2 22.1 %collective-permute-start.21 = (bf16[2,1984,128]{2,1,0:T(8,128)(2,1)S(1)}, bf16[2,1984,128]{2,1,0:T(8,128)(2,1)S(1)}, u32[]{:S(2)}, u32[]{:S(2)}) collective-permute-start(bf16[2,1984,128]{2,1,0:T(8,128)(2,1)S(1)} %get-tuple-element.106), channel_id=1, source_target_pairs={{0,16},{1,9},{2,18},{3,11},{4,20},{5,13},{6,22},{7,15},{8,24},{9,1... | collective-permute-start | bytes 3047432 | tf_op jit(solution)/shard_map/ppermute | solution.py:718
  133.9 26.7 %collective-permute-start.28 = (bf16[2,1984,128]{2,1,0:T(8,128)(2,1)S(1)}, bf16[2,1984,128]{2,1,0:T(8,128)(2,1)S(1)}, u32[]{:S(2)}, u32[]{:S(2)}) collective-permute-start(bf16[2,1984,128]{2,1,0:T(8,128)(2,1)S(1)} %get-tuple-element.122), channel_id=1, source_target_pairs={{0,16},{1,9},{2,18},{3,11},{4,20},{5,13},{6,22},{7,15},{8,24},{9,1... | collective-permute-start | bytes 3047432 | tf_op jit(solution)/shard_map/ppermute | solution.py:718
  135.4 9.1 %collective-permute-start.24 = (bf16[992,128]{1,0:T(8,128)(2,1)S(1)}, bf16[992,128]{1,0:T(8,128)(2,1)S(1)}, u32[]{:S(2)}, u32[]{:S(2)}) collective-permute-start(bf16[992,128]{1,0:T(8,128)(2,1)S(1)} %get-tuple-element.113), channel_id=1, source_target_pairs={{0,8},{1,17},{2,10},{3,19},{4,12},{5,21},{6,14},{7,23},{8,0},{9,25... | collective-permute-start | bytes 761864 | tf_op jit(solution)/shard_map/ppermute | solution.py:718
  150.3 60.5 %copy-start.6 = (f32[943392]{0:T(1024)S(1)}, f32[943392]{0:T(1024)}, u32[]{:S(2)}) copy-start(f32[943392]{0:T(1024)} %refs_10_.1) | copy-start | bytes 11320708
  151.8 14.6 %collective-permute-start.26 = (bf16[1984,128]{1,0:T(8,128)(2,1)S(1)}, bf16[1984,128]{1,0:T(8,128)(2,1)S(1)}, u32[]{:S(2)}, u32[]{:S(2)}) collective-permute-start(bf16[1984,128]{1,0:T(8,128)(2,1)S(1)} %get-tuple-element.119), channel_id=1, source_target_pairs={{0,8},{1,17},{2,10},{3,19},{4,12},{5,21},{6,14},{7,23},{8,0},{9,25... | collective-permute-start | bytes 1523720 | tf_op jit(solution)/shard_map/ppermute | solution.py:718
  153.3 23.4 %collective-permute-start.25 = (bf16[2,1984,128]{2,1,0:T(8,128)(2,1)S(1)}, bf16[2,1984,128]{2,1,0:T(8,128)(2,1)S(1)}, u32[]{:S(2)}, u32[]{:S(2)}) collective-permute-start(bf16[2,1984,128]{2,1,0:T(8,128)(2,1)S(1)} %get-tuple-element.117), channel_id=1, source_target_pairs={{0,16},{1,9},{2,18},{3,11},{4,20},{5,13},{6,22},{7,15},{8,24},{9,1... | collective-permute-start | bytes 3047432 | tf_op jit(solution)/shard_map/ppermute | solution.py:718
  154.2 8.8 %collective-permute-start.27 = (bf16[992,128]{1,0:T(8,128)(2,1)S(1)}, bf16[992,128]{1,0:T(8,128)(2,1)S(1)}, u32[]{:S(2)}, u32[]{:S(2)}) collective-permute-start(bf16[992,128]{1,0:T(8,128)(2,1)S(1)} %get-tuple-element.120), channel_id=1, source_target_pairs={{0,2},{1,3},{2,6},{3,7},{6,4},{7,5},{4,0},{5,1},{8,10},{9,11},{10,... | collective-permute-start | bytes 761864 | tf_op jit(solution)/shard_map/ppermute | solution.py:728
  160.6 50.3 %copy-start.5 = (f32[943392]{0:T(1024)S(1)}, f32[943392]{0:T(1024)}, u32[]{:S(2)}) copy-start(f32[943392]{0:T(1024)} %refs_9_.1) | copy-start | bytes 11320708
  167.0 12.9 %collective-permute-start.31 = (bf16[1984,128]{1,0:T(8,128)(2,1)S(1)}, bf16[1984,128]{1,0:T(8,128)(2,1)S(1)}, u32[]{:S(2)}, u32[]{:S(2)}) collective-permute-start(bf16[1984,128]{1,0:T(8,128)(2,1)S(1)} %get-tuple-element.130), channel_id=1, source_target_pairs={{0,2},{1,3},{2,6},{3,7},{6,4},{7,5},{4,0},{5,1},{8,10},{9,11},{10,... | collective-permute-start | bytes 1523720 | tf_op jit(solution)/shard_map/ppermute | solution.py:728
  169.7 10.2 %collective-permute-start.30 = (bf16[1984,128]{1,0:T(8,128)(2,1)S(1)}, bf16[1984,128]{1,0:T(8,128)(2,1)S(1)}, u32[]{:S(2)}, u32[]{:S(2)}) collective-permute-start(bf16[1984,128]{1,0:T(8,128)(2,1)S(1)} %get-tuple-element.129), channel_id=1, source_target_pairs={{0,8},{1,17},{2,10},{3,19},{4,12},{5,21},{6,14},{7,23},{8,0},{9,25... | collective-permute-start | bytes 1523720 | tf_op jit(solution)/shard_map/ppermute | solution.py:718
  176.8 34.1 %copy-start.1 = (f32[943392]{0:T(1024)S(1)}, f32[943392]{0:T(1024)}, u32[]{:S(2)}) copy-start(f32[943392]{0:T(1024)} %refs_8_.1) | copy-start | bytes 11320708
  177.5 33.3 %copy-start.12 = (s32[168]{0:T(256)S(1)}, s32[168]{0:T(256)}, u32[]{:S(2)}) copy-start(s32[168]{0:T(256)} %constant.18.clone.table_ref) | copy-start | bytes 2020
  177.6 9.1 %collective-permute-start.29 = (bf16[992,128]{1,0:T(8,128)(2,1)S(1)}, bf16[992,128]{1,0:T(8,128)(2,1)S(1)}, u32[]{:S(2)}, u32[]{:S(2)}) collective-permute-start(bf16[992,128]{1,0:T(8,128)(2,1)S(1)} %get-tuple-element.127), channel_id=1, source_target_pairs={{0,8},{1,17},{2,10},{3,19},{4,12},{5,21},{6,14},{7,23},{8,0},{9,25... | collective-permute-start | bytes 761864 | tf_op jit(solution)/shard_map/ppermute | solution.py:718
  180.6 10.0 %collective-permute-start.32 = (bf16[992,128]{1,0:T(8,128)(2,1)S(1)}, bf16[992,128]{1,0:T(8,128)(2,1)S(1)}, u32[]{:S(2)}, u32[]{:S(2)}) collective-permute-start(bf16[992,128]{1,0:T(8,128)(2,1)S(1)} %get-tuple-element.132), channel_id=1, source_target_pairs={{0,2},{1,3},{2,6},{3,7},{6,4},{7,5},{4,0},{5,1},{8,10},{9,11},{10,... | collective-permute-start | bytes 761864 | tf_op jit(solution)/shard_map/ppermute | solution.py:728
  184.2 8.7 %collective-permute-start.33 = (bf16[992,128]{1,0:T(8,128)(2,1)S(1)}, bf16[992,128]{1,0:T(8,128)(2,1)S(1)}, u32[]{:S(2)}, u32[]{:S(2)}) collective-permute-start(bf16[992,128]{1,0:T(8,128)(2,1)S(1)} %get-tuple-element.136), channel_id=1, source_target_pairs={{0,8},{1,17},{2,10},{3,19},{4,12},{5,21},{6,14},{7,23},{8,0},{9,25... | collective-permute-start | bytes 761864 | tf_op jit(solution)/shard_map/ppermute | solution.py:718
  186.2 8.1 %collective-permute-start.34 = (bf16[992,128]{1,0:T(8,128)(2,1)S(1)}, bf16[992,128]{1,0:T(8,128)(2,1)S(1)}, u32[]{:S(2)}, u32[]{:S(2)}) collective-permute-start(bf16[992,128]{1,0:T(8,128)(2,1)S(1)} %get-tuple-element.137), channel_id=1, source_target_pairs={{0,2},{1,3},{2,6},{3,7},{6,4},{7,5},{4,0},{5,1},{8,10},{9,11},{10,... | collective-permute-start | bytes 761864 | tf_op jit(solution)/shard_map/ppermute | solution.py:728
  191.3 7.2 %collective-permute-start.35 = (bf16[992,128]{1,0:T(8,128)(2,1)S(1)}, bf16[992,128]{1,0:T(8,128)(2,1)S(1)}, u32[]{:S(2)}, u32[]{:S(2)}) collective-permute-start(bf16[992,128]{1,0:T(8,128)(2,1)S(1)} %get-tuple-element.134.refs_0_), channel_id=1, source_target_pairs={{0,8},{1,17},{2,10},{3,19},{4,12},{5,21},{6,14},{7,23},{8,0},{9,25... | collective-permute-start | bytes 761864 | tf_op jit(solution)/shard_map/ppermute | solution.py:718
  195.4 9.1 %collective-permute-start.36 = (bf16[992,128]{1,0:T(8,128)(2,1)S(1)}, bf16[992,128]{1,0:T(8,128)(2,1)S(1)}, u32[]{:S(2)}, u32[]{:S(2)}) collective-permute-start(bf16[992,128]{1,0:T(8,128)(2,1)S(1)} %get-tuple-element.139.refs_1_), channel_id=1, source_target_pairs={{0,8},{1,17},{2,10},{3,19},{4,12},{5,21},{6,14},{7,23},{8,0},{9,25... | collective-permute-start | bytes 761864 | tf_op jit(solution)/shard_map/ppermute | solution.py:718
  196.3 10.0 %collective-permute-start.37 = (bf16[992,128]{1,0:T(8,128)(2,1)S(1)}, bf16[992,128]{1,0:T(8,128)(2,1)S(1)}, u32[]{:S(2)}, u32[]{:S(2)}) collective-permute-start(bf16[992,128]{1,0:T(8,128)(2,1)S(1)} %get-tuple-element.134.refs_0_), channel_id=1, source_target_pairs={{0,16},{1,9},{2,18},{3,11},{4,20},{5,13},{6,22},{7,15},{8,24},{9,1... | collective-permute-start | bytes 761864 | tf_op jit(solution)/shard_map/ppermute | solution.py:718
  198.4 7.9 %collective-permute-start.38 = (bf16[992,128]{1,0:T(8,128)(2,1)S(1)}, bf16[992,128]{1,0:T(8,128)(2,1)S(1)}, u32[]{:S(2)}, u32[]{:S(2)}) collective-permute-start(bf16[992,128]{1,0:T(8,128)(2,1)S(1)} %get-tuple-element.139.refs_1_), channel_id=1, source_target_pairs={{0,16},{1,9},{2,18},{3,11},{4,20},{5,13},{6,22},{7,15},{8,24},{9,1... | collective-permute-start | bytes 761864 | tf_op jit(solution)/shard_map/ppermute | solution.py:718
  198.5 9.7 %collective-permute-start.39 = (bf16[992,128]{1,0:T(8,128)(2,1)S(1)}, bf16[992,128]{1,0:T(8,128)(2,1)S(1)}, u32[]{:S(2)}, u32[]{:S(2)}) collective-permute-start(bf16[992,128]{1,0:T(8,128)(2,1)S(1)} %collective-permute-done.35.refs_2_), channel_id=1, source_target_pairs={{0,16},{1,9},{2,18},{3,11},{4,20},{5,13},{6,22},{7,15},{8,24},{9,1... | collective-permute-start | bytes 761864 | tf_op jit(solution)/shard_map/ppermute | solution.py:718
  204.4 6.4 %collective-permute-start.40 = (bf16[992,128]{1,0:T(8,128)(2,1)S(1)}, bf16[992,128]{1,0:T(8,128)(2,1)S(1)}, u32[]{:S(2)}, u32[]{:S(2)}) collective-permute-start(bf16[992,128]{1,0:T(8,128)(2,1)S(1)} %collective-permute-done.36.refs_3_), channel_id=1, source_target_pairs={{0,16},{1,9},{2,18},{3,11},{4,20},{5,13},{6,22},{7,15},{8,24},{9,1... | collective-permute-start | bytes 761864 | tf_op jit(solution)/shard_map/ppermute | solution.py:718
  (8 other events, 21.1 us)

commit v4 on v3

--- a/solution.py
+++ b/solution.py
@@ -301,6 +301,8 @@
     ]
     in_count = sum(geo.shards if isinstance(runs, int) else len(runs) for runs in piece_places(0, 0))
     out_count = sum(shape[0] for shape in grad_shapes)
+    half = len(grad_shapes) // 2
+    near_grads = [half > 0 and i % half < 1 for i in range(len(grad_shapes))]
 
     def kernel(where_ref, lengths_ref, tokens_ref, cotangent_ref, sinusoid_ref, *refs):
         piece_refs = refs[:count]
@@ -328,16 +330,18 @@
             if isinstance(runs, int):
                 runs = [(block, None, ref.shape[1], runs) for block in range(geo.shards)]
             for block, start, length, at in runs:
+                if start is not None and ref.shape[0] < geo.rows:
+                    store[block, pl.ds(aligned(at), length), :] = ref[pl.ds(start, length), :]
+                    continue
                 source = ref.at[block] if start is None else ref.at[pl.ds(start, length), :]
                 target = store.at[block, pl.ds(aligned(at), length), :]
                 arrivals.append((block, pltpu.make_async_copy(source, target, in_sems.at[len(arrivals)])))
+                arrivals[-1][1].start()
 
         def read_first(block):
             early, late = block <= geo.attention_blocks, block >= geo.vector_blocks
             return early or late if isinstance(block, int) else early | late
 
-        in_waves(arrivals, read_first, True, lambda copy: copy.start())
-        in_waves(arrivals, read_first, False, lambda copy: copy.start())
         in_waves(arrivals, read_first, True, lambda copy: copy.wait())
 
         def spans(matrix, low, high):
@@ -478,8 +482,11 @@
             d_hidden[...] += nt(d_up, load_wide(UP, 2 * tile, 2))
             save_wide(UP, 2 * tile, nn(hidden_t[...], d_up))
 
-        departures = []
-        for ref, (blocks, at, length) in zip(grad_refs, grad_parts(index)):
+        departures, near_refs = [], []
+        for near, ref, (blocks, at, length) in zip(near_grads, grad_refs, grad_parts(index)):
+            if near:
+                near_refs.append((ref, blocks[0]))
+                continue
             for i, block in enumerate(range(geo.shards) if blocks is None else blocks):
                 source = store.at[block, pl.ds(at, length), :]
                 departures.append((block, pltpu.make_async_copy(source, ref.at[i], out_sems.at[len(departures)])))
@@ -545,6 +552,8 @@
         save(VEC, 0, vec_grads[...].astype(BF16))
 
         in_waves(departures, done_first, False, lambda copy: copy.start())
+        for ref, block in near_refs:
+            ref[0] = store[block]
         in_waves(departures, done_first, True, lambda copy: copy.wait())
         in_waves(departures, done_first, False, lambda copy: copy.wait())
 
@@ -553,8 +562,8 @@
         kernel,
         in_specs=[pl.BlockSpec(memory_space=pltpu.SMEM)] * 2
         + [whole] * 3
-        + [pl.BlockSpec(memory_space=pl.ANY)] * count,
-        out_specs=[whole] * 2 + [pl.BlockSpec(memory_space=pl.ANY)] * len(grad_shapes),
+        + [pl.BlockSpec(memory_space=pl.ANY) if item.size >= geo.rows * LANES else whole for item in pieces],
+        out_specs=[whole] * 2 + [whole if near else pl.BlockSpec(memory_space=pltpu.HBM) for near in near_grads],
         out_shape=[
             jax.ShapeDtypeStruct((rows, D), BF16),
             jax.ShapeDtypeStruct((rows, D), F32),
@@ -610,22 +619,18 @@
     )(*scalars, *inputs, *after)
 
 
-def stack_up(after, items):
+def stack_up(after, *groups):
     def body(scalars, inputs, outs):
-        at = 0
-        for ref in inputs:
-            outs[0][pl.ds(at, ref.shape[0]), :] = ref[...]
-            at += ref.shape[0]
-
-    return small_step("stack_up", body, [], items, [(sum(item.shape[0] for item in items), LANES)], after)
-
-
-def join_block(geo, where, after, quarters):
-    def body(scalars, inputs, outs):
-        for ref, quarter in zip(inputs, neighbor_quarters(scalars[0][0], scalars[0][1])):
-            outs[0][pl.ds(aligned(quarter * geo.quarter), geo.quarter), :] = ref[...]
-
-    return small_step("join_block", body, [where], quarters, [(geo.rows, LANES)], after)
+        inputs = list(inputs)
+        for group, out in zip(groups, outs):
+            at = 0
+            for item in group:
+                out[pl.ds(at, item.shape[0]), :] = inputs.pop(0)[...]
+                at += item.shape[0]
+
+    items = [item for group in groups for item in group]
+    shapes = [(sum(item.shape[0] for item in group), LANES) for group in groups]
+    return small_step("stack_up", body, [], items, shapes, after)
 
 
 def reduce_step(geo, where, after, cores=None, pair=None, items=None, head=None, tails=None, halves=False):
@@ -752,41 +757,42 @@
         if direct_links:
             swapped = core_swap(block)
             pieces = [block, swapped]
-            quarter_1, token = stack_up([], [ring_hop(quarter)])
-            hop, one_1, two_1 = ring_hop(quarter_1), first_way(quarter_1), second_way(quarter_1)
-            quarter_2, token = stack_up([token, swapped], [hop])
-            hop, one_2, two_2 = ring_hop(quarter_2), first_way(quarter_2), second_way(quarter_2)
-            passed, token = stack_up([token, two_1], [one_1])
-            three_1 = second_way(passed)
-            quarter_3, token = stack_up([token], [hop])
-            one_3, two_3 = first_way(quarter_3), second_way(quarter_3)
-            passed, token = stack_up([token, two_2], [one_2])
-            three_2 = second_way(passed)
-            block, token = join_block(geo, where, [token], [quarter_1, one_1, two_1, three_1])
-            swapped = core_swap(block)
-            pieces += [block, swapped]
-            passed, token = stack_up([token, two_3], [one_3])
-            three_3 = second_way(passed)
-            stack, token = stack_up([token], [quarter_2, one_2, two_2, quarter_3, one_3, two_3])
-            stack_swapped = core_swap(stack)
-            pieces += [stack, stack_swapped]
-            last_2, token = stack_up([token], [three_2])
-            last_3, token = stack_up([token, swapped, stack_swapped], [three_3])
-            for item in (last_2, last_3):
-                pieces += [item, core_swap(item)]
+
+            def swap(item):
+                other = core_swap(item)
+                pieces.extend([item, other])
+                return other
+
+            near_1, token = stack_up([], [ring_hop(quarter)])
+            hop, one_1, two_1 = ring_hop(near_1), first_way(near_1), second_way(near_1)
+            near_2, pair_1, token = stack_up([token, swapped, swap(near_1), two_1], [hop], [hop, one_1])
+            hop, one_2, far_1 = ring_hop(near_2), first_way(near_2), second_way(pair_1)
+            near_3, pair_2, token = stack_up([token, swap(two_1), swap(pair_1)], [hop], [hop, one_2])
+            one_3, far_2 = first_way(near_3), second_way(pair_2)
+            one_3, token = stack_up([token, swap(pair_2)], [one_3])
+            three_3 = second_way(one_3)
+            for item in (far_1, one_3, far_2, three_3):
+                swap(item)
 
             def weight_places(index, replica):
-                places = []
-                for hops in range(2):
-                    for other in range(2):
-                        places.append([(block_of(hops, other)(index), 0, geo.rows, 0)])
                 size = geo.quarter
-                for which in ((0, 2), (1, 2), (2, 2), (0, 3), (1, 3), (2, 3)), ((3, 2),), ((3, 3),):
+                groups = (
+                    ((1, 0),),
+                    ((1, 2),),
+                    ((2, 0), (1, 1)),
+                    ((3, 0), (2, 1)),
+                    ((2, 2), (1, 3)),
+                    ((3, 1),),
+                    ((3, 2), (2, 3)),
+                    ((3, 3),),
+                )
+                places = [[(block_of(0, other)(index), 0, geo.rows, 0)] for other in range(2)]
+                for group in groups:
                     for other in range(2):
                         quarters = neighbor_quarters(index ^ other, replica)
                         places.append([
                             (block_of(hops, other)(index), i * size, size, quarters[quarter] * size)
-                            for i, (quarter, hops) in enumerate(which)
+                            for i, (hops, quarter) in enumerate(group)
                         ])
                 return places
 

time: 220 us -> 217 us (0.986)
  starting transfers between devices: 49.5 us -> 42.8 us
  waiting for transfers between devices: 110 us -> 116 us
    ppermute x24 -> x22, waiting for transfers between devices: 58.1 us -> 84.4 us  [permute(): return lax.ppermute(value, axes, pairs)]
    ppermute x8, waiting for transfers between devices: 46.8 us -> 26.7 us  [ring_hop(): return lax.ppermute(value, 'fsdp', pairs)]
    ppermute x24 -> x22, starting transfers between devices: 30.7 us -> 23.8 us  [permute(): return lax.ppermute(value, axes, pairs)]
    ppermute x9 -> x13, starting transfers between devices: 2.12 us -> 4.59 us  [core_swap(): lax.ppermute(value, 'fsdp', [(index, index ^ 1) for index in range(fsdp)])]
    ppermute x8, starting transfers between devices: 16.7 us -> 14.4 us  [ring_hop(): return lax.ppermute(value, 'fsdp', pairs)]
    pallas_call x21 -> x15, Pallas kernels: 11.7 us -> 10.7 us  [small_step(): pl.pallas_call(kernel, in_specs=[pl.BlockSpec(memory_space=pltpu.SMEM)] *...]
    unnamed x30 -> x24, local copies, waits for them, and re-layouts: 4.42 us -> 3.96 us
    ppermute x9 -> x13, waiting for transfers between devices: 4.73 us -> 4.6 us  [core_swap(): lax.ppermute(value, 'fsdp', [(index, index ^ 1) for index in range(fsdp)])]
  transfers between devices with their start and end apart: 41 -> 43, of which waited for: 23 -> 23; matrix products, arithmetic and copies ran while one was open for 0% -> 0% of each run, Pallas kernels for 5% -> 5%
where the time goes in v4:
time: 217 us
  waiting for transfers between devices  116 us (53%)
  Pallas kernels  53 us (24%)
  starting transfers between devices  42.8 us (20%)
  local copies, waits for them, and re-layouts  3.96 us (2%)
    ppermute x22, waiting for transfers between devices, permute(): return lax.ppermute(value, axes, pairs)  84.4 us
    pallas_call x1, Pallas kernels, model_step(): pl.pallas_call(kernel, in_specs=[pl.BlockSpec(memory_space=pltpu.SMEM)] *...  31.3 us
    ppermute x8, waiting for transfers between devices, ring_hop(): return lax.ppermute(value, 'fsdp', pairs)  26.7 us
    ppermute x22, starting transfers between devices, permute(): return lax.ppermute(value, axes, pairs)  23.8 us
    ppermute x8, starting transfers between devices, ring_hop(): return lax.ppermute(value, 'fsdp', pairs)  14.4 us
    pallas_call x15, Pallas kernels, small_step(): pl.pallas_call(kernel, in_specs=[pl.BlockSpec(memory_space=pltpu.SMEM)] *...  10.7 us
    pallas_call x1, Pallas kernels, optimizer_step(): pl.pallas_call(kernel, grid=(steps,), in_specs=[pl.BlockSpec(memory_space...  7.8 us
    ppermute x13, waiting for transfers between devices, core_swap(): lax.ppermute(value, 'fsdp', [(index, index ^ 1) for index in range(fsdp)])  4.6 us
  transfers between devices with their start and end apart: 43, of which 23 were waited for; matrix products, arithmetic and copies ran while one was open for 0% of the time, Pallas kernels for 5%

profile of v4, /device:TPU:0, one launch (start us, length us, event | category | flops | bytes accessed | tf_op | source)
XLA Modules:
  0.0 216.6 jit_solution(635801016643224172)
XLA Ops:
  0.7 2.1 copy-done
  3.5 3.1 %pack_block.1 = (bf16[7936,128]{1,0:T(8,128)(2,1)S(1)}, bf16[1984,128]{1,0:T(8,128)(2,1)S(1)}) custom-call(s32[2]{0:T(128)S(1)} %pad_add_fusion.where_ref.refs_0_, s32[168]{0:T(256)S(1)} %copy-done.8, f32[943392]{0:T(1024)S(1)} %copy-done), custom_call_target="tpu_custom_call" | custom-call | tf_op jit(solution)/shard_map/pack_block/pallas_call | solution.py:186
  7.0 2.8 %collective-permute-start.1 = (bf16[1984,128]{1,0:T(8,128)(2,1)S(1)}, bf16[1984,128]{1,0:T(8,128)(2,1)S(1)}, u32[]{:S(2)}, u32[]{:S(2)}) collective-permute-start(bf16[1984,128]{1,0:T(8,128)(2,1)S(1)} %get-tuple-element.65), channel_id=1, source_target_pairs={{0,2},{1,3},{2,6},{3,7},{6,4},{7,5},{4,0},{5,1},{8,10},{9,11},{10,... | collective-permute-start | bytes 1523720 | tf_op jit(solution)/shard_map/ppermute | solution.py:733
  9.8 13.1 %collective-permute-done.1.refs_0_ = bf16[1984,128]{1,0:T(8,128)(2,1)S(1)} collective-permute-done((bf16[1984,128]{1,0:T(8,128)(2,1)S(1)}, bf16[1984,128]{1,0:T(8,128)(2,1)S(1)}, u32[]{:S(2)}, u32[]{:S(2)}) %collective-permute-start.1) | collective-permute-done | bytes 507936 | tf_op jit(solution)/shard_map/ppermute | solution.py:733
  22.9 1.7 collective-permute-start.6
  25.5 1.5 collective-permute-start.3
  27.0 9.8 %collective-permute-done.6.refs_2_ = bf16[1984,128]{1,0:T(8,128)(2,1)S(1)} collective-permute-done((bf16[1984,128]{1,0:T(8,128)(2,1)S(1)}, bf16[1984,128]{1,0:T(8,128)(2,1)S(1)}, u32[]{:S(2)}, u32[]{:S(2)}) %collective-permute-start.6) | collective-permute-done | bytes 507936 | tf_op jit(solution)/shard_map/ppermute | solution.py:723
  36.8 1.6 collective-permute-done.5.refs_0_.refs_1_
  38.5 1.2 copy-done.2
  40.2 1.5 collective-permute-start.9
  43.1 11.6 %collective-permute-done.9.refs_2_ = bf16[1984,128]{1,0:T(8,128)(2,1)S(1)} collective-permute-done((bf16[1984,128]{1,0:T(8,128)(2,1)S(1)}, bf16[1984,128]{1,0:T(8,128)(2,1)S(1)}, u32[]{:S(2)}, u32[]{:S(2)}) %collective-permute-start.9) | collective-permute-done | bytes 507936 | tf_op jit(solution)/shard_map/ppermute | solution.py:723
  55.1 1.5 collective-permute-start.15
  56.6 1.5 collective-permute-start.13
  58.1 1.0 collective-permute-done.11.refs_10_
  59.1 0.9 collective-permute-start.12
  60.1 11.1 %collective-permute-done.13.refs_0_ = bf16[1984,128]{1,0:T(8,128)(2,1)S(1)} collective-permute-done((bf16[1984,128]{1,0:T(8,128)(2,1)S(1)}, bf16[1984,128]{1,0:T(8,128)(2,1)S(1)}, u32[]{:S(2)}, u32[]{:S(2)}) %collective-permute-start.13) | collective-permute-done | bytes 507936 | tf_op jit(solution)/shard_map/ppermute | solution.py:723
  72.3 3.1 %collective-permute-done.15.refs_14_ = bf16[3968,128]{1,0:T(8,128)(2,1)S(1)} collective-permute-done((bf16[3968,128]{1,0:T(8,128)(2,1)S(1)}, bf16[3968,128]{1,0:T(8,128)(2,1)S(1)}, u32[]{:S(2)}, u32[]{:S(2)}) %collective-permute-start.15) | collective-permute-done | bytes 1015840 | tf_op jit(solution)/shard_map/ppermute | solution.py:723
  76.4 4.5 %collective-permute-done.17.refs_16_ = bf16[1984,128]{1,0:T(8,128)(2,1)S(1)} collective-permute-done((bf16[1984,128]{1,0:T(8,128)(2,1)S(1)}, bf16[1984,128]{1,0:T(8,128)(2,1)S(1)}, u32[]{:S(2)}, u32[]{:S(2)}) %collective-permute-start.17) | collective-permute-done | bytes 507936 | tf_op jit(solution)/shard_map/ppermute | solution.py:723
  81.8 1.3 collective-permute-done.18.refs_17_
  83.1 31.3 %model_step.1 = (bf16[256,768]{1,0:T(8,128)(2,1)}, f32[256,768]{1,0:T(8,128)}, bf16[1,7936,128]{2,1,0:T(8,128)(2,1)S(1)}, bf16[1,7936,128]{2,1,0:T(8,128)(2,1)S(...) custom-call(s32[2]{0:T(128)S(1)} %pad_add_fusion.where_ref.refs_0_, ...), custom_call_target="tpu_custom_call" | custom-call | tf_op jit(solution)/shard_map/model_step/pallas_call | solution.py:561
  115.5 3.3 %collective-permute-done.20.refs_2_ = bf16[7936,128]{1,0:T(8,128)(2,1)S(1)} collective-permute-done((bf16[7936,128]{1,0:T(8,128)(2,1)}, bf16[7936,128]{1,0:T(8,128)(2,1)S(1)}, u32[]{:S(2)}, u32[]{:S(2)}) %collective-permute-start.20) | collective-permute-done | bytes 2031648 | tf_op jit(solution)/shard_map/ppermute | solution.py:726
  118.8 1.0 reduce_step.11
  120.6 1.5 collective-permute-start.21
  122.2 1.0 reduce_step.12
  123.2 1.4 collective-permute-start.23
  124.6 4.2 %collective-permute-done.25.refs_4_ = bf16[2,992,128]{2,1,0:T(8,128)(2,1)S(1)} collective-permute-done((bf16[2,992,128]{2,1,0:T(8,128)(2,1)S(1)}, bf16[2,992,128]{2,1,0:T(8,128)(2,1)S(1)}, u32[]{:S(2)}, u32[]{:S(2)}) %collective-permute-start.25) | collective-permute-done | bytes 507936 | tf_op jit(solution)/shard_map/ppermute | solution.py:723
  128.9 1.1 reduce_step.13
  130.8 1.3 collective-permute-start.26
  132.2 7.8 %collective-permute-done.26.refs_2_ = bf16[992,128]{1,0:T(8,128)(2,1)S(1)} collective-permute-done((bf16[992,128]{1,0:T(8,128)(2,1)S(1)}, bf16[992,128]{1,0:T(8,128)(2,1)S(1)}, u32[]{:S(2)}, u32[]{:S(2)}) %collective-permute-start.26) | collective-permute-done | bytes 253984 | tf_op jit(solution)/shard_map/ppermute | solution.py:723
  140.5 5.3 %collective-permute-done.21.refs_3_ = bf16[3968,128]{1,0:T(8,128)(2,1)S(1)} collective-permute-done((bf16[3968,128]{1,0:T(8,128)(2,1)S(1)}, bf16[3968,128]{1,0:T(8,128)(2,1)S(1)}, u32[]{:S(2)}, u32[]{:S(2)}) %collective-permute-start.21) | collective-permute-done | bytes 1015840 | tf_op jit(solution)/shard_map/ppermute | solution.py:733
  145.8 1.4 reduce_step.15
  148.5 2.4 %collective-permute-start.29 = (bf16[992,128]{1,0:T(8,128)(2,1)S(1)}, bf16[992,128]{1,0:T(8,128)(2,1)S(1)}, u32[]{:S(2)}, u32[]{:S(2)}) collective-permute-start(bf16[992,128]{1,0:T(8,128)(2,1)S(1)} %get-tuple-element.100), channel_id=1, source_target_pairs={{0,2},{1,3},{2,6},{3,7},{6,4},{7,5},{4,0},{5,1},{8,10},{9,11},{10,... | collective-permute-start | bytes 761864 | tf_op jit(solution)/shard_map/ppermute | solution.py:733
  150.8 6.0 %collective-permute-done.30.refs_2_ = bf16[2,1984,128]{2,1,0:T(8,128)(2,1)S(1)} collective-permute-done((bf16[2,1984,128]{2,1,0:T(8,128)(2,1)S(1)}, bf16[2,1984,128]{2,1,0:T(8,128)(2,1)S(1)}, u32[]{:S(2)}, u32[]{:S(2)}) %collective-permute-start.30) | collective-permute-done | bytes 1015840 | tf_op jit(solution)/shard_map/ppermute | solution.py:723
  157.6 4.1 %collective-permute-done.28.refs_2_ = bf16[1984,128]{1,0:T(8,128)(2,1)S(1)} collective-permute-done((bf16[1984,128]{1,0:T(8,128)(2,1)S(1)}, bf16[1984,128]{1,0:T(8,128)(2,1)S(1)}, u32[]{:S(2)}, u32[]{:S(2)}) %collective-permute-start.28) | collective-permute-done | bytes 507936 | tf_op jit(solution)/shard_map/ppermute | solution.py:723
  162.5 2.0 collective-permute-start.33
  165.1 8.5 %collective-permute-done.27.refs_2_ = bf16[2,1984,128]{2,1,0:T(8,128)(2,1)S(1)} collective-permute-done((bf16[2,1984,128]{2,1,0:T(8,128)(2,1)S(1)}, bf16[2,1984,128]{2,1,0:T(8,128)(2,1)S(1)}, u32[]{:S(2)}, u32[]{:S(2)}) %collective-permute-start.27) | collective-permute-done | bytes 1015840 | tf_op jit(solution)/shard_map/ppermute | solution.py:723
  174.3 3.3 %collective-permute-start.31 = (bf16[992,128]{1,0:T(8,128)(2,1)S(1)}, bf16[992,128]{1,0:T(8,128)(2,1)S(1)}, u32[]{:S(2)}, u32[]{:S(2)}) collective-permute-start(bf16[992,128]{1,0:T(8,128)(2,1)S(1)} %get-tuple-element.107), channel_id=1, source_target_pairs={{0,8},{1,17},{2,10},{3,19},{4,12},{5,21},{6,14},{7,23},{8,0},{9,25... | collective-permute-start | bytes 761864 | tf_op jit(solution)/shard_map/ppermute | solution.py:723
  178.6 3.8 %collective-permute-start.36 = (bf16[992,128]{1,0:T(8,128)(2,1)S(1)}, bf16[992,128]{1,0:T(8,128)(2,1)S(1)}, u32[]{:S(2)}, u32[]{:S(2)}) collective-permute-start(bf16[992,128]{1,0:T(8,128)(2,1)S(1)} %get-tuple-element.117), channel_id=1, source_target_pairs={{0,2},{1,3},{2,6},{3,7},{6,4},{7,5},{4,0},{5,1},{8,10},{9,11},{10,... | collective-permute-start | bytes 761864 | tf_op jit(solution)/shard_map/ppermute | solution.py:733
  182.4 5.3 %collective-permute-done.34.refs_3_ = bf16[992,128]{1,0:T(8,128)(2,1)S(1)} collective-permute-done((bf16[992,128]{1,0:T(8,128)(2,1)S(1)}, bf16[992,128]{1,0:T(8,128)(2,1)S(1)}, u32[]{:S(2)}, u32[]{:S(2)}) %collective-permute-start.34) | collective-permute-done | bytes 253984 | tf_op jit(solution)/shard_map/ppermute | solution.py:733
  189.2 1.3 collective-permute-done.36.refs_3_
  190.4 1.1 reduce_step.21
  191.5 1.3 collective-permute-start.38
  193.5 1.3 collective-permute-start.40
  194.9 2.1 collective-permute-done.37.refs_2_
  197.6 4.9 %collective-permute-done.38.refs_3_ = bf16[992,128]{1,0:T(8,128)(2,1)S(1)} collective-permute-done((bf16[992,128]{1,0:T(8,128)(2,1)S(1)}, bf16[992,128]{1,0:T(8,128)(2,1)S(1)}, u32[]{:S(2)}, u32[]{:S(2)}) %collective-permute-start.38) | collective-permute-done | bytes 253984 | tf_op jit(solution)/shard_map/ppermute | solution.py:723
  203.0 1.5 collective-permute-done.41.refs_6_
  204.6 4.2 %collective-permute-done.42.refs_7_ = bf16[992,128]{1,0:T(8,128)(2,1)S(1)} collective-permute-done((bf16[992,128]{1,0:T(8,128)(2,1)S(1)}, bf16[992,128]{1,0:T(8,128)(2,1)S(1)}, u32[]{:S(2)}, u32[]{:S(2)}) %collective-permute-start.42) | collective-permute-done | bytes 253984 | tf_op jit(solution)/shard_map/ppermute | solution.py:723
  208.8 7.8 %optimizer_step.1 = (f32[943392]{0:T(1024)}, f32[943392]{0:T(1024)}, f32[943392]{0:T(1024)}) custom-call(s32[2]{0:T(128)S(1)} %pad_add_fusion.where_ref.refs_0_, s32[168]{0:T(256)S(1)} %copy-done.9, bf16[992,128]{1,0:T(8,128)(2,1)S(1)} %get-tuple-element.114.refs_0_, bf16[992,128]{1,0:T(8,128)(2,1)S(1)} %get-tuple-element.119.refs_1_, ...), custom_call_target="tpu_custom_call" | custom-call | tf_op jit(solution)/shard_map/optimizer_step/pallas_call | solution.py:254
  (85 shorter events, 19.3 us)
Async XLA Ops:
  6.6 31.9 %copy-start.5 = (bf16[7936,128]{1,0:T(8,128)(2,1)}, bf16[7936,128]{1,0:T(8,128)(2,1)S(1)}, u32[]{:S(2)}) copy-start(bf16[7936,128]{1,0:T(8,128)(2,1)S(1)} %get-tuple-element.64.refs_0_) | copy-start | bytes 6094852
  6.6 31.8 %collective-permute-start = (bf16[7936,128]{1,0:T(8,128)(2,1)S(1)}, bf16[7936,128]{1,0:T(8,128)(2,1)S(1)}, u32[]{:S(2)}, u32[]{:S(2)}) collective-permute-start(bf16[7936,128]{1,0:T(8,128)(2,1)S(1)} %get-tuple-element.64.refs_0_), channel_id=1, source_target_pairs={{0,1},{1,0},{2,3},{3,2},{4,5},{5,4},{6,7},{7,6},{8,9},{9,8},{10,11... | collective-permute-start | bytes 6094856 | tf_op jit(solution)/shard_map/ppermute | solution.py:726
  7.0 15.9 %collective-permute-start.1 = (bf16[1984,128]{1,0:T(8,128)(2,1)S(1)}, bf16[1984,128]{1,0:T(8,128)(2,1)S(1)}, u32[]{:S(2)}, u32[]{:S(2)}) collective-permute-start(bf16[1984,128]{1,0:T(8,128)(2,1)S(1)} %get-tuple-element.65), channel_id=1, source_target_pairs={{0,2},{1,3},{2,6},{3,7},{6,4},{7,5},{4,0},{5,1},{8,10},{9,11},{10,... | collective-permute-start | bytes 1523720 | tf_op jit(solution)/shard_map/ppermute | solution.py:733
  22.9 13.9 %collective-permute-start.6 = (bf16[1984,128]{1,0:T(8,128)(2,1)S(1)}, bf16[1984,128]{1,0:T(8,128)(2,1)S(1)}, u32[]{:S(2)}, u32[]{:S(2)}) collective-permute-start(bf16[1984,128]{1,0:T(8,128)(2,1)S(1)} %get-tuple-element.66.refs_2_), channel_id=1, source_target_pairs={{0,8},{1,17},{2,10},{3,19},{4,12},{5,21},{6,14},{7,23},{8,0},{9,25... | collective-permute-start | bytes 1523720 | tf_op jit(solution)/shard_map/ppermute | solution.py:723
  24.6 13.8 %collective-permute-start.5 = (bf16[1984,128]{1,0:T(8,128)(2,1)S(1)}, bf16[1984,128]{1,0:T(8,128)(2,1)S(1)}, u32[]{:S(2)}, u32[]{:S(2)}) collective-permute-start(bf16[1984,128]{1,0:T(8,128)(2,1)S(1)} %get-tuple-element.66.refs_2_), channel_id=1, source_target_pairs={{0,2},{1,3},{2,6},{3,7},{6,4},{7,5},{4,0},{5,1},{8,10},{9,11},{10,... | collective-permute-start | bytes 1523720 | tf_op jit(solution)/shard_map/ppermute | solution.py:733
  25.5 12.9 %collective-permute-start.3 = (bf16[1984,128]{1,0:T(8,128)(2,1)S(1)}, bf16[1984,128]{1,0:T(8,128)(2,1)S(1)}, u32[]{:S(2)}, u32[]{:S(2)}) collective-permute-start(bf16[1984,128]{1,0:T(8,128)(2,1)S(1)} %get-tuple-element.66.refs_2_), channel_id=1, source_target_pairs={{0,16},{1,9},{2,18},{3,11},{4,20},{5,13},{6,22},{7,15},{8,24},{9,1... | collective-permute-start | bytes 1523720 | tf_op jit(solution)/shard_map/ppermute | solution.py:723
  27.0 11.4 %collective-permute-start.2 = (bf16[1984,128]{1,0:T(8,128)(2,1)S(1)}, bf16[1984,128]{1,0:T(8,128)(2,1)S(1)}, u32[]{:S(2)}, u32[]{:S(2)}) collective-permute-start(bf16[1984,128]{1,0:T(8,128)(2,1)S(1)} %get-tuple-element.66.refs_2_), channel_id=1, source_target_pairs={{0,1},{1,0},{2,3},{3,2},{4,5},{5,4},{6,7},{7,6},{8,9},{9,8},{10,11... | collective-permute-start | bytes 1523720 | tf_op jit(solution)/shard_map/ppermute | solution.py:726
  39.7 15.2 %collective-permute-start.7 = (bf16[3968,128]{1,0:T(8,128)(2,1)S(1)}, bf16[3968,128]{1,0:T(8,128)(2,1)S(1)}, u32[]{:S(2)}, u32[]{:S(2)}) collective-permute-start(bf16[3968,128]{1,0:T(8,128)(2,1)S(1)} %get-tuple-element.68.refs_6_), channel_id=1, source_target_pairs={{0,1},{1,0},{2,3},{3,2},{4,5},{5,4},{6,7},{7,6},{8,9},{9,8},{10,11... | collective-permute-start | bytes 3047432 | tf_op jit(solution)/shard_map/ppermute | solution.py:726
  39.7 3.4 %collective-permute-start.4 = (bf16[1984,128]{1,0:T(8,128)(2,1)S(1)}, bf16[1984,128]{1,0:T(8,128)(2,1)S(1)}, u32[]{:S(2)}, u32[]{:S(2)}) collective-permute-start(bf16[1984,128]{1,0:T(8,128)(2,1)S(1)} %collective-permute-done.3.refs_6_.refs_4_), channel_id=1, source_target_pairs={{0,1},{1,0},{2,3},{3,2},{4,5},{5,4},{6,7},{7,6},{8,9},{9,8},{10,11... | collective-permute-start | bytes 1523720 | tf_op jit(solution)/shard_map/ppermute | solution.py:726
  40.2 14.4 %collective-permute-start.9 = (bf16[1984,128]{1,0:T(8,128)(2,1)S(1)}, bf16[1984,128]{1,0:T(8,128)(2,1)S(1)}, u32[]{:S(2)}, u32[]{:S(2)}) collective-permute-start(bf16[1984,128]{1,0:T(8,128)(2,1)S(1)} %get-tuple-element.69), channel_id=1, source_target_pairs={{0,8},{1,17},{2,10},{3,19},{4,12},{5,21},{6,14},{7,23},{8,0},{9,25... | collective-permute-start | bytes 1523720 | tf_op jit(solution)/shard_map/ppermute | solution.py:723
  41.7 13.2 %collective-permute-start.8 = (bf16[1984,128]{1,0:T(8,128)(2,1)S(1)}, bf16[1984,128]{1,0:T(8,128)(2,1)S(1)}, u32[]{:S(2)}, u32[]{:S(2)}) collective-permute-start(bf16[1984,128]{1,0:T(8,128)(2,1)S(1)} %get-tuple-element.69), channel_id=1, source_target_pairs={{0,2},{1,3},{2,6},{3,7},{6,4},{7,5},{4,0},{5,1},{8,10},{9,11},{10,... | collective-permute-start | bytes 1523720 | tf_op jit(solution)/shard_map/ppermute | solution.py:733
  42.6 16.6 %collective-permute-start.11 = (bf16[3968,128]{1,0:T(8,128)(2,1)S(1)}, bf16[3968,128]{1,0:T(8,128)(2,1)S(1)}, u32[]{:S(2)}, u32[]{:S(2)}) collective-permute-start(bf16[3968,128]{1,0:T(8,128)(2,1)S(1)} %get-tuple-element.68.refs_6_), channel_id=1, source_target_pairs={{0,16},{1,9},{2,18},{3,11},{4,20},{5,13},{6,22},{7,15},{8,24},{9,1... | collective-permute-start | bytes 3047432 | tf_op jit(solution)/shard_map/ppermute | solution.py:723
  55.0 16.1 %collective-permute-start.10 = (bf16[3968,128]{1,0:T(8,128)(2,1)S(1)}, bf16[3968,128]{1,0:T(8,128)(2,1)S(1)}, u32[]{:S(2)}, u32[]{:S(2)}) collective-permute-start(bf16[3968,128]{1,0:T(8,128)(2,1)S(1)} %get-tuple-element.71.refs_8_), channel_id=1, source_target_pairs={{0,1},{1,0},{2,3},{3,2},{4,5},{5,4},{6,7},{7,6},{8,9},{9,8},{10,11... | collective-permute-start | bytes 3047432 | tf_op jit(solution)/shard_map/ppermute | solution.py:726
  55.1 20.4 %collective-permute-start.15 = (bf16[3968,128]{1,0:T(8,128)(2,1)S(1)}, bf16[3968,128]{1,0:T(8,128)(2,1)S(1)}, u32[]{:S(2)}, u32[]{:S(2)}) collective-permute-start(bf16[3968,128]{1,0:T(8,128)(2,1)S(1)} %get-tuple-element.71.refs_8_), channel_id=1, source_target_pairs={{0,16},{1,9},{2,18},{3,11},{4,20},{5,13},{6,22},{7,15},{8,24},{9,1... | collective-permute-start | bytes 3047432 | tf_op jit(solution)/shard_map/ppermute | solution.py:723
  56.6 14.5 %collective-permute-start.13 = (bf16[1984,128]{1,0:T(8,128)(2,1)S(1)}, bf16[1984,128]{1,0:T(8,128)(2,1)S(1)}, u32[]{:S(2)}, u32[]{:S(2)}) collective-permute-start(bf16[1984,128]{1,0:T(8,128)(2,1)S(1)} %get-tuple-element.72), channel_id=1, source_target_pairs={{0,8},{1,17},{2,10},{3,19},{4,12},{5,21},{6,14},{7,23},{8,0},{9,25... | collective-permute-start | bytes 1523720 | tf_op jit(solution)/shard_map/ppermute | solution.py:723
  59.1 22.6 %collective-permute-start.12 = (bf16[3968,128]{1,0:T(8,128)(2,1)S(1)}, bf16[3968,128]{1,0:T(8,128)(2,1)S(1)}, u32[]{:S(2)}, u32[]{:S(2)}) collective-permute-start(bf16[3968,128]{1,0:T(8,128)(2,1)S(1)} %collective-permute-done.11.refs_10_), channel_id=1, source_target_pairs={{0,1},{1,0},{2,3},{3,2},{4,5},{5,4},{6,7},{7,6},{8,9},{9,8},{10,11... | collective-permute-start | bytes 3047432 | tf_op jit(solution)/shard_map/ppermute | solution.py:726
  71.8 9.1 %collective-permute-start.17 = (bf16[1984,128]{1,0:T(8,128)(2,1)S(1)}, bf16[1984,128]{1,0:T(8,128)(2,1)S(1)}, u32[]{:S(2)}, u32[]{:S(2)}) collective-permute-start(bf16[1984,128]{1,0:T(8,128)(2,1)S(1)} %get-tuple-element.74.refs_12_), channel_id=1, source_target_pairs={{0,16},{1,9},{2,18},{3,11},{4,20},{5,13},{6,22},{7,15},{8,24},{9,1... | collective-permute-start | bytes 1523720 | tf_op jit(solution)/shard_map/ppermute | solution.py:723
  75.5 6.3 %collective-permute-start.16 = (bf16[3968,128]{1,0:T(8,128)(2,1)S(1)}, bf16[3968,128]{1,0:T(8,128)(2,1)S(1)}, u32[]{:S(2)}, u32[]{:S(2)}) collective-permute-start(bf16[3968,128]{1,0:T(8,128)(2,1)S(1)} %collective-permute-done.15.refs_14_), channel_id=1, source_target_pairs={{0,1},{1,0},{2,3},{3,2},{4,5},{5,4},{6,7},{7,6},{8,9},{9,8},{10,11... | collective-permute-start | bytes 3047432 | tf_op jit(solution)/shard_map/ppermute | solution.py:726
  76.4 5.4 %collective-permute-start.14 = (bf16[1984,128]{1,0:T(8,128)(2,1)S(1)}, bf16[1984,128]{1,0:T(8,128)(2,1)S(1)}, u32[]{:S(2)}, u32[]{:S(2)}) collective-permute-start(bf16[1984,128]{1,0:T(8,128)(2,1)S(1)} %get-tuple-element.74.refs_12_), channel_id=1, source_target_pairs={{0,1},{1,0},{2,3},{3,2},{4,5},{5,4},{6,7},{7,6},{8,9},{9,8},{10,11... | collective-permute-start | bytes 1523720 | tf_op jit(solution)/shard_map/ppermute | solution.py:726
  80.9 2.2 collective-permute-start.18
  114.4 4.4 %collective-permute-start.20 = (bf16[7936,128]{1,0:T(8,128)(2,1)}, bf16[7936,128]{1,0:T(8,128)(2,1)S(1)}, u32[]{:S(2)}, u32[]{:S(2)}) collective-permute-start(bf16[7936,128]{1,0:T(8,128)(2,1)} %bitcast.23), channel_id=1, source_target_pairs={{0,1},{1,0},{2,3},{3,2},{4,5},{5,4},{6,7},{7,6},{8,9},{9,8},{10,11... | collective-permute-start | bytes 6094856 | tf_op jit(solution)/shard_map/ppermute | solution.py:726
  114.9 7.3 %collective-permute-start.22 = (bf16[7936,128]{1,0:T(8,128)(2,1)}, bf16[7936,128]{1,0:T(8,128)(2,1)S(1)}, u32[]{:S(2)}, u32[]{:S(2)}) collective-permute-start(bf16[7936,128]{1,0:T(8,128)(2,1)} %bitcast.22), channel_id=1, source_target_pairs={{0,1},{1,0},{2,3},{3,2},{4,5},{5,4},{6,7},{7,6},{8,9},{9,8},{10,11... | collective-permute-start | bytes 6094856 | tf_op jit(solution)/shard_map/ppermute | solution.py:726
  115.0 9.7 %collective-permute-start.24 = (bf16[7936,128]{1,0:T(8,128)(2,1)}, bf16[7936,128]{1,0:T(8,128)(2,1)S(1)}, u32[]{:S(2)}, u32[]{:S(2)}) collective-permute-start(bf16[7936,128]{1,0:T(8,128)(2,1)} %bitcast.21), channel_id=1, source_target_pairs={{0,1},{1,0},{2,3},{3,2},{4,5},{5,4},{6,7},{7,6},{8,9},{9,8},{10,11... | collective-permute-start | bytes 6094856 | tf_op jit(solution)/shard_map/ppermute | solution.py:726
  115.4 25.1 %collective-permute-start.19 = (bf16[7936,128]{1,0:T(8,128)(2,1)}, bf16[7936,128]{1,0:T(8,128)(2,1)S(1)}, u32[]{:S(2)}, u32[]{:S(2)}) collective-permute-start(bf16[7936,128]{1,0:T(8,128)(2,1)} %bitcast.20), channel_id=1, source_target_pairs={{0,1},{1,0},{2,3},{3,2},{4,5},{5,4},{6,7},{7,6},{8,9},{9,8},{10,11... | collective-permute-start | bytes 6094856 | tf_op jit(solution)/shard_map/ppermute | solution.py:726
  119.8 9.1 %collective-permute-start.25 = (bf16[2,992,128]{2,1,0:T(8,128)(2,1)S(1)}, bf16[2,992,128]{2,1,0:T(8,128)(2,1)S(1)}, u32[]{:S(2)}, u32[]{:S(2)}) collective-permute-start(bf16[2,992,128]{2,1,0:T(8,128)(2,1)S(1)} %get-tuple-element.90), channel_id=1, source_target_pairs={{0,16},{1,9},{2,18},{3,11},{4,20},{5,13},{6,22},{7,15},{8,24},{9,1... | collective-permute-start | bytes 1523720 | tf_op jit(solution)/shard_map/ppermute | solution.py:723
  120.6 25.2 %collective-permute-start.21 = (bf16[3968,128]{1,0:T(8,128)(2,1)S(1)}, bf16[3968,128]{1,0:T(8,128)(2,1)S(1)}, u32[]{:S(2)}, u32[]{:S(2)}) collective-permute-start(bf16[3968,128]{1,0:T(8,128)(2,1)S(1)} %get-tuple-element.81), channel_id=1, source_target_pairs={{0,4},{1,5},{2,0},{3,1},{6,2},{7,3},{4,6},{5,7},{8,12},{9,13},{10,... | collective-permute-start | bytes 3047432 | tf_op jit(solution)/shard_map/ppermute | solution.py:733
  123.2 22.6 %collective-permute-start.23 = (bf16[2,1984,128]{2,1,0:T(8,128)(2,1)S(1)}, bf16[2,1984,128]{2,1,0:T(8,128)(2,1)S(1)}, u32[]{:S(2)}, u32[]{:S(2)}) collective-permute-start(bf16[2,1984,128]{2,1,0:T(8,128)(2,1)S(1)} %get-tuple-element.86), channel_id=1, source_target_pairs={{0,16},{1,9},{2,18},{3,11},{4,20},{5,13},{6,22},{7,15},{8,24},{9,1... | collective-permute-start | bytes 3047432 | tf_op jit(solution)/shard_map/ppermute | solution.py:723
  130.0 26.9 %collective-permute-start.30 = (bf16[2,1984,128]{2,1,0:T(8,128)(2,1)S(1)}, bf16[2,1984,128]{2,1,0:T(8,128)(2,1)S(1)}, u32[]{:S(2)}, u32[]{:S(2)}) collective-permute-start(bf16[2,1984,128]{2,1,0:T(8,128)(2,1)S(1)} %get-tuple-element.102), channel_id=1, source_target_pairs={{0,16},{1,9},{2,18},{3,11},{4,20},{5,13},{6,22},{7,15},{8,24},{9,1... | collective-permute-start | bytes 3047432 | tf_op jit(solution)/shard_map/ppermute | solution.py:723
  130.8 9.1 %collective-permute-start.26 = (bf16[992,128]{1,0:T(8,128)(2,1)S(1)}, bf16[992,128]{1,0:T(8,128)(2,1)S(1)}, u32[]{:S(2)}, u32[]{:S(2)}) collective-permute-start(bf16[992,128]{1,0:T(8,128)(2,1)S(1)} %get-tuple-element.93), channel_id=1, source_target_pairs={{0,8},{1,17},{2,10},{3,19},{4,12},{5,21},{6,14},{7,23},{8,0},{9,25... | collective-permute-start | bytes 761864 | tf_op jit(solution)/shard_map/ppermute | solution.py:723
  145.8 62.9 %copy-start.4 = (f32[943392]{0:T(1024)S(1)}, f32[943392]{0:T(1024)}, u32[]{:S(2)}) copy-start(f32[943392]{0:T(1024)} %refs_10_.1) | copy-start | bytes 11320708
  147.2 14.6 %collective-permute-start.28 = (bf16[1984,128]{1,0:T(8,128)(2,1)S(1)}, bf16[1984,128]{1,0:T(8,128)(2,1)S(1)}, u32[]{:S(2)}, u32[]{:S(2)}) collective-permute-start(bf16[1984,128]{1,0:T(8,128)(2,1)S(1)} %get-tuple-element.99), channel_id=1, source_target_pairs={{0,8},{1,17},{2,10},{3,19},{4,12},{5,21},{6,14},{7,23},{8,0},{9,25... | collective-permute-start | bytes 1523720 | tf_op jit(solution)/shard_map/ppermute | solution.py:723
  147.8 25.8 %collective-permute-start.27 = (bf16[2,1984,128]{2,1,0:T(8,128)(2,1)S(1)}, bf16[2,1984,128]{2,1,0:T(8,128)(2,1)S(1)}, u32[]{:S(2)}, u32[]{:S(2)}) collective-permute-start(bf16[2,1984,128]{2,1,0:T(8,128)(2,1)S(1)} %get-tuple-element.97), channel_id=1, source_target_pairs={{0,16},{1,9},{2,18},{3,11},{4,20},{5,13},{6,22},{7,15},{8,24},{9,1... | collective-permute-start | bytes 3047432 | tf_op jit(solution)/shard_map/ppermute | solution.py:723
  148.5 9.2 %collective-permute-start.29 = (bf16[992,128]{1,0:T(8,128)(2,1)S(1)}, bf16[992,128]{1,0:T(8,128)(2,1)S(1)}, u32[]{:S(2)}, u32[]{:S(2)}) collective-permute-start(bf16[992,128]{1,0:T(8,128)(2,1)S(1)} %get-tuple-element.100), channel_id=1, source_target_pairs={{0,2},{1,3},{2,6},{3,7},{6,4},{7,5},{4,0},{5,1},{8,10},{9,11},{10,... | collective-permute-start | bytes 761864 | tf_op jit(solution)/shard_map/ppermute | solution.py:733
  156.9 51.9 %copy-start.3 = (f32[943392]{0:T(1024)S(1)}, f32[943392]{0:T(1024)}, u32[]{:S(2)}) copy-start(f32[943392]{0:T(1024)} %refs_9_.1) | copy-start | bytes 11320708
  162.5 15.2 %collective-permute-start.33 = (bf16[1984,128]{1,0:T(8,128)(2,1)S(1)}, bf16[1984,128]{1,0:T(8,128)(2,1)S(1)}, u32[]{:S(2)}, u32[]{:S(2)}) collective-permute-start(bf16[1984,128]{1,0:T(8,128)(2,1)S(1)} %get-tuple-element.110), channel_id=1, source_target_pairs={{0,2},{1,3},{2,6},{3,7},{6,4},{7,5},{4,0},{5,1},{8,10},{9,11},{10,... | collective-permute-start | bytes 1523720 | tf_op jit(solution)/shard_map/ppermute | solution.py:733
  164.5 13.2 %collective-permute-start.32 = (bf16[1984,128]{1,0:T(8,128)(2,1)S(1)}, bf16[1984,128]{1,0:T(8,128)(2,1)S(1)}, u32[]{:S(2)}, u32[]{:S(2)}) collective-permute-start(bf16[1984,128]{1,0:T(8,128)(2,1)S(1)} %get-tuple-element.109), channel_id=1, source_target_pairs={{0,8},{1,17},{2,10},{3,19},{4,12},{5,21},{6,14},{7,23},{8,0},{9,25... | collective-permute-start | bytes 1523720 | tf_op jit(solution)/shard_map/ppermute | solution.py:723
  173.6 35.2 %copy-start.1 = (f32[943392]{0:T(1024)S(1)}, f32[943392]{0:T(1024)}, u32[]{:S(2)}) copy-start(f32[943392]{0:T(1024)} %refs_8_.1) | copy-start | bytes 11320708
  174.3 34.4 %copy-start.9 = (s32[168]{0:T(256)S(1)}, s32[168]{0:T(256)}, u32[]{:S(2)}) copy-start(s32[168]{0:T(256)} %constant.18.clone.table_ref) | copy-start | bytes 2020
  174.3 8.0 %collective-permute-start.31 = (bf16[992,128]{1,0:T(8,128)(2,1)S(1)}, bf16[992,128]{1,0:T(8,128)(2,1)S(1)}, u32[]{:S(2)}, u32[]{:S(2)}) collective-permute-start(bf16[992,128]{1,0:T(8,128)(2,1)S(1)} %get-tuple-element.107), channel_id=1, source_target_pairs={{0,8},{1,17},{2,10},{3,19},{4,12},{5,21},{6,14},{7,23},{8,0},{9,25... | collective-permute-start | bytes 761864 | tf_op jit(solution)/shard_map/ppermute | solution.py:723
  178.4 9.3 %collective-permute-start.34 = (bf16[992,128]{1,0:T(8,128)(2,1)S(1)}, bf16[992,128]{1,0:T(8,128)(2,1)S(1)}, u32[]{:S(2)}, u32[]{:S(2)}) collective-permute-start(bf16[992,128]{1,0:T(8,128)(2,1)S(1)} %get-tuple-element.112), channel_id=1, source_target_pairs={{0,2},{1,3},{2,6},{3,7},{6,4},{7,5},{4,0},{5,1},{8,10},{9,11},{10,... | collective-permute-start | bytes 761864 | tf_op jit(solution)/shard_map/ppermute | solution.py:733
  178.5 10.7 %collective-permute-start.35 = (bf16[992,128]{1,0:T(8,128)(2,1)S(1)}, bf16[992,128]{1,0:T(8,128)(2,1)S(1)}, u32[]{:S(2)}, u32[]{:S(2)}) collective-permute-start(bf16[992,128]{1,0:T(8,128)(2,1)S(1)} %get-tuple-element.116), channel_id=1, source_target_pairs={{0,8},{1,17},{2,10},{3,19},{4,12},{5,21},{6,14},{7,23},{8,0},{9,25... | collective-permute-start | bytes 761864 | tf_op jit(solution)/shard_map/ppermute | solution.py:723
  178.6 11.9 %collective-permute-start.36 = (bf16[992,128]{1,0:T(8,128)(2,1)S(1)}, bf16[992,128]{1,0:T(8,128)(2,1)S(1)}, u32[]{:S(2)}, u32[]{:S(2)}) collective-permute-start(bf16[992,128]{1,0:T(8,128)(2,1)S(1)} %get-tuple-element.117), channel_id=1, source_target_pairs={{0,2},{1,3},{2,6},{3,7},{6,4},{7,5},{4,0},{5,1},{8,10},{9,11},{10,... | collective-permute-start | bytes 761864 | tf_op jit(solution)/shard_map/ppermute | solution.py:733
  188.3 8.7 %collective-permute-start.37 = (bf16[992,128]{1,0:T(8,128)(2,1)S(1)}, bf16[992,128]{1,0:T(8,128)(2,1)S(1)}, u32[]{:S(2)}, u32[]{:S(2)}) collective-permute-start(bf16[992,128]{1,0:T(8,128)(2,1)S(1)} %get-tuple-element.114.refs_0_), channel_id=1, source_target_pairs={{0,8},{1,17},{2,10},{3,19},{4,12},{5,21},{6,14},{7,23},{8,0},{9,25... | collective-permute-start | bytes 761864 | tf_op jit(solution)/shard_map/ppermute | solution.py:723
  191.5 10.9 %collective-permute-start.38 = (bf16[992,128]{1,0:T(8,128)(2,1)S(1)}, bf16[992,128]{1,0:T(8,128)(2,1)S(1)}, u32[]{:S(2)}, u32[]{:S(2)}) collective-permute-start(bf16[992,128]{1,0:T(8,128)(2,1)S(1)} %get-tuple-element.119.refs_1_), channel_id=1, source_target_pairs={{0,8},{1,17},{2,10},{3,19},{4,12},{5,21},{6,14},{7,23},{8,0},{9,25... | collective-permute-start | bytes 761864 | tf_op jit(solution)/shard_map/ppermute | solution.py:723
  192.8 10.2 %collective-permute-start.39 = (bf16[992,128]{1,0:T(8,128)(2,1)S(1)}, bf16[992,128]{1,0:T(8,128)(2,1)S(1)}, u32[]{:S(2)}, u32[]{:S(2)}) collective-permute-start(bf16[992,128]{1,0:T(8,128)(2,1)S(1)} %get-tuple-element.114.refs_0_), channel_id=1, source_target_pairs={{0,16},{1,9},{2,18},{3,11},{4,20},{5,13},{6,22},{7,15},{8,24},{9,1... | collective-permute-start | bytes 761864 | tf_op jit(solution)/shard_map/ppermute | solution.py:723
  193.5 9.5 %collective-permute-start.40 = (bf16[992,128]{1,0:T(8,128)(2,1)S(1)}, bf16[992,128]{1,0:T(8,128)(2,1)S(1)}, u32[]{:S(2)}, u32[]{:S(2)}) collective-permute-start(bf16[992,128]{1,0:T(8,128)(2,1)S(1)} %get-tuple-element.119.refs_1_), channel_id=1, source_target_pairs={{0,16},{1,9},{2,18},{3,11},{4,20},{5,13},{6,22},{7,15},{8,24},{9,1... | collective-permute-start | bytes 761864 | tf_op jit(solution)/shard_map/ppermute | solution.py:723
  197.0 7.6 %collective-permute-start.41 = (bf16[992,128]{1,0:T(8,128)(2,1)S(1)}, bf16[992,128]{1,0:T(8,128)(2,1)S(1)}, u32[]{:S(2)}, u32[]{:S(2)}) collective-permute-start(bf16[992,128]{1,0:T(8,128)(2,1)S(1)} %collective-permute-done.37.refs_2_), channel_id=1, source_target_pairs={{0,16},{1,9},{2,18},{3,11},{4,20},{5,13},{6,22},{7,15},{8,24},{9,1... | collective-permute-start | bytes 761864 | tf_op jit(solution)/shard_map/ppermute | solution.py:723
  202.5 6.3 %collective-permute-start.42 = (bf16[992,128]{1,0:T(8,128)(2,1)S(1)}, bf16[992,128]{1,0:T(8,128)(2,1)S(1)}, u32[]{:S(2)}, u32[]{:S(2)}) collective-permute-start(bf16[992,128]{1,0:T(8,128)(2,1)S(1)} %collective-permute-done.38.refs_3_), channel_id=1, source_target_pairs={{0,16},{1,9},{2,18},{3,11},{4,20},{5,13},{6,22},{7,15},{8,24},{9,1... | collective-permute-start | bytes 761864 | tf_op jit(solution)/shard_map/ppermute | solution.py:723
  (7 other events, 115.2 us)

commit v5 on v4

--- a/solution.py
+++ b/solution.py
@@ -100,49 +100,43 @@
         self.flat_rows = up_to(up_to(self.length, LANES) // LANES + 1, 8)
         self.buffer_rows = self.margin + self.flat_rows + self.margin + 8
 
-    def table(self):
-        out = []
-        for index, found in enumerate(self.regions):
-            line = [[0, 0, 0] for _ in MATRICES]
-            first_row = index * self.length // LANES
-            for matrix, first, last, base in found:
-                width = MATRICES[matrix][1] // LANES
-                start = self.offsets[matrix] // LANES + first * width - first_row + self.margin
-                line[matrix] = [start, (last - first) // ROUND, base]
-            out.extend(value for item in line for value in item)
-        return jnp.array(out, jnp.int32)
-
 
 def aligned(value, step=ROUND):
     return value if isinstance(value, int) else pl.multiple_of(value, step)
 
 
-def spread_steps(length):
-    steps = 4
-    return steps, up_to(-(-length // steps), 8 * 1024)
-
-
-def region_loop(table, index, body):
-    for matrix, (_, cols) in enumerate(MATRICES):
+def spread_steps(length, steps, unit):
+    return steps, up_to(-(-length // steps), unit)
+
+
+def region_loop(geo, index, body):
+    low = index * geo.length
+    base = jnp.int32(0)
+    for (rows, cols), offset in zip(MATRICES, geo.offsets):
         width = cols // LANES
-        at = (index * len(MATRICES) + matrix) * 3
-        start, groups, base = table[at], table[at + 1], table[at + 2]
-
-        def group_step(group, carry, width=width, start=start, groups=groups, base=base):
+        start = jnp.maximum(low - offset, 0)
+        stop = jnp.minimum(low + geo.length - offset, rows * cols)
+        there = stop > start
+        first = lax.div(start, ROUND * cols)
+        groups = jnp.where(there, lax.div(stop + (ROUND * cols - 1), ROUND * cols) - first, 0)
+        row = geo.margin + offset // LANES + first * (ROUND * width) - lax.div(low, LANES)
+
+        def group_step(group, carry, width=width, row=row, groups=groups, base=base):
             for column in range(width):
-                flat = start + group * (ROUND * width) + column
+                flat = row + group * (ROUND * width) + column
                 place = pl.multiple_of(base + (column * groups + group) * ROUND, ROUND)
                 body(flat, width, place)
             return carry
 
         lax.fori_loop(0, groups, group_step, 0)
+        base = base + groups * (ROUND * width)
 
 
 def pack_block(geo, params, where):
-    steps, chunk = spread_steps(geo.length)
+    steps, chunk = spread_steps(geo.length, 4, 8192)
     rows = chunk // LANES
 
-    def kernel(where_ref, table_ref, params_ref, block_ref, quarter_ref, buffer):
+    def kernel(where_ref, params_ref, block_ref, quarter_ref, buffer):
         step = pl.program_id(0)
         index = where_ref[0]
         shift = (index * geo.length) % LANES
@@ -177,7 +171,7 @@
                 above = buffer[pl.ds(flat - 1, ROUND, stride=width), :]
                 block_ref[pl.ds(place, ROUND), :] = jnp.where(late, here, above).astype(BF16)
 
-            region_loop(table_ref, index, move)
+            region_loop(geo, index, move)
             mine = pl.multiple_of(where_ref[1] * geo.quarter, ROUND)
             quarter_ref[...] = block_ref[pl.ds(mine, geo.quarter), :]
 
@@ -187,7 +181,6 @@
         kernel,
         grid=(steps,),
         in_specs=[
-            pl.BlockSpec(memory_space=pltpu.SMEM),
             pl.BlockSpec(memory_space=pltpu.SMEM),
             pl.BlockSpec((chunk,), lambda i: (i,)),
         ],
@@ -196,17 +189,17 @@
         scratch_shapes=[pltpu.VMEM((buffer_rows, LANES), F32)],
         compiler_params=pltpu.CompilerParams(vmem_limit_bytes=16 * 2**20),
         name="pack_block",
-    )(where, geo.table(), params)
+    )(where, params)
 
 
 def optimizer_step(geo, params, moment_one, moment_two, where, pieces, piece_places):
-    steps, chunk = spread_steps(geo.length)
+    steps, chunk = spread_steps(geo.length, 4, 8192)
     rows = chunk // LANES
     count = len(pieces)
     corr_one = 1.0 - BETA_ONE**STEP
     corr_two = 1.0 - BETA_TWO**STEP
 
-    def kernel(where_ref, table_ref, *refs):
+    def kernel(where_ref, *refs):
         piece_refs = refs[:count]
         params_ref, one_ref, two_ref, new_params_ref, new_one_ref, new_two_ref, block, buffer = refs[count:]
         step = pl.program_id(0)
@@ -221,7 +214,7 @@
             def move(flat, width, place):
                 buffer[pl.ds(flat, ROUND, stride=width), :] = block[pl.ds(place, ROUND), :].astype(F32)
 
-            region_loop(table_ref, index, move)
+            region_loop(geo, index, move)
 
         late = lax.broadcasted_iota(jnp.int32, (64, LANES), 1) >= shift
         place = lax.broadcasted_iota(jnp.int32, (64, LANES), 0) * LANES + lax.broadcasted_iota(
@@ -254,7 +247,7 @@
     return pl.pallas_call(
         kernel,
         grid=(steps,),
-        in_specs=[pl.BlockSpec(memory_space=pltpu.SMEM)] * 2
+        in_specs=[pl.BlockSpec(memory_space=pltpu.SMEM)]
         + [pl.BlockSpec(memory_space=pltpu.VMEM)] * count
         + [flat_spec] * 3,
         out_specs=[flat_spec] * 3,
@@ -265,7 +258,7 @@
         ],
         compiler_params=pltpu.CompilerParams(vmem_limit_bytes=24 * 2**20),
         name="optimizer_step",
-    )(where, geo.table(), *pieces, params, moment_one, moment_two)
+    )(where, *pieces, params, moment_one, moment_two)
 
 
 def nn(left, right):
@@ -455,7 +448,7 @@
             slope[:, cols] = below + pre * (jnp.exp(-0.5 * pre * pre) * (1.0 / math.sqrt(2.0 * math.pi)))
             return carry
 
-        lax.fori_loop(0, 12, up_step, 0)
+        lax.fori_loop(0, 12, up_step, 0, unroll=2)
         for tile in range(3):
             cols = pl.ds(tile * 256, 256)
             value = nn(act[...], load_wide(DOWN, 2 * tile, 2)) + vec(V_DOWN + 2 * tile, 2)
@@ -590,7 +583,7 @@
             pltpu.SemaphoreType.DMA((in_count,)),
             pltpu.SemaphoreType.DMA((out_count,)),
         ],
-        compiler_params=pltpu.CompilerParams(vmem_limit_bytes=18 * 2**20 + geo.shards * geo.rows * LANES * 2),
+        compiler_params=pltpu.CompilerParams(vmem_limit_bytes=20 * 2**20 + geo.shards * geo.rows * LANES * 2),
         name="model_step",
     )(where, lengths, tokens, cotangent, sinusoid, *pieces)
 

time: 217 us -> 216 us (level)
  waiting for transfers between devices: 116 us -> 120 us
  starting transfers between devices: 42.8 us -> 39 us
    ppermute x22, waiting for transfers between devices: 84.4 us -> 86.8 us  [permute(): return lax.ppermute(value, axes, pairs)]
    ppermute x8, starting transfers between devices: 14.4 us -> 11.9 us  [ring_hop(): return lax.ppermute(value, 'fsdp', pairs)]
  transfers between devices with their start and end apart: 43 -> 43, of which waited for: 23 -> 25; matrix products, arithmetic and copies ran while one was open for 0% -> 0% of each run, Pallas kernels for 5% -> 5%
where the time goes in v5:
time: 216 us
  waiting for transfers between devices  120 us (56%)
  Pallas kernels  52.8 us (24%)
  starting transfers between devices  39 us (18%)
  local copies, waits for them, and re-layouts  3.28 us (2%)
    ppermute x22, waiting for transfers between devices, permute(): return lax.ppermute(value, axes, pairs)  86.8 us
    pallas_call x1, Pallas kernels, model_step(): pl.pallas_call(kernel, in_specs=[pl.BlockSpec(memory_space=pltpu.SMEM)] *...  31.1 us
    ppermute x8, waiting for transfers between devices, ring_hop(): return lax.ppermute(value, 'fsdp', pairs)  27.5 us
    ppermute x22, starting transfers between devices, permute(): return lax.ppermute(value, axes, pairs)  22.4 us
    ppermute x8, starting transfers between devices, ring_hop(): return lax.ppermute(value, 'fsdp', pairs)  11.9 us
    pallas_call x15, Pallas kernels, small_step(): pl.pallas_call(kernel, in_specs=[pl.BlockSpec(memory_space=pltpu.SMEM)] *...  10.7 us
    pallas_call x1, Pallas kernels, optimizer_step(): pl.pallas_call(kernel, grid=(steps,), in_specs=[pl.BlockSpec(memory_space...  7.81 us
    ppermute x13, waiting for transfers between devices, core_swap(): lax.ppermute(value, 'fsdp', [(index, index ^ 1) for index in range(fsdp)])  5.46 us
  transfers between devices with their start and end apart: 43, of which 25 were waited for; matrix products, arithmetic and copies ran while one was open for 0% of the time, Pallas kernels for 5%

profile of v5, /device:TPU:0, one launch (start us, length us, event | category | flops | bytes accessed | tf_op | source)
XLA Modules:
  0.0 216.0 jit_solution(9329185813512966440)
XLA Ops:
  0.7 2.1 copy-done
  2.8 3.1 %pack_block.1 = (bf16[7936,128]{1,0:T(8,128)(2,1)S(1)}, bf16[1984,128]{1,0:T(8,128)(2,1)S(1)}) custom-call(s32[2]{0:T(128)S(1)} %pad_add_fusion.where_ref.refs_0_, f32[943392]{0:T(1024)S(1)} %copy-done), custom_call_target="tpu_custom_call" | custom-call | tf_op jit(solution)/shard_map/pack_block/pallas_call | solution.py:180
  6.3 2.8 %collective-permute-start.1 = (bf16[1984,128]{1,0:T(8,128)(2,1)S(1)}, bf16[1984,128]{1,0:T(8,128)(2,1)S(1)}, u32[]{:S(2)}, u32[]{:S(2)}) collective-permute-start(bf16[1984,128]{1,0:T(8,128)(2,1)S(1)} %get-tuple-element.65), channel_id=1, source_target_pairs={{0,2},{1,3},{2,6},{3,7},{6,4},{7,5},{4,0},{5,1},{8,10},{9,11},{10,... | collective-permute-start | bytes 1523720 | tf_op jit(solution)/shard_map/ppermute | solution.py:726
  9.2 13.1 %collective-permute-done.1.refs_0_ = bf16[1984,128]{1,0:T(8,128)(2,1)S(1)} collective-permute-done((bf16[1984,128]{1,0:T(8,128)(2,1)S(1)}, bf16[1984,128]{1,0:T(8,128)(2,1)S(1)}, u32[]{:S(2)}, u32[]{:S(2)}) %collective-permute-start.1) | collective-permute-done | bytes 507936 | tf_op jit(solution)/shard_map/ppermute | solution.py:726
  22.3 1.7 collective-permute-start.6
  23.9 0.9 collective-permute-start.5
  24.8 1.5 collective-permute-start.3
  26.3 9.8 %collective-permute-done.6.refs_2_ = bf16[1984,128]{1,0:T(8,128)(2,1)S(1)} collective-permute-done((bf16[1984,128]{1,0:T(8,128)(2,1)S(1)}, bf16[1984,128]{1,0:T(8,128)(2,1)S(1)}, u32[]{:S(2)}, u32[]{:S(2)}) %collective-permute-start.6) | collective-permute-done | bytes 507936 | tf_op jit(solution)/shard_map/ppermute | solution.py:716
  36.2 1.5 collective-permute-done.5.refs_0_.refs_1_
  37.9 1.2 copy-done.2
  39.5 1.5 collective-permute-start.9
  42.4 11.6 %collective-permute-done.9.refs_2_ = bf16[1984,128]{1,0:T(8,128)(2,1)S(1)} collective-permute-done((bf16[1984,128]{1,0:T(8,128)(2,1)S(1)}, bf16[1984,128]{1,0:T(8,128)(2,1)S(1)}, u32[]{:S(2)}, u32[]{:S(2)}) %collective-permute-start.9) | collective-permute-done | bytes 507936 | tf_op jit(solution)/shard_map/ppermute | solution.py:716
  54.5 1.5 collective-permute-start.15
  55.9 1.5 collective-permute-start.13
  57.4 1.0 collective-permute-done.11.refs_10_
  58.5 0.9 collective-permute-start.12
  59.4 11.0 %collective-permute-done.13.refs_0_ = bf16[1984,128]{1,0:T(8,128)(2,1)S(1)} collective-permute-done((bf16[1984,128]{1,0:T(8,128)(2,1)S(1)}, bf16[1984,128]{1,0:T(8,128)(2,1)S(1)}, u32[]{:S(2)}, u32[]{:S(2)}) %collective-permute-start.13) | collective-permute-done | bytes 507936 | tf_op jit(solution)/shard_map/ppermute | solution.py:716
  71.7 3.1 %collective-permute-done.15.refs_14_ = bf16[3968,128]{1,0:T(8,128)(2,1)S(1)} collective-permute-done((bf16[3968,128]{1,0:T(8,128)(2,1)S(1)}, bf16[3968,128]{1,0:T(8,128)(2,1)S(1)}, u32[]{:S(2)}, u32[]{:S(2)}) %collective-permute-start.15) | collective-permute-done | bytes 1015840 | tf_op jit(solution)/shard_map/ppermute | solution.py:716
  74.8 0.9 collective-permute-start.16
  75.7 4.5 %collective-permute-done.17.refs_16_ = bf16[1984,128]{1,0:T(8,128)(2,1)S(1)} collective-permute-done((bf16[1984,128]{1,0:T(8,128)(2,1)S(1)}, bf16[1984,128]{1,0:T(8,128)(2,1)S(1)}, u32[]{:S(2)}, u32[]{:S(2)}) %collective-permute-start.17) | collective-permute-done | bytes 507936 | tf_op jit(solution)/shard_map/ppermute | solution.py:716
  81.1 1.3 collective-permute-done.18.refs_17_
  82.4 31.1 %model_step.1 = (bf16[256,768]{1,0:T(8,128)(2,1)}, f32[256,768]{1,0:T(8,128)}, bf16[1,7936,128]{2,1,0:T(8,128)(2,1)S(1)}, bf16[1,7936,128]{2,1,0:T(8,128)(2,1)S(...) custom-call(s32[2]{0:T(128)S(1)} %pad_add_fusion.where_ref.refs_0_, ...), custom_call_target="tpu_custom_call" | custom-call | tf_op jit(solution)/shard_map/model_step/pallas_call | solution.py:554
  114.6 3.3 %collective-permute-done.20.refs_2_ = bf16[7936,128]{1,0:T(8,128)(2,1)S(1)} collective-permute-done((bf16[7936,128]{1,0:T(8,128)(2,1)}, bf16[7936,128]{1,0:T(8,128)(2,1)S(1)}, u32[]{:S(2)}, u32[]{:S(2)}) %collective-permute-start.20) | collective-permute-done | bytes 2031648 | tf_op jit(solution)/shard_map/ppermute | solution.py:719
  117.9 1.0 reduce_step.11
  120.8 1.0 reduce_step.12
  121.8 1.2 collective-permute-start.23
  123.7 4.3 %collective-permute-done.25.refs_4_ = bf16[2,992,128]{2,1,0:T(8,128)(2,1)S(1)} collective-permute-done((bf16[2,992,128]{2,1,0:T(8,128)(2,1)S(1)}, bf16[2,992,128]{2,1,0:T(8,128)(2,1)S(1)}, u32[]{:S(2)}, u32[]{:S(2)}) %collective-permute-start.25) | collective-permute-done | bytes 507936 | tf_op jit(solution)/shard_map/ppermute | solution.py:716
  128.0 1.1 reduce_step.13
  129.9 1.4 collective-permute-start.26
  131.3 7.7 %collective-permute-done.26.refs_2_ = bf16[992,128]{1,0:T(8,128)(2,1)S(1)} collective-permute-done((bf16[992,128]{1,0:T(8,128)(2,1)S(1)}, bf16[992,128]{1,0:T(8,128)(2,1)S(1)}, u32[]{:S(2)}, u32[]{:S(2)}) %collective-permute-start.26) | collective-permute-done | bytes 253984 | tf_op jit(solution)/shard_map/ppermute | solution.py:716
  139.6 5.3 %collective-permute-done.21.refs_3_ = bf16[3968,128]{1,0:T(8,128)(2,1)S(1)} collective-permute-done((bf16[3968,128]{1,0:T(8,128)(2,1)S(1)}, bf16[3968,128]{1,0:T(8,128)(2,1)S(1)}, u32[]{:S(2)}, u32[]{:S(2)}) %collective-permute-start.21) | collective-permute-done | bytes 1015840 | tf_op jit(solution)/shard_map/ppermute | solution.py:726
  144.9 1.4 reduce_step.15
  147.6 1.7 collective-permute-start.29
  149.3 6.6 %collective-permute-done.30.refs_2_ = bf16[2,1984,128]{2,1,0:T(8,128)(2,1)S(1)} collective-permute-done((bf16[2,1984,128]{2,1,0:T(8,128)(2,1)S(1)}, bf16[2,1984,128]{2,1,0:T(8,128)(2,1)S(1)}, u32[]{:S(2)}, u32[]{:S(2)}) %collective-permute-start.30) | collective-permute-done | bytes 1015840 | tf_op jit(solution)/shard_map/ppermute | solution.py:716
  156.7 4.1 %collective-permute-done.28.refs_2_ = bf16[1984,128]{1,0:T(8,128)(2,1)S(1)} collective-permute-done((bf16[1984,128]{1,0:T(8,128)(2,1)S(1)}, bf16[1984,128]{1,0:T(8,128)(2,1)S(1)}, u32[]{:S(2)}, u32[]{:S(2)}) %collective-permute-start.28) | collective-permute-done | bytes 507936 | tf_op jit(solution)/shard_map/ppermute | solution.py:716
  161.6 1.4 collective-permute-start.33
  163.5 9.7 %collective-permute-done.27.refs_2_ = bf16[2,1984,128]{2,1,0:T(8,128)(2,1)S(1)} collective-permute-done((bf16[2,1984,128]{2,1,0:T(8,128)(2,1)S(1)}, bf16[2,1984,128]{2,1,0:T(8,128)(2,1)S(1)}, u32[]{:S(2)}, u32[]{:S(2)}) %collective-permute-start.27) | collective-permute-done | bytes 1015840 | tf_op jit(solution)/shard_map/ppermute | solution.py:716
  174.0 2.5 %collective-permute-start.31 = (bf16[992,128]{1,0:T(8,128)(2,1)S(1)}, bf16[992,128]{1,0:T(8,128)(2,1)S(1)}, u32[]{:S(2)}, u32[]{:S(2)}) collective-permute-start(bf16[992,128]{1,0:T(8,128)(2,1)S(1)} %get-tuple-element.107), channel_id=1, source_target_pairs={{0,8},{1,17},{2,10},{3,19},{4,12},{5,21},{6,14},{7,23},{8,0},{9,25... | collective-permute-start | bytes 761864 | tf_op jit(solution)/shard_map/ppermute | solution.py:716
  177.5 3.4 %collective-permute-start.36 = (bf16[992,128]{1,0:T(8,128)(2,1)S(1)}, bf16[992,128]{1,0:T(8,128)(2,1)S(1)}, u32[]{:S(2)}, u32[]{:S(2)}) collective-permute-start(bf16[992,128]{1,0:T(8,128)(2,1)S(1)} %get-tuple-element.117), channel_id=1, source_target_pairs={{0,2},{1,3},{2,6},{3,7},{6,4},{7,5},{4,0},{5,1},{8,10},{9,11},{10,... | collective-permute-start | bytes 761864 | tf_op jit(solution)/shard_map/ppermute | solution.py:726
  180.8 5.9 %collective-permute-done.34.refs_3_ = bf16[992,128]{1,0:T(8,128)(2,1)S(1)} collective-permute-done((bf16[992,128]{1,0:T(8,128)(2,1)S(1)}, bf16[992,128]{1,0:T(8,128)(2,1)S(1)}, u32[]{:S(2)}, u32[]{:S(2)}) %collective-permute-start.34) | collective-permute-done | bytes 253984 | tf_op jit(solution)/shard_map/ppermute | solution.py:726
  188.1 1.4 collective-permute-done.36.refs_3_
  189.5 1.1 reduce_step.21
  191.2 0.9 collective-permute-start.39
  192.2 1.1 collective-permute-start.40
  193.2 3.2 %collective-permute-done.37.refs_2_ = bf16[992,128]{1,0:T(8,128)(2,1)S(1)} collective-permute-done((bf16[992,128]{1,0:T(8,128)(2,1)S(1)}, bf16[992,128]{1,0:T(8,128)(2,1)S(1)}, u32[]{:S(2)}, u32[]{:S(2)}) %collective-permute-start.37) | collective-permute-done | bytes 253984 | tf_op jit(solution)/shard_map/ppermute | solution.py:716
  197.3 4.6 %collective-permute-done.38.refs_3_ = bf16[992,128]{1,0:T(8,128)(2,1)S(1)} collective-permute-done((bf16[992,128]{1,0:T(8,128)(2,1)S(1)}, bf16[992,128]{1,0:T(8,128)(2,1)S(1)}, u32[]{:S(2)}, u32[]{:S(2)}) %collective-permute-start.38) | collective-permute-done | bytes 253984 | tf_op jit(solution)/shard_map/ppermute | solution.py:716
  202.9 5.2 %collective-permute-done.42.refs_7_ = bf16[992,128]{1,0:T(8,128)(2,1)S(1)} collective-permute-done((bf16[992,128]{1,0:T(8,128)(2,1)S(1)}, bf16[992,128]{1,0:T(8,128)(2,1)S(1)}, u32[]{:S(2)}, u32[]{:S(2)}) %collective-permute-start.42) | collective-permute-done | bytes 253984 | tf_op jit(solution)/shard_map/ppermute | solution.py:716
  208.2 7.8 %optimizer_step.1 = (f32[943392]{0:T(1024)}, f32[943392]{0:T(1024)}, f32[943392]{0:T(1024)}) custom-call(s32[2]{0:T(128)S(1)} %pad_add_fusion.where_ref.refs_0_, bf16[992,128]{1,0:T(8,128)(2,1)S(1)} %get-tuple-element.114.refs_0_, bf16[992,128]{1,0:T(8,128)(2,1)S(1)} %get-tuple-element.119.refs_1_, bf16[992,128]{1,0:T(8,128)(2,1)S(1)} %collective-permute-done.37.refs_2_, ...), custom_call_target="tpu_custom_call" | custom-call | tf_op jit(solution)/shard_map/optimizer_step/pallas_call | solution.py:247
  (83 shorter events, 19.0 us)
Async XLA Ops:
  5.9 31.9 %copy-start.5 = (bf16[7936,128]{1,0:T(8,128)(2,1)}, bf16[7936,128]{1,0:T(8,128)(2,1)S(1)}, u32[]{:S(2)}) copy-start(bf16[7936,128]{1,0:T(8,128)(2,1)S(1)} %get-tuple-element.64.refs_0_) | copy-start | bytes 6094852
  5.9 31.8 %collective-permute-start = (bf16[7936,128]{1,0:T(8,128)(2,1)S(1)}, bf16[7936,128]{1,0:T(8,128)(2,1)S(1)}, u32[]{:S(2)}, u32[]{:S(2)}) collective-permute-start(bf16[7936,128]{1,0:T(8,128)(2,1)S(1)} %get-tuple-element.64.refs_0_), channel_id=1, source_target_pairs={{0,1},{1,0},{2,3},{3,2},{4,5},{5,4},{6,7},{7,6},{8,9},{9,8},{10,11... | collective-permute-start | bytes 6094856 | tf_op jit(solution)/shard_map/ppermute | solution.py:719
  6.3 15.9 %collective-permute-start.1 = (bf16[1984,128]{1,0:T(8,128)(2,1)S(1)}, bf16[1984,128]{1,0:T(8,128)(2,1)S(1)}, u32[]{:S(2)}, u32[]{:S(2)}) collective-permute-start(bf16[1984,128]{1,0:T(8,128)(2,1)S(1)} %get-tuple-element.65), channel_id=1, source_target_pairs={{0,2},{1,3},{2,6},{3,7},{6,4},{7,5},{4,0},{5,1},{8,10},{9,11},{10,... | collective-permute-start | bytes 1523720 | tf_op jit(solution)/shard_map/ppermute | solution.py:726
  22.3 13.9 %collective-permute-start.6 = (bf16[1984,128]{1,0:T(8,128)(2,1)S(1)}, bf16[1984,128]{1,0:T(8,128)(2,1)S(1)}, u32[]{:S(2)}, u32[]{:S(2)}) collective-permute-start(bf16[1984,128]{1,0:T(8,128)(2,1)S(1)} %get-tuple-element.66.refs_2_), channel_id=1, source_target_pairs={{0,8},{1,17},{2,10},{3,19},{4,12},{5,21},{6,14},{7,23},{8,0},{9,25... | collective-permute-start | bytes 1523720 | tf_op jit(solution)/shard_map/ppermute | solution.py:716
  23.9 13.8 %collective-permute-start.5 = (bf16[1984,128]{1,0:T(8,128)(2,1)S(1)}, bf16[1984,128]{1,0:T(8,128)(2,1)S(1)}, u32[]{:S(2)}, u32[]{:S(2)}) collective-permute-start(bf16[1984,128]{1,0:T(8,128)(2,1)S(1)} %get-tuple-element.66.refs_2_), channel_id=1, source_target_pairs={{0,2},{1,3},{2,6},{3,7},{6,4},{7,5},{4,0},{5,1},{8,10},{9,11},{10,... | collective-permute-start | bytes 1523720 | tf_op jit(solution)/shard_map/ppermute | solution.py:726
  24.8 12.9 %collective-permute-start.3 = (bf16[1984,128]{1,0:T(8,128)(2,1)S(1)}, bf16[1984,128]{1,0:T(8,128)(2,1)S(1)}, u32[]{:S(2)}, u32[]{:S(2)}) collective-permute-start(bf16[1984,128]{1,0:T(8,128)(2,1)S(1)} %get-tuple-element.66.refs_2_), channel_id=1, source_target_pairs={{0,16},{1,9},{2,18},{3,11},{4,20},{5,13},{6,22},{7,15},{8,24},{9,1... | collective-permute-start | bytes 1523720 | tf_op jit(solution)/shard_map/ppermute | solution.py:716
  26.3 11.4 %collective-permute-start.2 = (bf16[1984,128]{1,0:T(8,128)(2,1)S(1)}, bf16[1984,128]{1,0:T(8,128)(2,1)S(1)}, u32[]{:S(2)}, u32[]{:S(2)}) collective-permute-start(bf16[1984,128]{1,0:T(8,128)(2,1)S(1)} %get-tuple-element.66.refs_2_), channel_id=1, source_target_pairs={{0,1},{1,0},{2,3},{3,2},{4,5},{5,4},{6,7},{7,6},{8,9},{9,8},{10,11... | collective-permute-start | bytes 1523720 | tf_op jit(solution)/shard_map/ppermute | solution.py:719
  39.0 15.2 %collective-permute-start.7 = (bf16[3968,128]{1,0:T(8,128)(2,1)S(1)}, bf16[3968,128]{1,0:T(8,128)(2,1)S(1)}, u32[]{:S(2)}, u32[]{:S(2)}) collective-permute-start(bf16[3968,128]{1,0:T(8,128)(2,1)S(1)} %get-tuple-element.68.refs_6_), channel_id=1, source_target_pairs={{0,1},{1,0},{2,3},{3,2},{4,5},{5,4},{6,7},{7,6},{8,9},{9,8},{10,11... | collective-permute-start | bytes 3047432 | tf_op jit(solution)/shard_map/ppermute | solution.py:719
  39.0 3.4 %collective-permute-start.4 = (bf16[1984,128]{1,0:T(8,128)(2,1)S(1)}, bf16[1984,128]{1,0:T(8,128)(2,1)S(1)}, u32[]{:S(2)}, u32[]{:S(2)}) collective-permute-start(bf16[1984,128]{1,0:T(8,128)(2,1)S(1)} %collective-permute-done.3.refs_6_.refs_4_), channel_id=1, source_target_pairs={{0,1},{1,0},{2,3},{3,2},{4,5},{5,4},{6,7},{7,6},{8,9},{9,8},{10,11... | collective-permute-start | bytes 1523720 | tf_op jit(solution)/shard_map/ppermute | solution.py:719
  39.5 14.4 %collective-permute-start.9 = (bf16[1984,128]{1,0:T(8,128)(2,1)S(1)}, bf16[1984,128]{1,0:T(8,128)(2,1)S(1)}, u32[]{:S(2)}, u32[]{:S(2)}) collective-permute-start(bf16[1984,128]{1,0:T(8,128)(2,1)S(1)} %get-tuple-element.69), channel_id=1, source_target_pairs={{0,8},{1,17},{2,10},{3,19},{4,12},{5,21},{6,14},{7,23},{8,0},{9,25... | collective-permute-start | bytes 1523720 | tf_op jit(solution)/shard_map/ppermute | solution.py:716
  41.0 13.2 %collective-permute-start.8 = (bf16[1984,128]{1,0:T(8,128)(2,1)S(1)}, bf16[1984,128]{1,0:T(8,128)(2,1)S(1)}, u32[]{:S(2)}, u32[]{:S(2)}) collective-permute-start(bf16[1984,128]{1,0:T(8,128)(2,1)S(1)} %get-tuple-element.69), channel_id=1, source_target_pairs={{0,2},{1,3},{2,6},{3,7},{6,4},{7,5},{4,0},{5,1},{8,10},{9,11},{10,... | collective-permute-start | bytes 1523720 | tf_op jit(solution)/shard_map/ppermute | solution.py:726
  41.9 16.5 %collective-permute-start.11 = (bf16[3968,128]{1,0:T(8,128)(2,1)S(1)}, bf16[3968,128]{1,0:T(8,128)(2,1)S(1)}, u32[]{:S(2)}, u32[]{:S(2)}) collective-permute-start(bf16[3968,128]{1,0:T(8,128)(2,1)S(1)} %get-tuple-element.68.refs_6_), channel_id=1, source_target_pairs={{0,16},{1,9},{2,18},{3,11},{4,20},{5,13},{6,22},{7,15},{8,24},{9,1... | collective-permute-start | bytes 3047432 | tf_op jit(solution)/shard_map/ppermute | solution.py:716
  54.2 28.2 %copy-start.8 = (bf16[2,128,768]{2,1,0:T(8,128)(2,1)S(1)}, bf16[2,128,768]{2,1,0:T(8,128)(2,1)}, u32[]{:S(2)}) copy-start(bf16[2,128,768]{2,1,0:T(8,128)(2,1)} %param.10) | copy-start | bytes 1179652
  54.4 16.1 %collective-permute-start.10 = (bf16[3968,128]{1,0:T(8,128)(2,1)S(1)}, bf16[3968,128]{1,0:T(8,128)(2,1)S(1)}, u32[]{:S(2)}, u32[]{:S(2)}) collective-permute-start(bf16[3968,128]{1,0:T(8,128)(2,1)S(1)} %get-tuple-element.71.refs_8_), channel_id=1, source_target_pairs={{0,1},{1,0},{2,3},{3,2},{4,5},{5,4},{6,7},{7,6},{8,9},{9,8},{10,11... | collective-permute-start | bytes 3047432 | tf_op jit(solution)/shard_map/ppermute | solution.py:719
  54.5 20.3 %collective-permute-start.15 = (bf16[3968,128]{1,0:T(8,128)(2,1)S(1)}, bf16[3968,128]{1,0:T(8,128)(2,1)S(1)}, u32[]{:S(2)}, u32[]{:S(2)}) collective-permute-start(bf16[3968,128]{1,0:T(8,128)(2,1)S(1)} %get-tuple-element.71.refs_8_), channel_id=1, source_target_pairs={{0,16},{1,9},{2,18},{3,11},{4,20},{5,13},{6,22},{7,15},{8,24},{9,1... | collective-permute-start | bytes 3047432 | tf_op jit(solution)/shard_map/ppermute | solution.py:716
  55.9 14.5 %collective-permute-start.13 = (bf16[1984,128]{1,0:T(8,128)(2,1)S(1)}, bf16[1984,128]{1,0:T(8,128)(2,1)S(1)}, u32[]{:S(2)}, u32[]{:S(2)}) collective-permute-start(bf16[1984,128]{1,0:T(8,128)(2,1)S(1)} %get-tuple-element.72), channel_id=1, source_target_pairs={{0,8},{1,17},{2,10},{3,19},{4,12},{5,21},{6,14},{7,23},{8,0},{9,25... | collective-permute-start | bytes 1523720 | tf_op jit(solution)/shard_map/ppermute | solution.py:716
  58.5 22.6 %collective-permute-start.12 = (bf16[3968,128]{1,0:T(8,128)(2,1)S(1)}, bf16[3968,128]{1,0:T(8,128)(2,1)S(1)}, u32[]{:S(2)}, u32[]{:S(2)}) collective-permute-start(bf16[3968,128]{1,0:T(8,128)(2,1)S(1)} %collective-permute-done.11.refs_10_), channel_id=1, source_target_pairs={{0,1},{1,0},{2,3},{3,2},{4,5},{5,4},{6,7},{7,6},{8,9},{9,8},{10,11... | collective-permute-start | bytes 3047432 | tf_op jit(solution)/shard_map/ppermute | solution.py:719
  71.1 9.1 %collective-permute-start.17 = (bf16[1984,128]{1,0:T(8,128)(2,1)S(1)}, bf16[1984,128]{1,0:T(8,128)(2,1)S(1)}, u32[]{:S(2)}, u32[]{:S(2)}) collective-permute-start(bf16[1984,128]{1,0:T(8,128)(2,1)S(1)} %get-tuple-element.74.refs_12_), channel_id=1, source_target_pairs={{0,16},{1,9},{2,18},{3,11},{4,20},{5,13},{6,22},{7,15},{8,24},{9,1... | collective-permute-start | bytes 1523720 | tf_op jit(solution)/shard_map/ppermute | solution.py:716
  74.8 6.3 %collective-permute-start.16 = (bf16[3968,128]{1,0:T(8,128)(2,1)S(1)}, bf16[3968,128]{1,0:T(8,128)(2,1)S(1)}, u32[]{:S(2)}, u32[]{:S(2)}) collective-permute-start(bf16[3968,128]{1,0:T(8,128)(2,1)S(1)} %collective-permute-done.15.refs_14_), channel_id=1, source_target_pairs={{0,1},{1,0},{2,3},{3,2},{4,5},{5,4},{6,7},{7,6},{8,9},{9,8},{10,11... | collective-permute-start | bytes 3047432 | tf_op jit(solution)/shard_map/ppermute | solution.py:719
  75.7 5.4 %collective-permute-start.14 = (bf16[1984,128]{1,0:T(8,128)(2,1)S(1)}, bf16[1984,128]{1,0:T(8,128)(2,1)S(1)}, u32[]{:S(2)}, u32[]{:S(2)}) collective-permute-start(bf16[1984,128]{1,0:T(8,128)(2,1)S(1)} %get-tuple-element.74.refs_12_), channel_id=1, source_target_pairs={{0,1},{1,0},{2,3},{3,2},{4,5},{5,4},{6,7},{7,6},{8,9},{9,8},{10,11... | collective-permute-start | bytes 1523720 | tf_op jit(solution)/shard_map/ppermute | solution.py:719
  80.2 2.2 %collective-permute-start.18 = (bf16[1984,128]{1,0:T(8,128)(2,1)S(1)}, bf16[1984,128]{1,0:T(8,128)(2,1)S(1)}, u32[]{:S(2)}, u32[]{:S(2)}) collective-permute-start(bf16[1984,128]{1,0:T(8,128)(2,1)S(1)} %collective-permute-done.17.refs_16_), channel_id=1, source_target_pairs={{0,1},{1,0},{2,3},{3,2},{4,5},{5,4},{6,7},{7,6},{8,9},{9,8},{10,11... | collective-permute-start | bytes 1523720 | tf_op jit(solution)/shard_map/ppermute | solution.py:719
  113.5 4.4 %collective-permute-start.20 = (bf16[7936,128]{1,0:T(8,128)(2,1)}, bf16[7936,128]{1,0:T(8,128)(2,1)S(1)}, u32[]{:S(2)}, u32[]{:S(2)}) collective-permute-start(bf16[7936,128]{1,0:T(8,128)(2,1)} %bitcast.23), channel_id=1, source_target_pairs={{0,1},{1,0},{2,3},{3,2},{4,5},{5,4},{6,7},{7,6},{8,9},{9,8},{10,11... | collective-permute-start | bytes 6094856 | tf_op jit(solution)/shard_map/ppermute | solution.py:719
  114.0 6.8 %collective-permute-start.22 = (bf16[7936,128]{1,0:T(8,128)(2,1)}, bf16[7936,128]{1,0:T(8,128)(2,1)S(1)}, u32[]{:S(2)}, u32[]{:S(2)}) collective-permute-start(bf16[7936,128]{1,0:T(8,128)(2,1)} %bitcast.22), channel_id=1, source_target_pairs={{0,1},{1,0},{2,3},{3,2},{4,5},{5,4},{6,7},{7,6},{8,9},{9,8},{10,11... | collective-permute-start | bytes 6094856 | tf_op jit(solution)/shard_map/ppermute | solution.py:719
  114.1 9.6 %collective-permute-start.24 = (bf16[7936,128]{1,0:T(8,128)(2,1)}, bf16[7936,128]{1,0:T(8,128)(2,1)S(1)}, u32[]{:S(2)}, u32[]{:S(2)}) collective-permute-start(bf16[7936,128]{1,0:T(8,128)(2,1)} %bitcast.21), channel_id=1, source_target_pairs={{0,1},{1,0},{2,3},{3,2},{4,5},{5,4},{6,7},{7,6},{8,9},{9,8},{10,11... | collective-permute-start | bytes 6094856 | tf_op jit(solution)/shard_map/ppermute | solution.py:719
  114.5 25.1 %collective-permute-start.19 = (bf16[7936,128]{1,0:T(8,128)(2,1)}, bf16[7936,128]{1,0:T(8,128)(2,1)S(1)}, u32[]{:S(2)}, u32[]{:S(2)}) collective-permute-start(bf16[7936,128]{1,0:T(8,128)(2,1)} %bitcast.20), channel_id=1, source_target_pairs={{0,1},{1,0},{2,3},{3,2},{4,5},{5,4},{6,7},{7,6},{8,9},{9,8},{10,11... | collective-permute-start | bytes 6094856 | tf_op jit(solution)/shard_map/ppermute | solution.py:719
  118.9 9.1 %collective-permute-start.25 = (bf16[2,992,128]{2,1,0:T(8,128)(2,1)S(1)}, bf16[2,992,128]{2,1,0:T(8,128)(2,1)S(1)}, u32[]{:S(2)}, u32[]{:S(2)}) collective-permute-start(bf16[2,992,128]{2,1,0:T(8,128)(2,1)S(1)} %get-tuple-element.90), channel_id=1, source_target_pairs={{0,16},{1,9},{2,18},{3,11},{4,20},{5,13},{6,22},{7,15},{8,24},{9,1... | collective-permute-start | bytes 1523720 | tf_op jit(solution)/shard_map/ppermute | solution.py:716
  119.7 25.2 %collective-permute-start.21 = (bf16[3968,128]{1,0:T(8,128)(2,1)S(1)}, bf16[3968,128]{1,0:T(8,128)(2,1)S(1)}, u32[]{:S(2)}, u32[]{:S(2)}) collective-permute-start(bf16[3968,128]{1,0:T(8,128)(2,1)S(1)} %get-tuple-element.81), channel_id=1, source_target_pairs={{0,4},{1,5},{2,0},{3,1},{6,2},{7,3},{4,6},{5,7},{8,12},{9,13},{10,... | collective-permute-start | bytes 3047432 | tf_op jit(solution)/shard_map/ppermute | solution.py:726
  121.8 23.1 %collective-permute-start.23 = (bf16[2,1984,128]{2,1,0:T(8,128)(2,1)S(1)}, bf16[2,1984,128]{2,1,0:T(8,128)(2,1)S(1)}, u32[]{:S(2)}, u32[]{:S(2)}) collective-permute-start(bf16[2,1984,128]{2,1,0:T(8,128)(2,1)S(1)} %get-tuple-element.86), channel_id=1, source_target_pairs={{0,16},{1,9},{2,18},{3,11},{4,20},{5,13},{6,22},{7,15},{8,24},{9,1... | collective-permute-start | bytes 3047432 | tf_op jit(solution)/shard_map/ppermute | solution.py:716
  129.1 26.8 %collective-permute-start.30 = (bf16[2,1984,128]{2,1,0:T(8,128)(2,1)S(1)}, bf16[2,1984,128]{2,1,0:T(8,128)(2,1)S(1)}, u32[]{:S(2)}, u32[]{:S(2)}) collective-permute-start(bf16[2,1984,128]{2,1,0:T(8,128)(2,1)S(1)} %get-tuple-element.102), channel_id=1, source_target_pairs={{0,16},{1,9},{2,18},{3,11},{4,20},{5,13},{6,22},{7,15},{8,24},{9,1... | collective-permute-start | bytes 3047432 | tf_op jit(solution)/shard_map/ppermute | solution.py:716
  129.9 9.1 %collective-permute-start.26 = (bf16[992,128]{1,0:T(8,128)(2,1)S(1)}, bf16[992,128]{1,0:T(8,128)(2,1)S(1)}, u32[]{:S(2)}, u32[]{:S(2)}) collective-permute-start(bf16[992,128]{1,0:T(8,128)(2,1)S(1)} %get-tuple-element.93), channel_id=1, source_target_pairs={{0,8},{1,17},{2,10},{3,19},{4,12},{5,21},{6,14},{7,23},{8,0},{9,25... | collective-permute-start | bytes 761864 | tf_op jit(solution)/shard_map/ppermute | solution.py:716
  144.9 63.3 %copy-start.4 = (f32[943392]{0:T(1024)S(1)}, f32[943392]{0:T(1024)}, u32[]{:S(2)}) copy-start(f32[943392]{0:T(1024)} %refs_10_.1) | copy-start | bytes 11320708
  146.3 14.6 %collective-permute-start.28 = (bf16[1984,128]{1,0:T(8,128)(2,1)S(1)}, bf16[1984,128]{1,0:T(8,128)(2,1)S(1)}, u32[]{:S(2)}, u32[]{:S(2)}) collective-permute-start(bf16[1984,128]{1,0:T(8,128)(2,1)S(1)} %get-tuple-element.99), channel_id=1, source_target_pairs={{0,8},{1,17},{2,10},{3,19},{4,12},{5,21},{6,14},{7,23},{8,0},{9,25... | collective-permute-start | bytes 1523720 | tf_op jit(solution)/shard_map/ppermute | solution.py:716
  146.9 26.3 %collective-permute-start.27 = (bf16[2,1984,128]{2,1,0:T(8,128)(2,1)S(1)}, bf16[2,1984,128]{2,1,0:T(8,128)(2,1)S(1)}, u32[]{:S(2)}, u32[]{:S(2)}) collective-permute-start(bf16[2,1984,128]{2,1,0:T(8,128)(2,1)S(1)} %get-tuple-element.97), channel_id=1, source_target_pairs={{0,16},{1,9},{2,18},{3,11},{4,20},{5,13},{6,22},{7,15},{8,24},{9,1... | collective-permute-start | bytes 3047432 | tf_op jit(solution)/shard_map/ppermute | solution.py:716
  147.6 9.1 %collective-permute-start.29 = (bf16[992,128]{1,0:T(8,128)(2,1)S(1)}, bf16[992,128]{1,0:T(8,128)(2,1)S(1)}, u32[]{:S(2)}, u32[]{:S(2)}) collective-permute-start(bf16[992,128]{1,0:T(8,128)(2,1)S(1)} %get-tuple-element.100), channel_id=1, source_target_pairs={{0,2},{1,3},{2,6},{3,7},{6,4},{7,5},{4,0},{5,1},{8,10},{9,11},{10,... | collective-permute-start | bytes 761864 | tf_op jit(solution)/shard_map/ppermute | solution.py:726
  155.9 52.2 %copy-start.3 = (f32[943392]{0:T(1024)S(1)}, f32[943392]{0:T(1024)}, u32[]{:S(2)}) copy-start(f32[943392]{0:T(1024)} %refs_9_.1) | copy-start | bytes 11320708
  161.6 15.0 %collective-permute-start.33 = (bf16[1984,128]{1,0:T(8,128)(2,1)S(1)}, bf16[1984,128]{1,0:T(8,128)(2,1)S(1)}, u32[]{:S(2)}, u32[]{:S(2)}) collective-permute-start(bf16[1984,128]{1,0:T(8,128)(2,1)S(1)} %get-tuple-element.110), channel_id=1, source_target_pairs={{0,2},{1,3},{2,6},{3,7},{6,4},{7,5},{4,0},{5,1},{8,10},{9,11},{10,... | collective-permute-start | bytes 1523720 | tf_op jit(solution)/shard_map/ppermute | solution.py:726
  163.0 13.6 %collective-permute-start.32 = (bf16[1984,128]{1,0:T(8,128)(2,1)S(1)}, bf16[1984,128]{1,0:T(8,128)(2,1)S(1)}, u32[]{:S(2)}, u32[]{:S(2)}) collective-permute-start(bf16[1984,128]{1,0:T(8,128)(2,1)S(1)} %get-tuple-element.109), channel_id=1, source_target_pairs={{0,8},{1,17},{2,10},{3,19},{4,12},{5,21},{6,14},{7,23},{8,0},{9,25... | collective-permute-start | bytes 1523720 | tf_op jit(solution)/shard_map/ppermute | solution.py:716
  173.2 35.0 %copy-start.1 = (f32[943392]{0:T(1024)S(1)}, f32[943392]{0:T(1024)}, u32[]{:S(2)}) copy-start(f32[943392]{0:T(1024)} %refs_8_.1) | copy-start | bytes 11320708
  174.0 6.8 %collective-permute-start.31 = (bf16[992,128]{1,0:T(8,128)(2,1)S(1)}, bf16[992,128]{1,0:T(8,128)(2,1)S(1)}, u32[]{:S(2)}, u32[]{:S(2)}) collective-permute-start(bf16[992,128]{1,0:T(8,128)(2,1)S(1)} %get-tuple-element.107), channel_id=1, source_target_pairs={{0,8},{1,17},{2,10},{3,19},{4,12},{5,21},{6,14},{7,23},{8,0},{9,25... | collective-permute-start | bytes 761864 | tf_op jit(solution)/shard_map/ppermute | solution.py:716
  177.3 9.5 %collective-permute-start.34 = (bf16[992,128]{1,0:T(8,128)(2,1)S(1)}, bf16[992,128]{1,0:T(8,128)(2,1)S(1)}, u32[]{:S(2)}, u32[]{:S(2)}) collective-permute-start(bf16[992,128]{1,0:T(8,128)(2,1)S(1)} %get-tuple-element.112), channel_id=1, source_target_pairs={{0,2},{1,3},{2,6},{3,7},{6,4},{7,5},{4,0},{5,1},{8,10},{9,11},{10,... | collective-permute-start | bytes 761864 | tf_op jit(solution)/shard_map/ppermute | solution.py:726
  177.4 10.7 %collective-permute-start.35 = (bf16[992,128]{1,0:T(8,128)(2,1)S(1)}, bf16[992,128]{1,0:T(8,128)(2,1)S(1)}, u32[]{:S(2)}, u32[]{:S(2)}) collective-permute-start(bf16[992,128]{1,0:T(8,128)(2,1)S(1)} %get-tuple-element.116), channel_id=1, source_target_pairs={{0,8},{1,17},{2,10},{3,19},{4,12},{5,21},{6,14},{7,23},{8,0},{9,25... | collective-permute-start | bytes 761864 | tf_op jit(solution)/shard_map/ppermute | solution.py:716
  177.5 12.0 %collective-permute-start.36 = (bf16[992,128]{1,0:T(8,128)(2,1)S(1)}, bf16[992,128]{1,0:T(8,128)(2,1)S(1)}, u32[]{:S(2)}, u32[]{:S(2)}) collective-permute-start(bf16[992,128]{1,0:T(8,128)(2,1)S(1)} %get-tuple-element.117), channel_id=1, source_target_pairs={{0,2},{1,3},{2,6},{3,7},{6,4},{7,5},{4,0},{5,1},{8,10},{9,11},{10,... | collective-permute-start | bytes 761864 | tf_op jit(solution)/shard_map/ppermute | solution.py:726
  187.4 9.0 %collective-permute-start.37 = (bf16[992,128]{1,0:T(8,128)(2,1)S(1)}, bf16[992,128]{1,0:T(8,128)(2,1)S(1)}, u32[]{:S(2)}, u32[]{:S(2)}) collective-permute-start(bf16[992,128]{1,0:T(8,128)(2,1)S(1)} %get-tuple-element.114.refs_0_), channel_id=1, source_target_pairs={{0,8},{1,17},{2,10},{3,19},{4,12},{5,21},{6,14},{7,23},{8,0},{9,25... | collective-permute-start | bytes 761864 | tf_op jit(solution)/shard_map/ppermute | solution.py:716
  190.6 11.3 %collective-permute-start.38 = (bf16[992,128]{1,0:T(8,128)(2,1)S(1)}, bf16[992,128]{1,0:T(8,128)(2,1)S(1)}, u32[]{:S(2)}, u32[]{:S(2)}) collective-permute-start(bf16[992,128]{1,0:T(8,128)(2,1)S(1)} %get-tuple-element.119.refs_1_), channel_id=1, source_target_pairs={{0,8},{1,17},{2,10},{3,19},{4,12},{5,21},{6,14},{7,23},{8,0},{9,25... | collective-permute-start | bytes 761864 | tf_op jit(solution)/shard_map/ppermute | solution.py:716
  191.2 11.5 %collective-permute-start.39 = (bf16[992,128]{1,0:T(8,128)(2,1)S(1)}, bf16[992,128]{1,0:T(8,128)(2,1)S(1)}, u32[]{:S(2)}, u32[]{:S(2)}) collective-permute-start(bf16[992,128]{1,0:T(8,128)(2,1)S(1)} %get-tuple-element.114.refs_0_), channel_id=1, source_target_pairs={{0,16},{1,9},{2,18},{3,11},{4,20},{5,13},{6,22},{7,15},{8,24},{9,1... | collective-permute-start | bytes 761864 | tf_op jit(solution)/shard_map/ppermute | solution.py:716
  192.2 10.5 %collective-permute-start.40 = (bf16[992,128]{1,0:T(8,128)(2,1)S(1)}, bf16[992,128]{1,0:T(8,128)(2,1)S(1)}, u32[]{:S(2)}, u32[]{:S(2)}) collective-permute-start(bf16[992,128]{1,0:T(8,128)(2,1)S(1)} %get-tuple-element.119.refs_1_), channel_id=1, source_target_pairs={{0,16},{1,9},{2,18},{3,11},{4,20},{5,13},{6,22},{7,15},{8,24},{9,1... | collective-permute-start | bytes 761864 | tf_op jit(solution)/shard_map/ppermute | solution.py:716
  196.4 6.5 %collective-permute-start.41 = (bf16[992,128]{1,0:T(8,128)(2,1)S(1)}, bf16[992,128]{1,0:T(8,128)(2,1)S(1)}, u32[]{:S(2)}, u32[]{:S(2)}) collective-permute-start(bf16[992,128]{1,0:T(8,128)(2,1)S(1)} %collective-permute-done.37.refs_2_), channel_id=1, source_target_pairs={{0,16},{1,9},{2,18},{3,11},{4,20},{5,13},{6,22},{7,15},{8,24},{9,1... | collective-permute-start | bytes 761864 | tf_op jit(solution)/shard_map/ppermute | solution.py:716
  201.9 6.3 %collective-permute-start.42 = (bf16[992,128]{1,0:T(8,128)(2,1)S(1)}, bf16[992,128]{1,0:T(8,128)(2,1)S(1)}, u32[]{:S(2)}, u32[]{:S(2)}) collective-permute-start(bf16[992,128]{1,0:T(8,128)(2,1)S(1)} %collective-permute-done.38.refs_3_), channel_id=1, source_target_pairs={{0,16},{1,9},{2,18},{3,11},{4,20},{5,13},{6,22},{7,15},{8,24},{9,1... | collective-permute-start | bytes 761864 | tf_op jit(solution)/shard_map/ppermute | solution.py:716
  (6 other events, 103.3 us)
